TPU v7x, 32 devices: a whole 2x2x4 slice. The times are simulated.
32 devices in a mesh: dp: 8 (over z, x), head: 4 (over y, core).
Axes of the slice: x: 2, y: 2, z: 4, core: 2. Of those that a mesh axis runs over, the one named last changes fastest.
Arguments:
- hidden_in: bfloat16 [8, 2048, 1024], P('dp', 'head'), may hold values from -6 to 6
- first_values: bfloat16 [8, 2048, 1024], P('dp', 'head'), may hold values from -6 to 6
- doc_lengths: int32 [8, 16], P('dp'), may hold values from 1 to 1537, as said below
- out_grad: bfloat16 [8, 2048, 1024], P('dp', 'head'), may hold values from -6 to 6
- qkv_weight: bfloat16 [1024, 3, 1024], P('dp', None, 'head'), may hold values from -0.1875 to 0.1875
- out_weight: bfloat16 [1024, 1024], P('head', 'dp'), may hold values from -6 to 6
- gate_up_weight: bfloat16 [1024, 2, 2816], P('dp', None, 'head'), may hold values from -0.1875 to 0.1875
- down_weight: bfloat16 [2816, 1024], P('head', 'dp'), may hold values from -0.109375 to 0.109375
- attn_gain: float32 [1024], replicated, may hold values from 0.1 to 1.9
- mlp_gain: float32 [1024], replicated, may hold values from 0.1 to 1.9
Outputs:
- layer_out: bfloat16 [8, 2048, 1024], P('dp', 'head')
- input_grad: float32 [8, 2048, 1024], P('dp', 'head')
- first_values_grad: float32 [8, 2048, 1024], P('dp', 'head')
- qkv_weight_grad: float32 [1024, 3, 1024], P('dp', None, 'head')
- out_weight_grad: float32 [1024, 1024], P('head', 'dp')
- gate_up_weight_grad: float32 [1024, 2, 2816], P('dp', None, 'head')
- down_weight_grad: float32 [2816, 1024], P('head', 'dp')
- attn_gain_grad: float32 [1024], replicated
- mlp_gain_grad: float32 [1024], replicated
Inputs may be any that keep to these rules, and one draw needn't show every extreme that they name: `doc_lengths`: each row's lengths sum to 2048.
All inputs are finite; a program needn't handle non-finite values.
Results may differ from a plain program's by a relative error of at most 0.023.
Values may be sent and summed in bfloat16 or wider, within the bound.
No kernel may reach another device: no remote copies, remote signals or barrier semaphores. Data moves between devices by JAX's collectives and lax.ppermute only.
A program may use at most 256 MiB of HBM per device.

v0:
```python
import math

import jax
import jax.numpy as jnp
from jax import lax
from jax.sharding import PartitionSpec as P

HEAD_DIM = 64
SEQ = 2048
NDOC = 16
QBLOCK = 512


norm_eps = 1e-06


def doc_layout(lengths):
    tok_index = jnp.arange(SEQ, dtype=jnp.int32)
    doc_ends = jnp.cumsum(lengths)
    starts = doc_ends - lengths
    segment = jnp.sum((tok_index[:, None] >= doc_ends[None, :]).astype(jnp.int32), axis=1)
    owners = segment[:, None] == jnp.arange(NDOC, dtype=jnp.int32)[None, :]
    positions = tok_index - jnp.sum(jnp.where(owners, starts[None, :], 0), axis=1)
    return (segment, positions)


def rope_tables(positions):
    freq_index = jnp.arange(HEAD_DIM // 2, dtype=jnp.float32)
    inverse = jnp.exp(freq_index * (-2.0 * math.log(10000.0) / HEAD_DIM))
    angles = positions.astype(jnp.float32)[..., None] * inverse
    angles = jnp.concatenate([angles, angles], axis=-1)
    return (jnp.cos(angles), jnp.sin(angles))


def rotate(tensor, cos_table, sin_table):
    half_dim = tensor.shape[-1] // 2
    turned = jnp.concatenate([-tensor[..., half_dim:], tensor[..., :half_dim]], axis=-1)
    return tensor * cos_table + turned * sin_table


def rotate_back(gradient, cos_table, sin_table):
    half_dim = gradient.shape[-1] // 2
    turned = gradient * sin_table
    return gradient * cos_table + jnp.concatenate(
        [turned[..., half_dim:], -turned[..., :half_dim]], axis=-1
    )


def rms_scale(stream):
    return lax.rsqrt(jnp.mean(stream * stream, axis=-1, keepdims=True) + norm_eps)


def norm_back(gradient, stream, scale_rows, gain):
    normed = stream * scale_rows
    scaled = gradient * gain
    grad_stream = scale_rows * (scaled - normed * jnp.mean(scaled * normed, axis=-1, keepdims=True))
    return (grad_stream, jnp.sum(gradient * normed, axis=(0, 1)))


def block_scores(queries, key_rows, segment, first_q, last_q):
    q_index = jnp.arange(first_q, last_q, dtype=jnp.int32)
    key_index = jnp.arange(last_q, dtype=jnp.int32)
    allowed = (segment[first_q:last_q, None] == segment[None, :last_q]) & (
        key_index[None, :] <= q_index[:, None]
    )
    scores = jnp.einsum(
        "qhd,khd->hqk",
        queries[first_q:last_q],
        key_rows[:last_q],
        preferred_element_type=jnp.float32,
    ) * HEAD_DIM ** (-0.5)
    return jnp.where(allowed[None], scores, -1e30)


def attend_row(queries, key_rows, value_rows, segment):
    outputs = []
    log_sums = []
    for block_id in range(SEQ // QBLOCK):
        first_q = block_id * QBLOCK
        last_q = first_q + QBLOCK
        scores = block_scores(queries, key_rows, segment, first_q, last_q)
        row_max = jnp.max(scores, axis=-1, keepdims=True)
        exp_terms = jnp.exp(scores - row_max)
        row_sum = jnp.sum(exp_terms, axis=-1, keepdims=True)
        weights_p = (exp_terms / row_sum).astype(jnp.bfloat16)
        outputs.append(
            jnp.einsum(
                "hqk,khd->qhd", weights_p, value_rows[:last_q], preferred_element_type=jnp.float32
            )
        )
        log_sums.append(row_max + jnp.log(row_sum))
    return (jnp.concatenate(outputs, axis=0), jnp.concatenate(log_sums, axis=1))


def attend_back(queries, key_rows, value_rows, segment, log_sums, grad_context):
    grad_queries = []
    grad_keys = jnp.zeros(key_rows.shape, jnp.float32)
    grad_values = jnp.zeros(value_rows.shape, jnp.float32)
    for block_id in range(SEQ // QBLOCK):
        first_q = block_id * QBLOCK
        last_q = first_q + QBLOCK
        scores = block_scores(queries, key_rows, segment, first_q, last_q)
        weights_p = jnp.exp(scores - log_sums[:, first_q:last_q])
        grad_probs = jnp.einsum(
            "qhd,khd->hqk",
            grad_context[first_q:last_q],
            value_rows[:last_q],
            preferred_element_type=jnp.float32,
        )
        delta_rows = jnp.sum(weights_p * grad_probs, axis=-1, keepdims=True)
        grad_scores = (HEAD_DIM ** (-0.5) * weights_p * (grad_probs - delta_rows)).astype(
            jnp.bfloat16
        )
        grad_queries.append(
            jnp.einsum(
                "hqk,khd->qhd", grad_scores, key_rows[:last_q], preferred_element_type=jnp.float32
            )
        )
        grad_keys = grad_keys.at[:last_q].add(
            jnp.einsum(
                "hqk,qhd->khd",
                grad_scores,
                queries[first_q:last_q],
                preferred_element_type=jnp.float32,
            )
        )
        grad_values = grad_values.at[:last_q].add(
            jnp.einsum(
                "hqk,qhd->khd",
                weights_p.astype(jnp.bfloat16),
                grad_context[first_q:last_q],
                preferred_element_type=jnp.float32,
            )
        )
    return (jnp.concatenate(grad_queries, axis=0), grad_keys, grad_values)


def mlp_forward(normed_in, w_gate_up, w_down):
    gate_up = jnp.einsum("rsd,dcf->rscf", normed_in, w_gate_up, preferred_element_type=jnp.float32)
    mixed_act = (jax.nn.silu(gate_up[:, :, 0]) * gate_up[:, :, 1]).astype(jnp.bfloat16)
    return (
        gate_up,
        mixed_act,
        jnp.einsum("rsf,fd->rsd", mixed_act, w_down, preferred_element_type=jnp.float32),
    )


def mlp_backward(normed_in, gate_up, mixed_act, grad_rows, w_gate_up, w_down):
    grad_mixed = jnp.einsum("rsd,fd->rsf", grad_rows, w_down, preferred_element_type=jnp.float32)
    grad_down = jnp.einsum("rsf,rsd->fd", mixed_act, grad_rows, preferred_element_type=jnp.float32)
    gate_part = gate_up[:, :, 0]
    up_part = gate_up[:, :, 1]
    sigmoid_g = jax.nn.sigmoid(gate_part)
    grad_gate = grad_mixed * up_part * sigmoid_g * (1.0 + gate_part * (1.0 - sigmoid_g))
    grad_up = grad_mixed * gate_part * sigmoid_g
    grad_gu = jnp.stack([grad_gate, grad_up], axis=2).astype(jnp.bfloat16)
    grad_gate_up = jnp.einsum(
        "rsd,rscf->dcf", normed_in, grad_gu, preferred_element_type=jnp.float32
    )
    grad_normed = jnp.einsum(
        "rscf,dcf->rsd", grad_gu, w_gate_up, preferred_element_type=jnp.float32
    )
    return (grad_normed, grad_gate_up, grad_down)


def local(
    hidden_in,
    first_values,
    doc_lengths,
    out_grad,
    qkv_weight,
    out_weight,
    gate_up_weight,
    down_weight,
    attn_gain,
    mlp_gain,
):
    w_qkv, w_out, w_gate_up, w_down = (
        lax.all_gather(qkv_weight, "dp", axis=0, tiled=True),
        lax.all_gather(out_weight, "dp", axis=1, tiled=True),
        lax.all_gather(gate_up_weight, "dp", axis=0, tiled=True),
        lax.all_gather(down_weight, "dp", axis=1, tiled=True),
    )
    row_count = hidden_in.shape[0]
    head_cols = w_qkv.shape[2]
    head_count = head_cols // HEAD_DIM
    stream = hidden_in.astype(jnp.float32)
    scale_one = rms_scale(stream)
    normed_one = (stream * scale_one * attn_gain).astype(jnp.bfloat16)
    full_in = lax.all_gather(normed_one, "head", axis=1, tiled=True)
    first_own = lax.all_to_all(
        first_values, "head", split_axis=2, concat_axis=1, tiled=True
    ).astype(jnp.float32)
    segment, positions = jax.vmap(doc_layout)(doc_lengths)
    cos_table, sin_table = rope_tables(positions)
    cos_table = cos_table[:, :, None, :]
    sin_table = sin_table[:, :, None, :]
    project = jnp.einsum("rsd,dcf->rscf", full_in, w_qkv, preferred_element_type=jnp.float32)
    head_shape = (row_count, SEQ, head_count, HEAD_DIM)
    queries = rotate(project[:, :, 0].reshape(head_shape), cos_table, sin_table).astype(
        jnp.bfloat16
    )
    key_rows = rotate(project[:, :, 1].reshape(head_shape), cos_table, sin_table).astype(
        jnp.bfloat16
    )
    value_rows = (0.5 * project[:, :, 2] + 0.5 * first_own).reshape(head_shape).astype(jnp.bfloat16)
    row_id = 0
    context_one, lse_one = attend_row(
        queries[row_id], key_rows[row_id], value_rows[row_id], segment[row_id]
    )
    context_rows = [context_one]
    lse_rows = [lse_one]
    context = jnp.stack(context_rows).reshape(row_count, SEQ, head_cols).astype(jnp.bfloat16)
    log_sums = jnp.stack(lse_rows)
    attn_part = jnp.einsum("rsf,fd->rsd", context, w_out, preferred_element_type=jnp.float32)
    attn_result = lax.psum_scatter(
        attn_part.astype(jnp.bfloat16), "head", scatter_dimension=1, tiled=True
    ).astype(jnp.float32)
    middle = stream + attn_result
    scale_two = rms_scale(middle)
    normed_two = (middle * scale_two * mlp_gain).astype(jnp.bfloat16)
    grad_layer = out_grad.astype(jnp.float32)
    normed_full = lax.all_gather(normed_two, "head", axis=1, tiled=True)
    gate_up, mixed_act, mlp_part = mlp_forward(normed_full, w_gate_up, w_down)
    mlp_result = lax.psum_scatter(
        mlp_part.astype(jnp.bfloat16), "head", scatter_dimension=1, tiled=True
    ).astype(jnp.float32)
    layer_out = (middle + mlp_result).astype(jnp.bfloat16)
    grad_full = lax.all_gather(out_grad, "head", axis=1, tiled=True)
    grad_normed_part, grad_gate_up, grad_down = mlp_backward(
        normed_full, gate_up, mixed_act, grad_full, w_gate_up, w_down
    )
    grad_normed_two = lax.psum_scatter(
        grad_normed_part.astype(jnp.bfloat16), "head", scatter_dimension=1, tiled=True
    ).astype(jnp.float32)
    grad_mid_norm, gain_two_part = norm_back(grad_normed_two, middle, scale_two, mlp_gain)
    grad_middle = grad_layer + grad_mid_norm
    grad_attn = grad_middle.astype(jnp.bfloat16)
    grad_attn_full = lax.all_gather(grad_attn, "head", axis=1, tiled=True)
    grad_context = jnp.einsum(
        "rsd,fd->rsf", grad_attn_full, w_out, preferred_element_type=jnp.float32
    ).astype(jnp.bfloat16)
    grad_out_weight = jnp.einsum(
        "rsf,rsd->fd", context, grad_attn_full, preferred_element_type=jnp.float32
    )
    grad_context = grad_context.reshape(head_shape)
    row_id = 0
    grad_q_one, grad_k_one, grad_v_one = attend_back(
        queries[row_id],
        key_rows[row_id],
        value_rows[row_id],
        segment[row_id],
        log_sums[row_id],
        grad_context[row_id],
    )
    grad_q_rows = [grad_q_one]
    grad_k_rows = [grad_k_one]
    grad_v_rows = [grad_v_one]
    grad_q_all = rotate_back(jnp.stack(grad_q_rows), cos_table, sin_table).reshape(
        row_count, SEQ, head_cols
    )
    grad_k_all = rotate_back(jnp.stack(grad_k_rows), cos_table, sin_table).reshape(
        row_count, SEQ, head_cols
    )
    grad_v_half = 0.5 * jnp.stack(grad_v_rows).reshape(row_count, SEQ, head_cols)
    grad_project = jnp.stack([grad_q_all, grad_k_all, grad_v_half], axis=2).astype(jnp.bfloat16)
    grad_qkv = jnp.einsum(
        "rsd,rscf->dcf", full_in, grad_project, preferred_element_type=jnp.float32
    )
    grad_normed_one_part = jnp.einsum(
        "rscf,dcf->rsd", grad_project, w_qkv, preferred_element_type=jnp.float32
    )
    first_grad = lax.all_to_all(
        grad_v_half.astype(jnp.bfloat16), "head", split_axis=1, concat_axis=2, tiled=True
    ).astype(grad_v_half.dtype)
    grad_normed_one = lax.psum_scatter(
        grad_normed_one_part.astype(jnp.bfloat16), "head", scatter_dimension=1, tiled=True
    ).astype(jnp.float32)
    grad_in_norm, gain_one_part = norm_back(grad_normed_one, stream, scale_one, attn_gain)
    input_grad = grad_middle + grad_in_norm
    qkv_grad, out_grad_w, gate_up_grad, down_grad = (
        lax.psum_scatter(
            grad_qkv.astype(jnp.bfloat16), "dp", scatter_dimension=0, tiled=True
        ).astype(jnp.float32),
        lax.psum_scatter(
            grad_out_weight.astype(jnp.bfloat16), "dp", scatter_dimension=1, tiled=True
        ).astype(jnp.float32),
        lax.psum_scatter(
            grad_gate_up.astype(jnp.bfloat16), "dp", scatter_dimension=0, tiled=True
        ).astype(jnp.float32),
        lax.psum_scatter(
            grad_down.astype(jnp.bfloat16), "dp", scatter_dimension=1, tiled=True
        ).astype(jnp.float32),
    )
    gain_one, gain_two = lax.psum((gain_one_part, gain_two_part), ("dp", "head"))
    return (
        layer_out,
        input_grad,
        first_grad,
        qkv_grad,
        out_grad_w,
        gate_up_grad,
        down_grad,
        gain_one,
        gain_two,
    )


def solution(mesh):
    return jax.shard_map(
        local,
        mesh=mesh,
        in_specs=(
            P("dp", "head", None),
            P("dp", "head", None),
            P("dp", None),
            P("dp", "head", None),
            P("dp", None, "head"),
            P("head", "dp"),
            P("dp", None, "head"),
            P("head", "dp"),
            P(),
            P(),
        ),
        out_specs=(
            P("dp", "head", None),
            P("dp", "head", None),
            P("dp", "head", None),
            P("dp", None, "head"),
            P("head", "dp"),
            P("dp", None, "head"),
            P("head", "dp"),
            P(),
            P(),
        ),
        check_vma=False,
    )
```

profile of v0, /device:TPU:0, one launch (start us, length us, event | category | flops | bytes accessed | tf_op | source)
XLA Modules:
  0.0 872.8 jit_solution(2770652325299205901)
XLA Ops:
  11.2 2.5 fusion.102
  16.1 7.0 reduce.24
  25.2 4.2 all-to-all-start
  29.9 33.2 %all_gather.26 = bf16[256,1024]{1,0:T(8,128)(2,1)} all-gather(bf16[256,128]{1,0:T(8,128)(2,1)S(1)} %copy-done.59), channel_id=1, replica_groups=mesh['dp'=8,'head'=4] {'dp'}, dimensions={1}, use_global_device_ids=true | all-gather | bytes 589824 | tf_op jit(solution)/shard_map/all_gather | solution.py:180
  72.9 3.1 copy.90
  78.4 2.4 reshape.1308
  80.9 19.2 %all-gather.8.cloned.1.call-done = bf16[1,2048,1024]{2,1,0:T(8,128)(2,1)} async-done(((bf16[1,512,1024]{2,1,0:T(8,128)(2,1)}), bf16[1,2048,1024]{2,1,0:T(8,128)(2,1)}) %all-gather.8.cloned.1.call-update) | async-done | bytes 4194320 | tf_op jit(solution)/shard_map/all_gather | solution.py:190
  100.0 5.9 fusion.44
  118.1 3.0 fusion.147
  121.1 2.5 fusion.181
  125.5 2.7 copy-done
  128.2 4.8 fusion.148
  135.7 8.6 fusion.180
  144.3 8.2 fusion
  152.6 7.9 fusion.149
  161.1 3.3 convert_bitcast_fusion.1
  165.0 44.1 %reduce-scatter.15.cloned.1.call-done = bf16[1,512,1024]{2,1,0:T(8,128)(2,1)} async-done(((bf16[1,2048,1024]{2,1,0:T(8,128)(2,1)}), bf16[1,512,1024]{2,1,0:T(8,128)(2,1)}) %reduce-scatter.15.cloned.1.call-update) | async-done | bytes 1048592 | tf_op jit(solution)/shard_map/reduce_scatter | solution.py:216
  210.8 2.6 multiply_convert_fusion.6
  214.8 56.5 %all-gather.14.cloned.1.call-done = bf16[1024,2,704]{0,2,1:T(8,128)(2,1)} async-done(((bf16[128,2,704]{0,2,1:T(8,128)(2,1)}), bf16[1024,2,704]{0,2,1:T(8,128)(2,1)}) %all-gather.14.cloned.1.call-update) | async-done | bytes 2883600 | tf_op jit(solution)/shard_map/all_gather | solution.py:181
  271.3 34.8 %all-gather.12.cloned.1.call-done = bf16[1,2048,1024]{2,1,0:T(8,128)(2,1)} async-done(((bf16[1,512,1024]{2,1,0:T(8,128)(2,1)}), bf16[1,2048,1024]{2,1,0:T(8,128)(2,1)}) %all-gather.12.cloned.1.call-update) | async-done | bytes 4194320 | tf_op jit(solution)/shard_map/all_gather | solution.py:223
  306.0 11.5 %convolution_bitcast_fusion = f32[1,2048,2,704]{1,3,2,0:T(8,128)} fusion(bf16[1024,2,704]{0,2,1:T(8,128)(2,1)} %all-gather.14.cloned.1.call-done, bf16[1,2048,1024]{2,1,0:T(8,128)(2,1)} %all-gather.12.cloned.1.call-done), kind=kOutput, calls=%fused_computation.50 | convolution fusion | flops 5905580032 | bytes 18612224 | tf_op jit(solution)/shard_map/rsd,dcf->rscf/dot_general | solution.py:139
  317.5 34.5 %all-gather.16.cloned.1.call-done = bf16[704,1024]{1,0:T(8,128)(2,1)} async-done(((bf16[704,128]{1,0:T(8,128)(2,1)}), bf16[704,1024]{1,0:T(8,128)(2,1)}) %all-gather.16.cloned.1.call-update) | async-done | bytes 1441808 | tf_op jit(solution)/shard_map/all_gather | solution.py:182
  352.0 34.5 %all-gather.18.cloned.1.call-done = bf16[1,2048,1024]{2,1,0:T(8,128)(2,1)} async-done(((bf16[1,512,1024]{2,1,0:T(8,128)(2,1)}), bf16[1,2048,1024]{2,1,0:T(8,128)(2,1)}) %all-gather.18.cloned.1.call-update) | async-done | bytes 4194320 | tf_op jit(solution)/shard_map/all_gather | solution.py:229
  386.5 9.6 %fusion.59 = (bf16[2048,1,704]{0,2,1:T(8,128)(2,1)S(1)}, bf16[2048,1,704]{0,2,1:T(8,128)(2,1)S(1)}) fusion(f32[1,2048,2,704]{1,3,2,0:T(8,128)} %convolution_bitcast_fusion, bf16[704,1024]{1,0:T(8,128)(2,1)} %all-gather.16.cloned.1.call-done, bf16[1,2048,1024]{2,1,0:T(8,128)(2,1)} %all-gather.18.cloned.1.call-done), kind=kOutput, calls=%fused_computation.96 | convolution fusion | flops 2971533312 | bytes 22937600 | tf_op jit(solution)/shard_map/rsd,fd->rsf/dot_general | solution.py:149
  398.6 8.5 fusion.48
  407.3 44.5 %reduce-scatter.19.cloned.1.call-done = bf16[1,512,1024]{2,1,0:T(8,128)(2,1)} async-done(((bf16[1,2048,1024]{2,1,0:T(8,128)(2,1)}), bf16[1,512,1024]{2,1,0:T(8,128)(2,1)}) %reduce-scatter.19.cloned.1.call-update) | async-done | bytes 1048592 | tf_op jit(solution)/shard_map/reduce_scatter | solution.py:233
  451.7 2.7 fusion.101
  454.4 3.3 fusion.175
  457.8 8.7 fusion.124
  470.4 10.6 %fusion.93 = bf16[1024,2,704]{0,2,1:T(8,128)(2,1)} fusion(bf16[2048,1,704]{0,2,1:T(8,128)(2,1)} %copy-done.74, bf16[2048,1,704]{0,2,1:T(8,128)(2,1)} %copy-done.73, bf16[1,2048,1024]{2,1,0:T(8,128)(2,1)} %all-gather.12.cloned.1.call-done), kind=kOutput, calls=%fused_computation.117 | convolution fusion | flops 5918556160 | bytes 12845056 | tf_op jit(solution)/shard_map/rsd,rscf->dcf/dot_general | solution.py:157
  481.0 4.6 copy.87
  485.9 6.5 all-gather.20.cloned.1.call-done
  492.4 3.6 fusion.90
  503.1 2.5 convolution_bitcast_fusion.4
  509.2 8.7 multiply_reduce_fusion.2
  517.9 4.8 fusion.137
  522.8 10.6 %multiply_reduce_fusion.1 = (f32[4,512]{1,0:T(4,128)S(1)}, f32[4,512,1536]{2,1,0:T(8,128)}) fusion(f32[4,512,1536]{2,1,0:T(8,128)} %copy-done, f32[4,512]{1,0:T(4,128)S(1)} %log_add_fusion.1, bf16[512,4,64]{0,2,1:T(8,128)(2,1)S(1)} %bitcast.372, bf16[1,2048,4,64]{1,3,2,0:T(8,128)(2,1)S(1)} %copy-done.25), kind=kOutput, calls=%fused_computation.9 | convolution fusion | flops 412088320 | bytes 26230784 | tf_op jit(solution)/shard_map/qhd,khd->hqk/dot_general | solution.py:104
  533.4 6.8 fusion.72
  540.9 7.9 multiply_reduce_fusion
  548.8 3.0 fusion.81
  555.2 2.6 scatter-add.20
  557.8 6.9 multiply_convert_fusion.2
  564.8 13.9 %multiply_convert_fusion.1 = bf16[4,512,1536]{2,1,0:T(8,128)(2,1)} fusion(f32[4,512,1536]{2,1,0:T(8,128)} %get-tuple-element.169, f32[4,512,1536]{2,1,0:T(8,128)} %copy-done, f32[4,512]{1,0:T(4,128)S(1)} %get-tuple-element.168, f32[4,512]{1,0:T(4,128)S(1)} %log_add_fusion.1), kind=kLoop, calls=%fused_computation.8 | loop fusion | flops 15728640 | bytes 31473664 | tf_op jit(solution)/shard_map/convert_element_type | solution.py:111
  581.9 10.9 %multiply_convert_fusion = bf16[4,512,2048]{2,1,0:T(8,128)(2,1)} fusion(f32[4,512,2048]{2,1,0:T(8,128)} %get-tuple-element.171, f32[4,512,2048]{2,1,0:T(8,128)S(1)} %bitcast.339, f32[4,512]{1,0:T(4,128)S(1)} %get-tuple-element.170, f32[4,512]{1,0:T(4,128)S(1)} %log_add_fusion), kind=kLoop, calls=%fused_computation | loop fusion | flops 20971520 | bytes 41959424 | tf_op jit(solution)/shard_map/convert_element_type | solution.py:111
  595.2 5.8 fusion.160
  603.1 6.3 fusion.186
  611.6 3.1 copy.65
  616.7 4.6 fusion.133
  621.4 3.7 fusion.64
  625.1 5.6 fusion.65
  634.9 2.5 fusion.115
  639.2 4.7 fusion.121
  644.2 7.2 fusion.49
  652.8 10.0 %convert_bitcast_fusion = bf16[1,2048,1024]{2,1,0:T(8,128)(2,1)} fusion(bf16[704,1024]{1,0:T(8,128)(2,1)S(1)} %copy-done.71, f32[1,2048,2,704]{1,3,2,0:T(8,128)} %convolution_bitcast_fusion), kind=kOutput, calls=%fused_computation.71 | convolution fusion | flops 2963537920 | bytes 17170432 | tf_op jit(solution)/shard_map/rsf,fd->rsd/dot_general | solution.py:144
  665.7 10.6 %reduce.25 = bf16[2048,256]{1,0:T(8,128)(2,1)S(1)} reduce(bf16[2048,1,256]{2,1,0:T(2,128)(2,1)S(1)} %bitcast.356, bf16[]{:T(256)} %broadcast.620), dimensions={1}, to_apply=%bitcast.282.reduce_sub_computation | reduce | bytes 2097154
  678.0 3.8 all-to-all-start.1
  685.7 10.4 %all-to-all-done.1 = bf16[4,2,65536]{2,1,0:T(2,128)(2,1)S(1)} async-done(((bf16[4,2,65536]{2,1,0:T(2,128)(2,1)}), bf16[4,2,65536]{2,1,0:T(2,128)(2,1)S(1)}, u32[]{:S(2)}, u32[]{:S(2)}) %all-to-all-start.1) | async-done | bytes 1048608 | tf_op jit(solution)/shard_map/all_to_all | solution.py:273
  699.3 2.7 copy.72
  702.0 3.4 reshape.1310
  707.1 60.7 %reduce-scatter.23.cloned.1.call-done = bf16[128,3,256]{2,0,1:T(8,128)(2,1)} async-done(((bf16[1024,3,256]{2,0,1:T(8,128)(2,1)}), bf16[128,3,256]{2,0,1:T(8,128)(2,1)}) %reduce-scatter.23.cloned.1.call-update) | async-done | bytes 196624 | tf_op jit(solution)/shard_map/reduce_scatter | solution.py:282
  769.5 44.4 %reduce-scatter.21.cloned.1.call-done = bf16[1,512,1024]{2,1,0:T(8,128)(2,1)} async-done(((bf16[1,2048,1024]{2,1,0:T(8,128)(2,1)}), bf16[1,512,1024]{2,1,0:T(8,128)(2,1)}) %reduce-scatter.21.cloned.1.call-update) | async-done | bytes 1048592 | tf_op jit(solution)/shard_map/reduce_scatter | solution.py:276
  815.9 39.7 %all-reduce.2 = (f32[1024]{0:T(1024)}, f32[1024]{0:T(1024)}) all-reduce(f32[1024]{0:T(1024)S(1)} %get-tuple-element.123, f32[1024]{0:T(1024)S(1)} %copy-done.67), channel_id=1, replica_groups=mesh['dp'=8,'head'=4] {'dp','head'}, use_global_device_ids=true, to_apply=%region_28.29 | all-reduce | flops 2048 | bytes 16384 | tf_op jit(solution)/shard_map/psum | solution.py:295
  855.6 5.9 reduce-scatter.17.cloned.1.call-done
  861.5 4.3 fusion.97
  (290 shorter events, 99.9 us)
Async XLA Ops:
  7.2 6.6 copy-start.40
  7.2 73.7 %all-gather.10.cloned.1.call-start = ((), (), s32[]{:S(2)}) async-start(), calls=%async_computation.11 | async-start | bytes 1769472 | tf_op jit(solution)/shard_map/all_gather | solution.py:179
  9.1 91.0 %all-gather.8.cloned.1.call-start = ((), (), s32[]{:S(2)}) async-start(), calls=%async_computation.10 | async-start | bytes 5242880 | tf_op jit(solution)/shard_map/all_gather | solution.py:190
  15.6 13.8 %copy-start.72 = (s32[1,16]{1,0:T(1,128)S(1)}, s32[1,16]{1,0:T(1,128)}, u32[]{:S(2)}) copy-start(s32[1,16]{1,0:T(1,128)} %param.32) | copy-start | bytes 196
  15.6 14.3 %copy-start.59 = (bf16[256,128]{1,0:T(8,128)(2,1)S(1)}, bf16[256,128]{1,0:T(8,128)(2,1)}, u32[]{:S(2)}) copy-start(bf16[256,128]{1,0:T(8,128)(2,1)} %param.35) | copy-start | bytes 196612
  25.2 45.4 %all-to-all-start = ((bf16[4,2,65536]{2,1,0:T(2,128)(2,1)}), bf16[4,2,65536]{2,1,0:T(2,128)(2,1)S(1)}, u32[]{:S(2)}, u32[]{:S(2)}) async-start(bf16[4,2,65536]{2,1,0:T(2,128)(2,1)} %reshape.1326), calls=%async_computation | async-start | bytes 2097152 | tf_op jit(solution)/shard_map/all_to_all | solution.py:191
  29.4 179.7 %reduce-scatter.15.cloned.1.call-start = ((), (), s32[]{:S(2)}) async-start(), calls=%async_computation.12 | async-start | bytes 5242880 | tf_op jit(solution)/shard_map/reduce_scatter | solution.py:216
  68.9 65.5 %copy-start.11 = (f32[2048,64]{0,1:T(8,128)}, f32[2048,64]{0,1:T(8,128)S(1)}, u32[]{:S(2)}) copy-start(f32[2048,64]{0,1:T(8,128)S(1)} %get-tuple-element.151) | copy-start | bytes 1572868
  106.4 6.6 copy-start.9
  109.7 11.4 %copy-start.26 = (bf16[1,2048,4,64]{1,3,2,0:T(8,128)(2,1)}, bf16[1,2048,4,64]{1,3,2,0:T(8,128)(2,1)S(1)}, u32[]{:S(2)}) copy-start(bf16[1,2048,4,64]{1,3,2,0:T(8,128)(2,1)S(1)} %get-tuple-element.149) | copy-start | bytes 3145732
  109.7 11.4 %copy-start.28 = (bf16[1,2048,4,64]{1,3,2,0:T(8,128)(2,1)}, bf16[1,2048,4,64]{1,3,2,0:T(8,128)(2,1)S(1)}, u32[]{:S(2)}) copy-start(bf16[1,2048,4,64]{1,3,2,0:T(8,128)(2,1)S(1)} %get-tuple-element.148) | copy-start | bytes 3145732
  116.2 44.2 %copy-start.49 = (bf16[4,64,512]{2,1,0:T(8,128)(2,1)}, bf16[4,64,512]{2,1,0:T(8,128)(2,1)S(1)}, u32[]{:S(2)}) copy-start(bf16[4,64,512]{2,1,0:T(8,128)(2,1)S(1)} %fusion.146) | copy-start | bytes 786436
  135.7 8.6 copy-start.13
  144.3 8.2 copy-start.22
  152.5 7.9 copy-start.51
  152.5 7.9 copy-start.53
  152.5 8.6 copy-start.47
  161.1 48.0 %copy-start.2 = (bf16[1,512,1024]{2,1,0:T(8,128)(2,1)S(1)}, bf16[1,512,1024]{2,1,0:T(8,128)(2,1)}, u32[]{:S(2)}) copy-start(bf16[1,512,1024]{2,1,0:T(8,128)(2,1)} %param.30) | copy-start | bytes 3145732
  164.4 46.4 %copy-start.57 = (f32[1024]{0:T(1024)S(1)}, f32[1024]{0:T(1024)}, u32[]{:S(2)}) copy-start(f32[1024]{0:T(1024)} %param.39) | copy-start | bytes 12292
  164.4 106.8 %all-gather.14.cloned.1.call-start = ((), (), s32[]{:S(2)}) async-start(), calls=%async_computation.14 | async-start | bytes 3244032 | tf_op jit(solution)/shard_map/all_gather | solution.py:181
  165.0 141.0 %all-gather.12.cloned.1.call-start = ((), (), s32[]{:S(2)}) async-start(), calls=%async_computation.13 | async-start | bytes 5242880 | tf_op jit(solution)/shard_map/all_gather | solution.py:223
  210.8 243.7 %copy-start.60 = (f32[512]{0:T(512)}, f32[512]{0:T(512)S(1)}, u32[]{:S(2)}) copy-start(f32[512]{0:T(512)S(1)} %add_rsqrt_fusion) | copy-start | bytes 6148
  213.4 138.6 %all-gather.16.cloned.1.call-start = ((), (), s32[]{:S(2)}) async-start(), calls=%async_computation.15 | async-start | bytes 1622016 | tf_op jit(solution)/shard_map/all_gather | solution.py:182
  214.0 172.5 %all-gather.18.cloned.1.call-start = ((), (), s32[]{:S(2)}) async-start(), calls=%async_computation.17 | async-start | bytes 5242880 | tf_op jit(solution)/shard_map/all_gather | solution.py:229
  214.7 237.0 %reduce-scatter.19.cloned.1.call-start = ((), (), s32[]{:S(2)}) async-start(), calls=%async_computation.18 | async-start | bytes 5242880 | tf_op jit(solution)/shard_map/reduce_scatter | solution.py:233
  386.5 12.0 %copy-start.70 = (bf16[1024,2,704]{0,2,1:T(8,128)(2,1)S(1)}, bf16[1024,2,704]{0,2,1:T(8,128)(2,1)}, u32[]{:S(2)}) copy-start(bf16[1024,2,704]{0,2,1:T(8,128)(2,1)} %all-gather.14.cloned.1.call-done) | copy-start | bytes 8650756
  407.0 44.7 %copy-start.7 = (bf16[1,512,1024]{2,1,0:T(8,128)(2,1)S(1)}, bf16[1,512,1024]{2,1,0:T(8,128)(2,1)}, u32[]{:S(2)}) copy-start(bf16[1,512,1024]{2,1,0:T(8,128)(2,1)} %reduce-scatter.15.cloned.1.call-done) | copy-start | bytes 3145732
  407.0 85.4 %all-gather.20.cloned.1.call-start = ((), (), s32[]{:S(2)}) async-start(), calls=%async_computation.19 | async-start | bytes 5242880 | tf_op jit(solution)/shard_map/all_gather | solution.py:239
  454.4 12.1 %copy-start.65 = (f32[512]{0:T(512)}, f32[512]{0:T(512)S(1)}, u32[]{:S(2)}) copy-start(f32[512]{0:T(512)S(1)} %broadcast_multiply_fusion.2) | copy-start | bytes 6148
  457.8 224.0 %reduce-scatter.29.cloned.1.call-start = ((), (), s32[]{:S(2)}) async-start(), calls=%async_computation.24 | async-start | bytes 1769472
  468.1 215.5 %reduce-scatter.27.cloned.1.call-start = ((), (), s32[]{:S(2)}) async-start(), calls=%async_computation.23 | async-start | bytes 3244032
  485.6 219.8 %reduce-scatter.25.cloned.1.call-start = ((), (), s32[]{:S(2)}) async-start(), calls=%async_computation.22 | async-start | bytes 589824
  509.2 8.7 copy-start.38
  522.8 17.4 %slice-start = ((s8[16777216]{0:T(1024)(128)(4,1)}), s8[4194304]{0:T(1024)(128)(4,1)S(1)}, s32[]{:S(2)}) async-start(s8[16777216]{0:T(1024)(128)(4,1)} %bitcast.336), calls=%async_computation.25 | async-start | bytes 8388608
  522.8 17.4 %slice-start.1 = ((s8[16777216]{0:T(1024)(128)(4,1)}), s8[4194304]{0:T(1024)(128)(4,1)S(1)}, s32[]{:S(2)}) async-start(s8[16777216]{0:T(1024)(128)(4,1)} %bitcast.336), calls=%async_computation.26 | async-start | bytes 8388608
  522.8 17.4 %slice-start.2 = ((s8[16777216]{0:T(1024)(128)(4,1)}), s8[4194304]{0:T(1024)(128)(4,1)S(1)}, s32[]{:S(2)}) async-start(s8[16777216]{0:T(1024)(128)(4,1)} %bitcast.336), calls=%async_computation.27 | async-start | bytes 8388608
  533.4 7.3 slice-start.3
  533.4 7.5 copy-start.23
  551.8 12.9 %copy-start.16 = (bf16[2048,4,64]{0,2,1:T(8,128)(2,1)}, bf16[2048,4,64]{0,2,1:T(8,128)(2,1)S(1)}, u32[]{:S(2)}) copy-start(bf16[2048,4,64]{0,2,1:T(8,128)(2,1)S(1)} %fusion.81) | copy-start | bytes 3145732
  564.7 28.0 %copy-start.6 = (bf16[4,512,1024]{2,1,0:T(8,128)(2,1)}, bf16[4,512,1024]{2,1,0:T(8,128)(2,1)S(1)}, u32[]{:S(2)}) copy-start(bf16[4,512,1024]{2,1,0:T(8,128)(2,1)S(1)} %multiply_convert_fusion.2) | copy-start | bytes 12582916
  564.7 13.9 %slice-start.4 = ((s8[16777216]{0:T(1024)(128)(4,1)}), s8[4194304]{0:T(1024)(128)(4,1)S(1)}, s32[]{:S(2)}) async-start(s8[16777216]{0:T(1024)(128)(4,1)} %bitcast.338), calls=%async_computation.29 | async-start | bytes 8388608
  564.7 14.7 %slice-start.5 = ((s8[16777216]{0:T(1024)(128)(4,1)}), s8[4194304]{0:T(1024)(128)(4,1)S(1)}, s32[]{:S(2)}) async-start(s8[16777216]{0:T(1024)(128)(4,1)} %bitcast.338), calls=%async_computation.30 | async-start | bytes 8388608
  564.8 15.9 %slice-start.6 = ((s8[16777216]{0:T(1024)(128)(4,1)}), s8[4194304]{0:T(1024)(128)(4,1)S(1)}, s32[]{:S(2)}) async-start(s8[16777216]{0:T(1024)(128)(4,1)} %bitcast.338), calls=%async_computation.31 | async-start | bytes 8388608
  564.8 17.1 %slice-start.7 = ((s8[16777216]{0:T(1024)(128)(4,1)}), s8[4194304]{0:T(1024)(128)(4,1)S(1)}, s32[]{:S(2)}) async-start(s8[16777216]{0:T(1024)(128)(4,1)} %bitcast.338), calls=%async_computation.32 | async-start | bytes 8388608
  581.9 10.9 %copy-start.29 = (bf16[1,2048,4,64]{1,3,2,0:T(8,128)(2,1)S(1)}, bf16[1,2048,4,64]{1,3,2,0:T(8,128)(2,1)}, u32[]{:S(2)}) copy-start(bf16[1,2048,4,64]{1,3,2,0:T(8,128)(2,1)} %copy-done.28) | copy-start | bytes 3145732
  594.2 6.8 copy-start.31
  595.2 7.8 copy-start.14
  603.0 6.3 copy-start.32
  603.0 6.3 copy-start.33
  603.1 6.3 copy-start.34
  611.6 9.8 %slice-start.8 = ((s8[6291456]{0:T(1024)(128)(4,1)}), s8[2097152]{0:T(1024)(128)(4,1)S(1)}, s32[]{:S(2)}) async-start(s8[6291456]{0:T(1024)(128)(4,1)} %bitcast.340), calls=%async_computation.33 | async-start | bytes 4194304
  634.8 133.0 %reduce-scatter.23.cloned.1.call-start = ((), (), s32[]{:S(2)}) async-start(), calls=%async_computation.21 | async-start | bytes 1769472 | tf_op jit(solution)/shard_map/reduce_scatter | solution.py:282
  644.0 169.9 %reduce-scatter.21.cloned.1.call-start = ((), (), s32[]{:S(2)}) async-start(), calls=%async_computation.20 | async-start | bytes 5242880 | tf_op jit(solution)/shard_map/reduce_scatter | solution.py:276
  651.5 210.0 %reduce-scatter.17.cloned.1.call-start = ((), (), s32[]{:S(2)}) async-start(), calls=%async_computation.16 | async-start | bytes 5242880 | tf_op jit(solution)/shard_map/reduce_scatter | solution.py:225
  678.0 18.2 %all-to-all-start.1 = ((bf16[4,2,65536]{2,1,0:T(2,128)(2,1)}), bf16[4,2,65536]{2,1,0:T(2,128)(2,1)S(1)}, u32[]{:S(2)}, u32[]{:S(2)}) async-start(bf16[4,2,65536]{2,1,0:T(2,128)(2,1)} %reshape.1328), calls=%async_computation.5 | async-start | bytes 2097152 | tf_op jit(solution)/shard_map/all_to_all | solution.py:273
  699.3 114.6 %copy-start.3 = (bf16[1,512,1024]{2,1,0:T(8,128)(2,1)S(1)}, bf16[1,512,1024]{2,1,0:T(8,128)(2,1)}, u32[]{:S(2)}) copy-start(bf16[1,512,1024]{2,1,0:T(8,128)(2,1)} %param.30) | copy-start | bytes 3145732
  699.3 114.6 %copy-start.62 = (f32[1024]{0:T(1024)S(1)}, f32[1024]{0:T(1024)}, u32[]{:S(2)}) copy-start(f32[1024]{0:T(1024)} %param.38) | copy-start | bytes 12292
  699.3 114.6 %copy-start.64 = (f32[512]{0:T(512)S(1)}, f32[512]{0:T(512)}, u32[]{:S(2)}) copy-start(f32[512]{0:T(512)} %copy-done.63) | copy-start | bytes 6148
  702.0 113.9 %copy-start.67 = (f32[1024]{0:T(1024)S(1)}, f32[1024]{0:T(1024)}, u32[]{:S(2)}) copy-start(f32[1024]{0:T(1024)} %get-tuple-element.121) | copy-start | bytes 12292
  702.0 159.5 %copy-start.8 = (bf16[1,512,1024]{2,1,0:T(8,128)(2,1)S(1)}, bf16[1,512,1024]{2,1,0:T(8,128)(2,1)}, u32[]{:S(2)}) copy-start(bf16[1,512,1024]{2,1,0:T(8,128)(2,1)} %reduce-scatter.15.cloned.1.call-done) | copy-start | bytes 3145732
  702.0 159.5 %copy-start.15 = (bf16[1,512,1024]{2,1,0:T(8,128)(2,1)S(1)}, bf16[1,512,1024]{2,1,0:T(8,128)(2,1)}, u32[]{:S(2)}) copy-start(bf16[1,512,1024]{2,1,0:T(8,128)(2,1)} %param.33) | copy-start | bytes 3145732
  702.0 159.5 %copy-start.58 = (f32[1024]{0:T(1024)S(1)}, f32[1024]{0:T(1024)}, u32[]{:S(2)}) copy-start(f32[1024]{0:T(1024)} %param.39) | copy-start | bytes 12292
  702.0 159.5 %copy-start.61 = (f32[512]{0:T(512)S(1)}, f32[512]{0:T(512)}, u32[]{:S(2)}) copy-start(f32[512]{0:T(512)} %copy-done.60) | copy-start | bytes 6148
  702.0 159.5 %copy-start.66 = (f32[512]{0:T(512)S(1)}, f32[512]{0:T(512)}, u32[]{:S(2)}) copy-start(f32[512]{0:T(512)} %copy-done.65) | copy-start | bytes 6148
  (38 other events, 129.5 us)
Sparse Core Ops, SparseCore 0:
  10.6 51.3 all-gather.9
  64.2 35.7 all-gather.7
  164.5 44.5 reduce-scatter.14
  211.2 60.0 all-gather.13
  273.3 32.6 all-gather.11
  308.1 43.8 all-gather.15
  353.6 32.8 all-gather.17
  407.2 44.5 reduce-scatter.18
  457.9 34.4 all-gather.19
  495.7 64.8 reduce-scatter.28
  564.5 70.6 reduce-scatter.26
  638.8 61.0 reduce-scatter.24
  703.3 64.4 reduce-scatter.22
  770.4 43.4 reduce-scatter.20
  816.2 45.1 reduce-scatter.16
where the time goes:
time: 880 us; the launch traced here: 873 us
  waiting for transfers between devices  398 us (45%)
  matrix products  192 us (22%)
  other arithmetic  110 us (12%)
  local copies, waits for them, and re-layouts  76 us (9%)
  blocking collectives  72.9 us (8%)
  between operations  15.5 us (2%)
  starting transfers between devices  9.17 us (1%)
    reduce_scatter x1, waiting for transfers between devices, local(): lax.psum_scatter(grad_qkv.astype(jnp.bfloat16), 'dp', scatter_dimension=0...  60.7 us
    all_gather x1, waiting for transfers between devices, local(): lax.all_gather(gate_up_weight, 'dp', axis=0, tiled=True)  56.5 us
    reduce_scatter x1, waiting for transfers between devices, local(): lax.psum_scatter(grad_normed_part.astype(jnp.bfloat16), 'head', scatter_d...  44.5 us
    reduce_scatter x1, waiting for transfers between devices, local(): lax.psum_scatter(grad_normed_one_part.astype(jnp.bfloat16), 'head', scatt...  44.4 us
    reduce_scatter x1, waiting for transfers between devices, local(): lax.psum_scatter(attn_part.astype(jnp.bfloat16), 'head', scatter_dimensio...  44.1 us
    psum x1, blocking collectives, local(): lax.psum((gain_one_part, gain_two_part), ('dp', 'head'))  39.7 us
    unnamed x183, local copies, waits for them, and re-layouts  39 us
    all_gather x1, waiting for transfers between devices, local(): normed_full = lax.all_gather(normed_two, 'head', axis=1, tiled=True)  34.8 us
  transfers between devices with their start and end apart: 17, of which 12 were waited for; matrix products, arithmetic and copies ran while one was open for 31% of the time, Pallas kernels for 0%

commit v1 on v0

v1 whole, which is shorter than its diff:
```python
import functools
import math

import jax
import jax.numpy as jnp
from jax import lax
from jax.experimental import pallas as pl
from jax.experimental.pallas import tpu as pltpu
from jax.sharding import PartitionSpec as P

HEAD_DIM = 64
HALF = HEAD_DIM // 2
SEQ = 2048
NDOC = 16
NORM_EPS = 1e-06
NEG = -1e30
F32 = jnp.float32
BF16 = jnp.bfloat16
VMEM_LIMIT = 56 << 20

VMEM = pl.BlockSpec(memory_space=pltpu.VMEM)
SMEM = pl.BlockSpec(memory_space=pltpu.SMEM)


def shape(dims, dtype):
    return jax.ShapeDtypeStruct(dims, dtype)


def dot(a, b):
    return jnp.dot(a, b, preferred_element_type=F32)


def dot_nt(a, b):
    return lax.dot_general(a, b, (((1,), (1,)), ((), ())), preferred_element_type=F32)


def dot_tn(a, b):
    return lax.dot_general(a, b, (((0,), (0,)), ((), ())), preferred_element_type=F32)


def call(body, name, ins, outs, scratch=(), flops=0):
    moved = sum(a.size * a.dtype.itemsize for a, _ in ins)
    moved += sum(math.prod(o.shape) * o.dtype.itemsize for o in outs)
    return pl.pallas_call(
        body,
        name=name,
        out_shape=outs,
        in_specs=[s for _, s in ins],
        out_specs=[VMEM] * len(outs),
        scratch_shapes=list(scratch),
        compiler_params=pltpu.CompilerParams(vmem_limit_bytes=VMEM_LIMIT),
        cost_estimate=pl.CostEstimate(flops=flops, bytes_accessed=moved, transcendentals=0),
    )(*[a for a, _ in ins])


def in_vmem(*arrays):
    return [(a, VMEM) for a in arrays]


def row_scale(stream):
    return lax.rsqrt(jnp.mean(stream * stream, axis=-1, keepdims=True) + NORM_EPS)


def swap(value, axis, size, bit):
    return lax.ppermute(value, axis, [(i, i ^ bit) for i in range(size)])


def bits_down(size):
    return [1 << b for b in reversed(range(size.bit_length() - 1))]


def gather_relative(value, axis, size):
    parts = {0: value}
    for bit in bits_down(size):
        parts.update({j | bit: swap(v, axis, size, bit) for j, v in list(parts.items())})
    return [parts[j] for j in range(size)]


def sum_relative(parts, axis, size):
    parts = dict(enumerate(parts))
    bit = 1
    while bit < size:
        kept = {}
        for j in sorted((j for j in parts if not j & bit), reverse=True):
            got = swap(parts[j | bit], axis, size, bit)
            total = parts[j].astype(F32) + got.astype(F32)
            kept[j] = total if bit * 2 == size else total.astype(BF16)
        parts = kept
        bit *= 2
    return parts[0]


def exchange_relative(parts, axis, size):
    return [p if j == 0 else swap(p, axis, size, j) for j, p in enumerate(parts)]


def assemble_kernel(dp_ref, *refs):
    *parts, out = refs
    lanes = parts[0].shape[1]
    for j, part in enumerate(parts):
        out[:, pl.ds(pl.multiple_of((dp_ref[0] ^ j) * lanes, 128), lanes)] = part[...]


def gather_columns(value, dp, size):
    if value.shape[1] % 128:
        return lax.all_gather(value, "dp", axis=1, tiled=True)
    half = value.shape[0] // 2
    parts = [value[:half], value[half:]]
    for bit in bits_down(size):
        parts = [jnp.concatenate([p, swap(p, "dp", size, bit)], axis=0) for p in parts]
    order = [0]
    for bit in bits_down(size):
        order = order + [j | bit for j in order]
    place = [order.index(j) for j in range(size)]
    pieces = []
    for p in parts:
        p = p.reshape(size, half, value.shape[1])
        ins = [(dp, SMEM)] + in_vmem(*[p[i] for i in place])
        pieces += call(
            assemble_kernel, "assemble", ins, [shape((half, size * value.shape[1]), BF16)]
        )
    return pieces


def project_kernel(n, tile, me_ref, *refs):
    xs, fvs = refs[:n], refs[n : 2 * n]
    w_ref, gain_ref, cos_ref, sin_ref, q_out, k_out, kt_out, v_out, vt_out = refs[2 * n :]
    width = q_out.shape[0]
    shard = xs[0].shape[0]
    for j in range(n):

        def step(t, carry, j=j):
            rows = pl.ds(pl.multiple_of(t * tile, tile), tile)
            at = pl.ds(pl.multiple_of((me_ref[0] ^ j) * shard + t * tile, tile), tile)
            stream = xs[j][rows, :].astype(F32)
            normed = (stream * row_scale(stream) * gain_ref[...]).astype(BF16)
            qk = dot_nt(w_ref[: 2 * width, :], normed)
            cos, sin = cos_ref[:, at], sin_ref[:, at]
            turned = []
            for row in range(0, 2 * width, HEAD_DIM):
                first, second = qk[row : row + HALF], qk[row + HALF : row + HEAD_DIM]
                turned += [first * cos - second * sin, second * cos + first * sin]
            turned = jnp.concatenate(turned, axis=0)
            q_out[:, at] = (turned[:width] * HEAD_DIM ** (-0.5)).astype(BF16)
            keys = turned[width:]
            kt_out[:, at] = keys.astype(BF16)
            k_out[at, :] = keys.T.astype(BF16)
            values = 0.5 * dot_nt(normed, w_ref[2 * width :, :]) + 0.5 * fvs[j][rows, :].astype(F32)
            v_out[at, :] = values.astype(BF16)
            vt_out[:, at] = values.T.astype(BF16)
            return carry

        lax.fori_loop(0, shard // tile, step, 0)


def doc_of(len_ref, token):
    run, first, last = jnp.int32(0), jnp.int32(0), jnp.int32(SEQ)
    for doc in range(NDOC):
        end = run + len_ref[0, doc]
        inside = (token >= run) & (token < end)
        first, last = jnp.where(inside, run, first), jnp.where(inside, end, last)
        run = end
    return first, last


def attend_kernel(bq, heads, len_ref, me_ref, q_ref, k_ref, vt_ref, start_ref, ctx_ref, ot_ref, lse_ref, s_ref):
    bk = bq
    block = pl.program_id(0)
    first, _ = doc_of(len_ref, block * bq)
    starts = start_ref[...]

    def score(kb, tops, diagonal):
        at = pl.ds(pl.multiple_of(kb * bk, bk), bk)
        key_index = lax.broadcasted_iota(jnp.int32, (bk, bq), 0) + kb * bk
        allowed = key_index >= starts
        if diagonal:
            allowed &= key_index <= lax.broadcasted_iota(jnp.int32, (bk, bq), 1) + block * bq
        out = []
        for h in range(heads):
            rows = slice(h * HEAD_DIM, (h + 1) * HEAD_DIM)
            scores = jnp.where(allowed, dot(k_ref[at, rows], q_ref[rows, :]), NEG)
            s_ref[h, at, :] = scores
            out.append(jnp.maximum(tops[h], jnp.max(scores.reshape(bk // 8, 8, bq), axis=0)))
        return tuple(out)

    tops = score(block, tuple(jnp.full((8, bq), NEG, F32) for _ in range(heads)), True)
    tops = lax.fori_loop(first // bk, block, lambda kb, c: score(kb, c, False), tops)
    tops = [jnp.max(t, axis=0, keepdims=True) for t in tops]

    def gather(kb, carry):
        at = pl.ds(pl.multiple_of(kb * bk, bk), bk)
        out = []
        for h in range(heads):
            rows = slice(h * HEAD_DIM, (h + 1) * HEAD_DIM)
            total, acc = carry[h]
            probs = jnp.exp(s_ref[h, at, :] - tops[h])
            total = total + jnp.sum(probs.reshape(bk // 8, 8, bq), axis=0)
            out.append((total, acc + dot(vt_ref[rows, at], probs.astype(BF16))))
        return tuple(out)

    zero = tuple((jnp.zeros((8, bq), F32), jnp.zeros((HEAD_DIM, bq), F32)) for _ in range(heads))
    sums = lax.fori_loop(first // bk, block + 1, gather, zero)
    outs = []
    for h in range(heads):
        total = jnp.sum(sums[h][0], axis=0, keepdims=True)
        outs.append(sums[h][1] * (1.0 / total))
        lse_ref[h : h + 1, :] = tops[h] + jnp.log(total)
    out = jnp.concatenate(outs, axis=0)
    ot_ref[...] = out.astype(BF16)
    ctx_ref[...] = out.T.astype(BF16).reshape(ctx_ref.shape)


def attend(lengths, me, q_t, keys, v_t, starts, shard):
    width = q_t.shape[0]
    heads = width // HEAD_DIM
    bq = min(512, shard)
    per = shard // bq
    spec = pltpu.PrefetchScalarGridSpec(
        num_scalar_prefetch=2,
        grid=(SEQ // bq,),
        in_specs=[
            pl.BlockSpec((width, bq), lambda i, l, h: (0, i)),
            pl.BlockSpec((SEQ, width), lambda i, l, h: (0, 0)),
            pl.BlockSpec((width, SEQ), lambda i, l, h: (0, 0)),
            pl.BlockSpec((1, bq), lambda i, l, h: (0, i)),
        ],
        out_specs=[
            pl.BlockSpec((1, bq, width), lambda i, l, h: ((i // per) ^ h[0], i % per, 0)),
            pl.BlockSpec((width, bq), lambda i, l, h: (0, i)),
            pl.BlockSpec((heads, bq), lambda i, l, h: (0, i)),
        ],
        scratch_shapes=[pltpu.VMEM((heads, SEQ, bq), F32)],
    )
    return pl.pallas_call(
        functools.partial(attend_kernel, bq, heads),
        name="attend",
        grid_spec=spec,
        out_shape=[
            shape((SEQ // shard, shard, width), BF16),
            shape((width, SEQ), BF16),
            shape((heads, SEQ), F32),
        ],
        compiler_params=pltpu.CompilerParams(vmem_limit_bytes=VMEM_LIMIT),
        cost_estimate=pl.CostEstimate(
            flops=16 * SEQ * SEQ * width, bytes_accessed=8 * SEQ * width, transcendentals=0
        ),
    )(lengths, me, q_t, keys, v_t, starts)


def attend_back_kernel(n, block, len_ref, me_ref, *refs):
    q_ref, k_ref, kt_ref, v_ref, ot_ref, lse_ref, start_ref, cos_ref, sin_ref = refs[:9]
    dos = refs[9 : 9 + n]
    out_ref, dq_ref, dk_ref, dv_ref, do_ref, delta_ref = refs[9 + n :]
    width = q_ref.shape[0]
    heads = width // HEAD_DIM
    shard = SEQ // n
    for j in range(n):
        at = pl.ds(pl.multiple_of((me_ref[0] ^ j) * shard, shard), shard)
        do_ref[:, at] = dos[j][...]
        product = dos[j][...].astype(F32) * ot_ref[:, at].astype(F32)
        for h in range(heads):
            delta_ref[h : h + 1, at] = jnp.sum(
                product[h * HEAD_DIM : (h + 1) * HEAD_DIM], axis=0, keepdims=True
            )
    dq_ref[...] = jnp.zeros_like(dq_ref)
    dk_ref[...] = jnp.zeros_like(dk_ref)
    dv_ref[...] = jnp.zeros_like(dv_ref)

    def pair(kb, qb, diagonal):
        k_at = pl.ds(pl.multiple_of(kb * block, block), block)
        q_at = pl.ds(pl.multiple_of(qb * block, block), block)
        key_index = lax.broadcasted_iota(jnp.int32, (block, block), 0) + kb * block
        allowed = key_index >= start_ref[:, q_at]
        if diagonal:
            allowed &= key_index <= lax.broadcasted_iota(jnp.int32, (block, block), 1) + qb * block
        every = range(heads)
        rows = [slice(h * HEAD_DIM, (h + 1) * HEAD_DIM) for h in every]
        q_t = [q_ref[r, q_at] for r in rows]
        do_t = [do_ref[r, q_at] for r in rows]
        scores = [dot(k_ref[k_at, r], q_t[h]) for h, r in enumerate(rows)]
        dprobs = [dot(v_ref[k_at, r], do_t[h]) for h, r in enumerate(rows)]
        probs = [
            jnp.exp(jnp.where(allowed, scores[h], NEG) - lse_ref[h : h + 1, q_at]) for h in every
        ]
        dscores = [
            (probs[h] * (dprobs[h] - delta_ref[h : h + 1, q_at])).astype(BF16) for h in every
        ]
        probs = [p.astype(BF16) for p in probs]
        dv = [dot_nt(do_t[h], probs[h]) for h in every]
        dk = [dot_nt(q_t[h], dscores[h]) for h in every]
        dq = [dot(kt_ref[rows[h], k_at], dscores[h]) for h in every]
        for h in every:
            dv_ref[rows[h], k_at] += dv[h]
            dk_ref[rows[h], k_at] += dk[h]
            dq_ref[rows[h], q_at] += dq[h]

    def outer(kb, carry):
        _, end = doc_of(len_ref, kb * block + block - 1)
        pair(kb, kb, True)

        def inner(qb, c):
            pair(kb, qb, False)
            return c

        lax.fori_loop(kb + 1, (end - 1) // block + 1, inner, 0)
        return carry

    lax.fori_loop(0, SEQ // block, outer, 0)
    cos, sin = cos_ref[...], sin_ref[...]
    for base, ref, scale in ((0, dq_ref, HEAD_DIM ** (-0.5)), (width, dk_ref, 1.0)):
        for row in range(0, width, HEAD_DIM):
            first = ref[row : row + HALF, :] * scale
            second = ref[row + HALF : row + HEAD_DIM, :] * scale
            out_ref[base + row : base + row + HALF, :] = (first * cos + second * sin).astype(BF16)
            out_ref[base + row + HALF : base + row + HEAD_DIM, :] = (
                second * cos - first * sin
            ).astype(BF16)
    out_ref[2 * width :, :] = (0.5 * dv_ref[...]).astype(BF16)


def join_kernel(n, *refs):
    ctx, w_out = refs[:n], refs[n : 2 * n]
    x_ref, gain_ref, mid_ref, normed_ref = refs[2 * n :]
    total = x_ref[...].astype(F32)
    for c, w in zip(ctx, w_out):
        total = total + dot(c[...], w[...])
    mid_ref[...] = total
    normed_ref[...] = (total * row_scale(total) * gain_ref[...]).astype(BF16)


def mlp_kernel(n, tile, *refs):
    normed, grads = refs[:n], refs[n : 2 * n]
    gu_ref, down_ref, mixed_ref, dgate_ref, dup_ref, gn_ref = refs[2 * n :]
    for j in range(n):

        def step(t, carry, j=j):
            rows = pl.ds(pl.multiple_of(t * tile, tile), tile)
            tokens = normed[j][rows, :]
            gate = dot_nt(tokens, gu_ref[0])
            up = dot_nt(tokens, gu_ref[1])
            gm = dot_nt(grads[j][rows, :], down_ref[...])
            sig = 1.0 / (1.0 + jnp.exp(-gate))
            act = gate * sig
            mixed_ref[j, rows, :] = (act * up).astype(BF16)
            dup = (gm * act).astype(BF16)
            dgate = (gm * up * sig * (1.0 + gate * (1.0 - sig))).astype(BF16)
            dup_ref[j, rows, :] = dup
            dgate_ref[j, rows, :] = dgate
            gn_ref[j, rows, :] = (dot(dgate, gu_ref[0]) + dot(dup, gu_ref[1])).astype(BF16)
            return carry

        lax.fori_loop(0, normed[j].shape[0] // tile, step, 0)


def mlp_out_kernel(tile, mixed_ref, down_ref, out_ref):
    for j in range(mixed_ref.shape[0]):

        def step(t, carry, j=j):
            rows = pl.ds(pl.multiple_of(t * tile, tile), tile)
            out_ref[j, rows, :] = dot(mixed_ref[j, rows, :], down_ref[...]).astype(BF16)
            return carry

        lax.fori_loop(0, mixed_ref.shape[1] // tile, step, 0)


def mlp_weights_kernel(n, out_ref_count, *refs):
    normed, grads = refs[:n], refs[n : 2 * n]
    groups = refs[2 * n : -2]
    out_ref, acc_ref = refs[-2], refs[-1]
    hidden = acc_ref.shape[0]
    lanes = out_ref.shape[2]
    per = len(groups) // 3
    for which in range(3):
        for j in range(n):
            ref = groups[which * per + j // (n // per)]
            left = ref[j % (n // per)]
            right = (grads if which == 2 else normed)[j][...]
            part = dot_tn(left, right)
            if j == 0:
                acc_ref[...] = part
            else:
                acc_ref[...] += part
        for i in range(out_ref.shape[0]):
            out_ref[i, which * hidden : (which + 1) * hidden, :] = acc_ref[
                :, i * lanes : (i + 1) * lanes
            ].astype(BF16)


def middle_back_kernel(n, *refs):
    gn_ref, mid_ref, og_ref, gain_ref = refs[:4]
    w_out = refs[4 : 4 + n]
    gmid_ref, ga_ref, gain_out, *gctx = refs[4 + n :]
    mid = mid_ref[...]
    grad = gn_ref[...]
    scale = row_scale(mid)
    normed = mid * scale
    scaled = grad * gain_ref[...]
    back = scale * (scaled - normed * jnp.mean(scaled * normed, axis=-1, keepdims=True))
    gain_out[...] = jnp.sum(grad * normed, axis=0, keepdims=True)
    gmid = og_ref[...].astype(F32) + back
    gmid_ref[...] = gmid
    ga = gmid.astype(BF16)
    ga_ref[...] = ga
    for w, out in zip(w_out, gctx):
        out[...] = dot_nt(w[...], ga).astype(BF16)


def out_weight_kernel(n, *refs):
    ctx, ga_ref, outs = refs[:n], refs[n], refs[n + 1 :]
    for c, out in zip(ctx, outs):
        out[...] = dot_tn(c[...], ga_ref[...]).astype(BF16)


def unproject_kernel(n, tile, me_ref, *refs):
    xs = refs[:n]
    gp_ref, w_ref, gain_ref, gn_ref, dv_ref, gain_out = refs[n:]
    shard = xs[0].shape[0]
    width = w_ref.shape[0] // 3
    gain_out[...] = jnp.zeros_like(gain_out)
    for j in range(n):

        def step(t, carry, j=j):
            rows = pl.ds(pl.multiple_of(t * tile, tile), tile)
            at = pl.ds(pl.multiple_of((me_ref[0] ^ j) * shard + t * tile, tile), tile)
            gp = gp_ref[:, at].T
            dv_ref[j, rows, :] = gp[:, 2 * width :]
            grad = dot(gp, w_ref[...])
            gn_ref[j, rows, :] = grad.astype(BF16)
            stream = xs[j][rows, :].astype(F32)
            gain_out[...] += jnp.sum(grad * (stream * row_scale(stream)), axis=0, keepdims=True)
            return carry

        lax.fori_loop(0, shard // tile, step, 0)


def qkv_weight_kernel(n, me_ref, *refs):
    xs = refs[:n]
    gp_ref, gain_ref, out_ref, acc_ref = refs[n:]
    shard = xs[0].shape[0]
    lanes = out_ref.shape[2]
    for j in range(n):
        at = pl.ds(pl.multiple_of((me_ref[0] ^ j) * shard, shard), shard)
        stream = xs[j][...].astype(F32)
        normed = (stream * row_scale(stream) * gain_ref[...]).astype(BF16)
        part = dot(gp_ref[:, at], normed)
        if j == 0:
            acc_ref[...] = part
        else:
            acc_ref[...] += part
    for i in range(out_ref.shape[0]):
        out_ref[i] = acc_ref[:, i * lanes : (i + 1) * lanes].astype(BF16)


def input_back_kernel(gn_ref, x_ref, gain_ref, gmid_ref, out_ref):
    stream = x_ref[...].astype(F32)
    scale = row_scale(stream)
    normed = stream * scale
    scaled = gn_ref[...] * gain_ref[...]
    back = scale * (scaled - normed * jnp.mean(scaled * normed, axis=-1, keepdims=True))
    out_ref[...] = gmid_ref[...] + back


def doc_tables(lengths):
    index = jnp.arange(SEQ, dtype=jnp.int32)
    ends = jnp.cumsum(lengths)
    begins = ends - lengths
    starts = jnp.max(jnp.where(begins[:, None] <= index[None, :], begins[:, None], 0), axis=0)
    inverse = jnp.exp(jnp.arange(HALF, dtype=F32) * (-2.0 * math.log(10000.0) / HEAD_DIM))
    angles = (index - starts).astype(F32)[None, :] * inverse[:, None]
    return starts[None, :], jnp.cos(angles), jnp.sin(angles)


def local(
    n,
    n_dp,
    hidden_in,
    first_values,
    doc_lengths,
    out_grad,
    qkv_weight,
    out_weight,
    gate_up_weight,
    down_weight,
    attn_gain,
    mlp_gain,
):
    shard, width = hidden_in.shape[1], qkv_weight.shape[2]
    hidden = down_weight.shape[0]
    lanes = qkv_weight.shape[0]
    dim = hidden_in.shape[2]
    tile = min(256, shard)
    me = lax.axis_index("head").reshape(1).astype(jnp.int32)
    dp = lax.axis_index("dp").reshape(1).astype(jnp.int32)
    x_own, og_own = hidden_in[0], out_grad[0]
    gain_one, gain_two = attn_gain[None, :], mlp_gain[None, :]

    xs = gather_relative(x_own, "head", n)
    qkv_out = jnp.concatenate(
        [qkv_weight.transpose(1, 2, 0).reshape(3 * width, lanes), out_weight], axis=0
    )
    gathered = gather_columns(qkv_out, dp, n_dp)
    if isinstance(gathered, list):
        gathered = jnp.concatenate(gathered, axis=0)
    w_qkv, w_out = gathered[: 3 * width], gathered[3 * width :]
    mlp_rows = jnp.concatenate(
        [gate_up_weight.transpose(1, 2, 0).reshape(2 * hidden, lanes), down_weight], axis=0
    )
    mlp_all = lax.all_gather(mlp_rows, "dp", axis=1, tiled=True)
    w_gu = mlp_all[: 2 * hidden].reshape(2, hidden, dim)
    w_down = mlp_all[2 * hidden :]

    fv_parts = [
        lax.dynamic_slice(first_values[0], (0, (me[0] ^ j) * width), (shard, width))
        for j in range(n)
    ]
    fvs = exchange_relative(fv_parts, "head", n)
    starts, cos, sin = doc_tables(doc_lengths[0])

    q_t, keys, k_t, values, v_t = call(
        functools.partial(project_kernel, n, tile),
        "project",
        [(me, SMEM)] + in_vmem(*xs, *fvs, w_qkv, gain_one, cos, sin),
        [
            shape((width, SEQ), BF16),
            shape((SEQ, width), BF16),
            shape((width, SEQ), BF16),
            shape((SEQ, width), BF16),
            shape((width, SEQ), BF16),
        ],
        flops=6 * SEQ * dim * width,
    )
    ctx, o_t, lse = attend(doc_lengths, me, q_t, keys, v_t, starts, shard)

    ctxs = exchange_relative([ctx[j] for j in range(n)], "head", n)
    w_outs = gather_relative(w_out, "head", n)
    middle, normed_two = call(
        functools.partial(join_kernel, n),
        "join",
        in_vmem(*ctxs, *w_outs, x_own, gain_two),
        [shape((shard, dim), F32), shape((shard, dim), BF16)],
        flops=2 * shard * dim * dim,
    )

    ogs = gather_relative(og_own, "head", n)
    normed = gather_relative(normed_two, "head", n)
    half = n // 2
    mlp_flops = 10 * half * shard * dim * hidden
    groups = []
    for lo in (0, half):
        groups.append(
            call(
                functools.partial(mlp_kernel, half, tile),
                "mlp",
                in_vmem(*normed[lo : lo + half], *ogs[lo : lo + half], w_gu, w_down),
                [shape((half, shard, hidden), BF16)] * 3 + [shape((half, shard, dim), BF16)],
                flops=mlp_flops,
            )
        )
    gn_parts = [g[3][j] for g in groups for j in range(half)]
    gn_two = sum_relative(gn_parts, "head", n)

    mlp_parts = []
    for g in groups:
        (out,) = call(
            functools.partial(mlp_out_kernel, tile),
            "mlp_out",
            in_vmem(g[0], w_down),
            [shape((half, shard, dim), BF16)],
            flops=2 * half * shard * dim * hidden,
        )
        mlp_parts += [out[j] for j in range(half)]
    (mlp_grads,) = call(
        functools.partial(mlp_weights_kernel, n, 1),
        "mlp_weights",
        in_vmem(*normed, *ogs, *[groups[i][k] for k in (1, 2, 0) for i in range(2)]),
        [shape((n_dp, 3 * hidden, lanes), BF16)],
        [pltpu.VMEM((hidden, dim), F32)],
        flops=6 * SEQ * dim * hidden,
    )
    mlp_grads = lax.psum_scatter(mlp_grads, "dp", scatter_dimension=0, tiled=False).astype(F32)

    layer_out = (middle + sum_relative(mlp_parts, "head", n)).astype(BF16)

    grad_middle, ga, gain_two_part, *gctx = call(
        functools.partial(middle_back_kernel, n),
        "middle_back",
        in_vmem(gn_two, middle, og_own, gain_two, *w_outs),
        [shape((shard, dim), F32), shape((shard, dim), BF16), shape((1, dim), F32)]
        + [shape((width, shard), BF16)] * n,
        flops=2 * shard * dim * dim,
    )
    dos = exchange_relative(gctx, "head", n)
    out_parts = call(
        functools.partial(out_weight_kernel, n),
        "out_weight",
        in_vmem(*ctxs, ga),
        [shape((width, dim), BF16)] * n,
        flops=2 * shard * dim * dim,
    )
    out_sum = sum_relative(out_parts, "head", n).astype(BF16)

    (gp_t,) = call(
        functools.partial(attend_back_kernel, n, min(256, shard)),
        "attend_back",
        [(doc_lengths, SMEM), (me, SMEM)]
        + in_vmem(q_t, keys, k_t, values, o_t, lse, starts, cos, sin, *dos),
        [shape((3 * width, SEQ), BF16)],
        [pltpu.VMEM((width, SEQ), F32)] * 3
        + [pltpu.VMEM((width, SEQ), BF16), pltpu.VMEM((width // HEAD_DIM, SEQ), F32)],
        flops=20 * SEQ * SEQ * width,
    )
    gn_one_parts, dv, gain_one_part = call(
        functools.partial(unproject_kernel, n, tile),
        "unproject",
        [(me, SMEM)] + in_vmem(*xs, gp_t, w_qkv, gain_one),
        [shape((n, shard, dim), BF16), shape((n, shard, width), BF16), shape((1, dim), F32)],
        flops=6 * SEQ * dim * width,
    )
    gn_one = sum_relative([gn_one_parts[j] for j in range(n)], "head", n)
    (qkv_grads,) = call(
        functools.partial(qkv_weight_kernel, n),
        "qkv_weight",
        [(me, SMEM)] + in_vmem(*xs, gp_t, gain_one),
        [shape((n_dp, 3 * width, lanes), BF16)],
        [pltpu.VMEM((3 * width, dim), F32)],
        flops=6 * SEQ * dim * width,
    )
    attn_grads = jnp.concatenate(
        [qkv_grads, out_sum.reshape(width, n_dp, lanes).transpose(1, 0, 2)], axis=1
    )
    attn_grads = lax.psum_scatter(attn_grads, "dp", scatter_dimension=0, tiled=False).astype(F32)
    gains = lax.psum(jnp.concatenate([gain_one_part, gain_two_part], axis=0), ("dp", "head"))

    dvs = jnp.stack(exchange_relative([dv[j] for j in range(n)], "head", n))
    first_grad = jnp.concatenate(
        [lax.dynamic_index_in_dim(dvs, me[0] ^ i, keepdims=False) for i in range(n)], axis=1
    ).astype(F32)
    (input_grad,) = call(
        input_back_kernel,
        "input_back",
        in_vmem(gn_one, x_own, gain_one, grad_middle),
        [shape((shard, dim), F32)],
    )
    return (
        layer_out[None],
        input_grad[None],
        first_grad[None],
        attn_grads[: 3 * width].reshape(3, width, lanes).transpose(2, 0, 1),
        attn_grads[3 * width :],
        mlp_grads[: 2 * hidden].reshape(2, hidden, lanes).transpose(2, 0, 1),
        mlp_grads[2 * hidden :],
        gains[0],
        gains[1],
    )


def solution(mesh):
    tokens = P("dp", "head", None)
    columns = P("dp", None, "head")
    rows = P("head", "dp")
    return jax.shard_map(
        functools.partial(local, mesh.shape["head"], mesh.shape["dp"]),
        mesh=mesh,
        in_specs=(tokens, tokens, P("dp", None), tokens, columns, rows, columns, rows, P(), P()),
        out_specs=(tokens, tokens, tokens, columns, rows, columns, rows, P(), P()),
        check_vma=False,
    )
```

time: 880 us -> 501 us (0.57)
  waiting for transfers between devices: 398 us -> 150 us
  matrix products: 192 us -> 0 us
  Pallas kernels: 0 us -> 170 us
  other arithmetic: 110 us -> 26.9 us
  local copies, waits for them, and re-layouts: 76 us -> 35.1 us
  starting transfers between devices: 9.17 us -> 27.7 us
    reduce_scatter x5 -> x2, waiting for transfers between devices: 199 us -> 4.52 us  [the longest x1 4.51 us: local(): lax.psum_scatter(mlp_grads, 'dp', scatter_dimension=0, tiled=False)]
    dot_general x36 -> x0, matrix products: 192 us -> none  [the longest x4 28.1 us: attend_back(): jnp.einsum('qhd,khd->hqk', grad_context[first_q:last_q], value_rows[:last...]
    all_gather x7 -> x1, waiting for transfers between devices: 186 us -> 0.01 us  [local(): mlp_all = lax.all_gather(mlp_rows, 'dp', axis=1, tiled=True)]
    pallas_call x0 -> x16, Pallas kernels: none -> 170 us  [the longest x15 150 us: call(): pl.pallas_call(body, name=name, out_shape=outs, in_specs=[s for _, s in i...]
    ppermute x0 -> x42, waiting for transfers between devices: none -> 145 us  [swap(): return lax.ppermute(value, axis, [(i, i ^ bit) for i in range(size)])]
    convert_element_type x17 -> x8, other arithmetic: 51 us -> 9.68 us  [the longest x4 5.92 us: sum_relative(): kept[j] = total if bit * 2 == size else total.astype(BF16)]
    unnamed x183 -> x74, local copies, waits for them, and re-layouts: 39 us -> 4.05 us
    all_gather x1 -> x0, blocking collectives: 33.2 us -> none  [local(): lax.all_gather(out_weight, 'dp', axis=1, tiled=True)]
  transfers between devices with their start and end apart: 17 -> 45, of which waited for: 12 -> 18; matrix products, arithmetic and copies ran while one was open for 31% -> 10% of each run, Pallas kernels for 0% -> 32%
where the time goes in v1:
time: 501 us; the launch traced here: 492 us
  Pallas kernels  170 us (34%)
  waiting for transfers between devices  150 us (30%)
  blocking collectives  68.6 us (14%)
  local copies, waits for them, and re-layouts  35.1 us (7%)
  starting transfers between devices  27.7 us (6%)
  other arithmetic  26.9 us (5%)
  between operations  14.6 us (3%)
    pallas_call x15, Pallas kernels, call(): pl.pallas_call(body, name=name, out_shape=outs, in_specs=[s for _, s in i...  150 us
    ppermute x42, waiting for transfers between devices, swap(): return lax.ppermute(value, axis, [(i, i ^ bit) for i in range(size)])  145 us
    psum x1, blocking collectives, local(): lax.psum(jnp.concatenate([gain_one_part, gain_two_part], axis=0), ('dp',...  68.6 us
    ppermute x42, starting transfers between devices, swap(): return lax.ppermute(value, axis, [(i, i ^ bit) for i in range(size)])  27.3 us
    pallas_call x1, Pallas kernels, attend(): pl.pallas_call(functools.partial(attend_kernel, bq, heads), name='attend'...  20.1 us
  transfers between devices with their start and end apart: 45, of which 18 were waited for; matrix products, arithmetic and copies ran while one was open for 10% of the time, Pallas kernels for 32%

profile of v1, /device:TPU:0, one launch (start us, length us, event | category | flops | bytes accessed | tf_op | source)
XLA Modules:
  0.0 492.5 jit_solution(7587507454643498871)
XLA Ops:
  7.2 3.0 collective-permute-start.1
  10.3 1.1 copy.30
  12.2 2.7 collective-permute-start.9
  16.4 2.0 dynamic-slice_bitcast_fusion
  19.6 5.5 %collective-permute-done.9.refs_4_ = bf16[512,128]{1,0:T(8,128)(2,1)S(1)} collective-permute-done((bf16[512,128]{1,0:T(8,128)(2,1)S(1)}, bf16[512,128]{1,0:T(8,128)(2,1)S(1)}, u32[]{:S(2)}, u32[]{:S(2)}) %collective-permute-start.9) | collective-permute-done | bytes 131104 | tf_op jit(solution)/shard_map/ppermute | solution.py:65
  25.6 2.0 collective-permute-done.6.refs_4_
  28.3 11.9 %collective-permute-done.10 = bf16[1024,128]{1,0:T(8,128)(2,1)S(1)} collective-permute-done((bf16[1024,128]{1,0:T(8,128)(2,1)S(1)}, bf16[1024,128]{1,0:T(8,128)(2,1)S(1)}, u32[]{:S(2)}, u32[]{:S(2)}) %collective-permute-start.10) | collective-permute-done | bytes 262176 | tf_op jit(solution)/shard_map/ppermute | solution.py:65
  40.3 1.6 collective-permute-start.11
  41.8 1.8 multiply_sine_fusion
  43.6 4.6 collective-permute-done.7
  48.3 1.6 collective-permute-start.8
  51.4 2.6 assemble.3
  55.8 2.0 collective-permute-start.4
  57.9 2.9 collective-permute-done.8
  61.6 2.6 assemble.2
  64.2 2.5 pad_maximum_fusion.1.refs_8_.refs_5_
  66.7 8.7 %collective-permute-done.4.refs_6_ = bf16[512,256]{1,0:T(8,128)(2,1)S(1)} collective-permute-done((bf16[512,256]{1,0:T(8,128)(2,1)S(1)}, bf16[512,256]{1,0:T(8,128)(2,1)S(1)}, u32[]{:S(2)}, u32[]{:S(2)}) %collective-permute-start.4) | collective-permute-done | bytes 262176 | tf_op jit(solution)/shard_map/ppermute | solution.py:65
  76.0 4.3 collective-permute-done.5.refs_7_
  81.3 12.2 %project.1 = (bf16[256,2048]{1,0:T(8,128)(2,1)}, bf16[2048,256]{1,0:T(8,128)(2,1)}, bf16[256,2048]{1,0:T(8,128)(2,1)}, bf16[2048,256]{1,0:T(8,128)(2,1)}, bf16[256,2048]{1,0:T(8,128)(2,1)}) custom-call(s32[1]{0:T(128)} %bitcast.me_ref, bf16[512,1024]{1,0:T(8,128)(2,1)} %bitcast.99, bf16[512,1024]{1,0:T(8,128)(2,1)} %collective-permute-done.refs_1_, ...), custom_call_target="tpu_custom_call" | custom-call | flops 3221225472 | bytes 12587012 | tf_op jit(solution)/shard_map/project/pallas_call | solution.py:44
  93.5 20.1 %attend.1 = (bf16[4,512,256]{2,1,0:T(8,128)(2,1)}, bf16[256,2048]{1,0:T(8,128)(2,1)}, f32[4,2048]{1,0:T(4,128)}) custom-call(s32[1,16]{1,0:T(1,128)} %len_ref.3, s32[1]{0:T(128)} %bitcast.me_ref, bf16[256,2048]{1,0:T(8,128)(2,1)} %get-tuple-element.41.q_ref.refs_0_, bf16[2048,256]{1,0:T(8,128)(2,1)} %get-tuple-element.42.k_ref.refs_1_, ...), custom_call_target="tpu_custom_call" | custom-call | flops 17179869184 | bytes 4194304 | tf_op jit(solution)/shard_map/attend/pallas_call | solution.py:234
  113.7 2.0 slice_bitcast_fusion.12
  118.5 7.0 %collective-permute-done.13.refs_2_ = bf16[512,256]{1,0:T(8,128)(2,1)S(1)} collective-permute-done((bf16[512,256]{1,0:T(8,128)(2,1)S(1)}, bf16[512,256]{1,0:T(8,128)(2,1)S(1)}, u32[]{:S(2)}, u32[]{:S(2)}) %collective-permute-start.13) | collective-permute-done | bytes 262176 | tf_op jit(solution)/shard_map/ppermute | solution.py:65
  125.5 3.7 collective-permute-done.14.refs_3_
  129.9 5.2 %join.1 = (f32[512,1024]{1,0:T(8,128)}, bf16[512,1024]{1,0:T(8,128)(2,1)}) custom-call(bf16[512,256]{1,0:T(8,128)(2,1)} %get-tuple-element.86.refs_0_, bf16[512,256]{1,0:T(8,128)(2,1)} %copy-done.19, bf16[512,256]{1,0:T(8,128)(2,1)} %copy-done.20, bf16[512,256]{1,0:T(8,128)(2,1)} %copy-done.21, bf16[256,1024]{1,0:T(8,128)(2,1)} %copy-done.2, ...), custom_call_target="tpu_custom_call" | custom-call | flops 1073741824 | bytes 7344128 | tf_op jit(solution)/shard_map/join/pallas_call | solution.py:44
  135.1 1.5 collective-permute-start.21
  136.6 17.1 %collective-permute-done.23.refs_2_.refs_6_ = bf16[512,1024]{1,0:T(8,128)(2,1)} collective-permute-done((bf16[512,1024]{1,0:T(8,128)(2,1)S(1)}, bf16[512,1024]{1,0:T(8,128)(2,1)}, u32[]{:S(2)}, u32[]{:S(2)}) %collective-permute-start.23) | collective-permute-done | bytes 1048608 | tf_op jit(solution)/shard_map/ppermute | solution.py:65
  153.7 21.4 %collective-permute-done.21.refs_0_.refs_2_ = bf16[512,1024]{1,0:T(8,128)(2,1)S(1)} collective-permute-done((bf16[512,1024]{1,0:T(8,128)(2,1)}, bf16[512,1024]{1,0:T(8,128)(2,1)S(1)}, u32[]{:S(2)}, u32[]{:S(2)}) %collective-permute-start.21) | collective-permute-done | bytes 1048608 | tf_op jit(solution)/shard_map/ppermute | solution.py:65
  175.6 2.7 slice.237.refs_5_.down_ref
  178.3 3.6 slice.236
  181.9 17.3 %mlp.3 = (bf16[2,512,704]{2,1,0:T(8,128)(2,1)}, bf16[2,512,704]{2,1,0:T(8,128)(2,1)}, bf16[2,512,704]{2,1,0:T(8,128)(2,1)}, bf16[2,512,1024]{2,1,0:T(8,128)(2,1)}) custom-call(bf16[512,1024]{1,0:T(8,128)(2,1)} %copy-done.28, bf16[512,1024]{1,0:T(8,128)(2,1)} %collective-permute-done.22.refs_1_.refs_3_, ...), custom_call_target="tpu_custom_call" | custom-call | flops 7381975040 | bytes 14942208 | tf_op jit(solution)/shard_map/mlp/pallas_call | solution.py:44
  199.2 1.3 slice_bitcast_fusion.6
  201.0 17.1 %mlp.2 = (bf16[2,512,704]{2,1,0:T(8,128)(2,1)}, bf16[2,512,704]{2,1,0:T(8,128)(2,1)}, bf16[2,512,704]{2,1,0:T(8,128)(2,1)}, bf16[2,512,1024]{2,1,0:T(8,128)(2,1)}) custom-call(bf16[512,1024]{1,0:T(8,128)(2,1)} %get-tuple-element.46.refs_0_, bf16[512,1024]{1,0:T(8,128)(2,1)} %collective-permute-done.18.refs_1_, bf16[512,1024]{1,0:T(8,128)(2,1)} %bitcast.112, ...), custom_call_target="tpu_custom_call" | custom-call | flops 7381975040 | bytes 14942208 | tf_op jit(solution)/shard_map/mlp/pallas_call | solution.py:44
  218.1 1.4 slice_bitcast_fusion.7
  220.9 1.4 collective-permute-done.27
  222.3 23.4 %collective-permute-done.29 = bf16[512,1024]{1,0:T(8,128)(2,1)S(1)} collective-permute-done((bf16[512,1024]{1,0:T(8,128)(2,1)S(1)}, bf16[512,1024]{1,0:T(8,128)(2,1)S(1)}, u32[]{:S(2)}, u32[]{:S(2)}) %collective-permute-start.29) | collective-permute-done | bytes 1048608 | tf_op jit(solution)/shard_map/ppermute | solution.py:65
  245.7 1.9 convert_add_fusion.7.refs_0_
  247.6 6.2 %middle_back.1 = (f32[512,1024]{1,0:T(8,128)}, bf16[512,1024]{1,0:T(8,128)(2,1)}, f32[1,1024]{1,0:T(1,128)}, bf16[256,512]{1,0:T(8,128)(2,1)}, bf16[256,512]{1,0...) custom-call(f32[512,1024]{1,0:T(8,128)} %convert_add_fusion.7.refs_0_, ...), custom_call_target="tpu_custom_call" | custom-call | flops 1073741824 | bytes 11542528 | tf_op jit(solution)/shard_map/middle_back/pallas_call | solution.py:44
  253.9 3.7 out_weight.1
  260.2 1.2 add_convert_fusion.2
  261.9 5.3 %collective-permute-done.31.refs_11_ = bf16[256,512]{1,0:T(8,128)(2,1)S(1)} collective-permute-done((bf16[256,512]{1,0:T(8,128)(2,1)S(1)}, bf16[256,512]{1,0:T(8,128)(2,1)S(1)}, u32[]{:S(2)}, u32[]{:S(2)}) %collective-permute-start.31) | collective-permute-done | bytes 262176 | tf_op jit(solution)/shard_map/ppermute | solution.py:65
  267.2 3.9 collective-permute-done.32.refs_12_
  271.8 30.3 %attend_back.1.refs_4_ = bf16[768,2048]{1,0:T(8,128)(2,1)} custom-call(s32[1,16]{1,0:T(1,128)} %len_ref.3, s32[1]{0:T(128)} %bitcast.me_ref, bf16[256,2048]{1,0:T(8,128)(2,1)} %get-tuple-element.41.q_ref.refs_0_, bf16[2048,256]{1,0:T(8,128)(2,1)} %get-tuple-element.42.k_ref.refs_1_, bf16[256,2048]{1,0:T(8,128)(2,1)} %get-tuple-element.49.refs_2_, ...), custom_call_target="tpu_custom_call" | custom-call | flops 21474836480 | bytes 10002500 | tf_op jit(solution)/shard_map/attend_back/pallas_call | solution.py:44
  302.1 8.2 %qkv_weight.1 = bf16[8,768,128]{2,1,0:T(8,128)(2,1)} custom-call(s32[1]{0:T(128)} %bitcast.me_ref, bf16[512,1024]{1,0:T(8,128)(2,1)} %bitcast.101, bf16[512,1024]{1,0:T(8,128)(2,1)} %collective-permute-done.refs_1_, bf16[512,1024]{1,0:T(8,128)(2,1)} %collective-permute-done.1.refs_2_, bf16[512,1024]{1,0:T(8,128)(2,1)} %copy-done.27, ...), custom_call_target="tpu_custom_call" | custom-call | flops 3221225472 | bytes 8916996 | tf_op jit(solution)/shard_map/qkv_weight/pallas_call | solution.py:44
  310.6 1.2 copy-done.12
  311.7 1.6 pad_maximum_fusion
  313.6 17.3 %mlp_weights.1 = bf16[8,2112,128]{2,1,0:T(8,128)(2,1)} custom-call(bf16[512,1024]{1,0:T(8,128)(2,1)} %get-tuple-element.46.refs_0_, bf16[512,1024]{1,0:T(8,128)(2,1)} %collective-permute-done.18.refs_1_, bf16[512,1024]{1,0:T(8,128)(2,1)} %copy-done.28, bf16[512,1024]{1,0:T(8,128)(2,1)} %collective-permute-done.22.refs_1_.refs_3_, ...), custom_call_target="tpu_custom_call" | custom-call | flops 8858370048 | bytes 21364736 | tf_op jit(solution)/shard_map/mlp_weights/pallas_call | solution.py:44
  330.9 5.7 %mlp_out.3 = bf16[2,512,1024]{2,1,0:T(8,128)(2,1)} custom-call(bf16[2,512,704]{2,1,0:T(8,128)(2,1)} %get-tuple-element.48.mixed_ref.refs_13_, bf16[704,1024]{1,0:T(8,128)(2,1)} %slice.237.refs_5_.down_ref), custom_call_target="tpu_custom_call" | custom-call | flops 1476395008 | bytes 4980736 | tf_op jit(solution)/shard_map/mlp_out/pallas_call | solution.py:44
  336.6 1.3 slice_bitcast_fusion
  337.9 1.7 collective-permute-start.25
  339.5 5.4 %mlp_out.2 = bf16[2,512,1024]{2,1,0:T(8,128)(2,1)} custom-call(bf16[2,512,704]{2,1,0:T(8,128)(2,1)} %get-tuple-element.47.mixed_ref.refs_12_, bf16[704,1024]{1,0:T(8,128)(2,1)} %slice.237.refs_5_.down_ref), custom_call_target="tpu_custom_call" | custom-call | flops 1476395008 | bytes 4980736 | tf_op jit(solution)/shard_map/mlp_out/pallas_call | solution.py:44
  345.0 2.3 slice_bitcast_fusion.2
  347.3 10.9 %unproject.1 = (bf16[4,512,1024]{2,1,0:T(8,128)(2,1)}, bf16[4,512,256]{2,1,0:T(8,128)(2,1)}, f32[1,1024]{1,0:T(1,128)}) custom-call(s32[1]{0:T(128)} %bitcast.me_ref, bf16[512,1024]{1,0:T(8,128)(2,1)} %bitcast.102, bf16[512,1024]{1,0:T(8,128)(2,1)} %collective-permute-done.refs_1_, bf16[512,1024]{1,0:T(8,128)(2,1)} %collective-permute-done.1.refs_2_, ...), custom_call_target="tpu_custom_call" | custom-call | flops 3221225472 | bytes 14163972 | tf_op jit(solution)/shard_map/unproject/pallas_call | solution.py:44
  358.2 3.2 slice_bitcast_fusion.5
  361.9 1.4 fusion.4
  364.4 2.9 fusion
  368.2 21.4 %collective-permute-done.26 = bf16[512,1024]{1,0:T(8,128)(2,1)} collective-permute-done((bf16[512,1024]{1,0:T(8,128)(2,1)}, bf16[512,1024]{1,0:T(8,128)(2,1)}, u32[]{:S(2)}, u32[]{:S(2)}) %collective-permute-start.26) | collective-permute-done | bytes 1048608 | tf_op jit(solution)/shard_map/ppermute | solution.py:65
  389.6 3.6 fusion.6
  393.9 1.3 collective-permute-start.38
  395.2 68.6 %psum.7 = f32[2,1024]{1,0:T(2,128)S(1)} all-reduce(f32[2,1024]{1,0:T(2,128)S(1)} %pad_maximum_fusion.9), channel_id=1, replica_groups=mesh['dp'=8,'head'=4] {'dp','head'}, use_global_device_ids=true, to_apply=%region_4.5 | all-reduce | flops 2048 | bytes 16384 | tf_op jit(solution)/shard_map/psum | solution.py:632
  464.7 1.6 maximum_convert_fusion
  466.3 3.4 convert_add_fusion.6.gn_ref
  469.8 4.8 input_back.1
  478.1 4.5 reduce-scatter.5.cloned.1.call-done
  482.6 1.2 convert_element_type.188
  (174 shorter events, 30.0 us)
Async XLA Ops:
  7.2 11.2 %copy-start.18 = (bf16[128,2,704]{0,2,1:T(8,128)(2,1)S(1)}, bf16[128,2,704]{0,2,1:T(8,128)(2,1)}, u32[]{:S(2)}) copy-start(bf16[128,2,704]{0,2,1:T(8,128)(2,1)} %param.16) | copy-start | bytes 1081348
  7.2 11.1 %copy-start.22 = (bf16[704,128]{1,0:T(8,128)(2,1)S(1)}, bf16[704,128]{1,0:T(8,128)(2,1)}, u32[]{:S(2)}) copy-start(bf16[704,128]{1,0:T(8,128)(2,1)} %param.17) | copy-start | bytes 540676
  7.2 168.4 %all-gather.2.cloned.1.call-start = ((), (), s32[]{:S(2)}) async-start(), calls=%async_computation.2 | async-start | bytes 4866048 | tf_op jit(solution)/shard_map/all_gather | solution.py:508
  7.2 42.6 %collective-permute-start.1 = (bf16[512,1024]{1,0:T(8,128)(2,1)}, bf16[512,1024]{1,0:T(8,128)(2,1)}, u32[]{:S(2)}, u32[]{:S(2)}) collective-permute-start(bf16[512,1024]{1,0:T(8,128)(2,1)} %bitcast.97), channel_id=1, source_target_pairs={{0,2},{1,3},{2,0},{3,1},{4,6},{5,7},{6,4},{7,5},{8,10},{9,11},{10,... | collective-permute-start | bytes 3145736 | tf_op jit(solution)/shard_map/ppermute | solution.py:65
  10.3 70.0 %collective-permute-start = (bf16[512,1024]{1,0:T(8,128)(2,1)}, bf16[512,1024]{1,0:T(8,128)(2,1)}, u32[]{:S(2)}, u32[]{:S(2)}) collective-permute-start(bf16[512,1024]{1,0:T(8,128)(2,1)} %bitcast.98), channel_id=1, source_target_pairs={{0,1},{1,0},{2,3},{3,2},{4,5},{5,4},{6,7},{7,6},{8,9},{9,8},{10,11... | collective-permute-start | bytes 3145736 | tf_op jit(solution)/shard_map/ppermute | solution.py:65
  12.2 28.0 %copy-start.10 = (bf16[512,128]{1,0:T(8,128)(2,1)}, bf16[512,128]{1,0:T(8,128)(2,1)S(1)}, u32[]{:S(2)}) copy-start(bf16[512,128]{1,0:T(8,128)(2,1)S(1)} %pad_maximum_fusion.8.refs_0_) | copy-start | bytes 393220
  12.2 7.0 %copy-start.26 = (s32[1,16]{1,0:T(1,128)S(1)}, s32[1,16]{1,0:T(1,128)}, u32[]{:S(2)}) copy-start(s32[1,16]{1,0:T(1,128)} %len_ref.3) | copy-start | bytes 196
  12.2 12.9 %collective-permute-start.9 = (bf16[512,128]{1,0:T(8,128)(2,1)S(1)}, bf16[512,128]{1,0:T(8,128)(2,1)S(1)}, u32[]{:S(2)}, u32[]{:S(2)}) collective-permute-start(bf16[512,128]{1,0:T(8,128)(2,1)S(1)} %pad_maximum_fusion.8.refs_0_), channel_id=1, source_target_pairs={{0,16},{4,20},{8,24},{12,28},{16,0},{20,4},{24,8},{28,12},{1,17},{... | collective-permute-start | bytes 393224 | tf_op jit(solution)/shard_map/ppermute | solution.py:65
  15.9 32.3 %copy-start.11 = (bf16[2,256,128]{2,1,0:T(8,128)(2,1)}, bf16[2,256,128]{2,1,0:T(8,128)(2,1)S(1)}, u32[]{:S(2)}) copy-start(bf16[2,256,128]{2,1,0:T(8,128)(2,1)S(1)} %copy.29) | copy-start | bytes 393220
  16.0 11.6 %collective-permute-start.6 = (bf16[512,128]{1,0:T(8,128)(2,1)S(1)}, bf16[512,128]{1,0:T(8,128)(2,1)S(1)}, u32[]{:S(2)}, u32[]{:S(2)}) collective-permute-start(bf16[512,128]{1,0:T(8,128)(2,1)S(1)} %bitcast.107), channel_id=1, source_target_pairs={{0,16},{4,20},{8,24},{12,28},{16,0},{20,4},{24,8},{28,12},{1,17},{... | collective-permute-start | bytes 393224 | tf_op jit(solution)/shard_map/ppermute | solution.py:65
  18.3 37.5 %collective-permute-start.3 = (bf16[512,256]{1,0:T(8,128)(2,1)S(1)}, bf16[512,256]{1,0:T(8,128)(2,1)}, u32[]{:S(2)}, u32[]{:S(2)}) collective-permute-start(bf16[512,256]{1,0:T(8,128)(2,1)S(1)} %get-tuple-element.88), channel_id=1, source_target_pairs={{0,1},{1,0},{2,3},{3,2},{4,5},{5,4},{6,7},{7,6},{8,9},{9,8},{10,11... | collective-permute-start | bytes 786440 | tf_op jit(solution)/shard_map/ppermute | solution.py:65
  19.2 455.4 %reduce-scatter.3.cloned.1.call-start = ((), (), s32[]{:S(2)}) async-start(), calls=%async_computation.3 | async-start | bytes 2359296 | tf_op jit(solution)/shard_map/reduce_scatter | solution.py:631
  19.6 30.9 %copy-start.23 = (s32[2048]{0:T(1024)}, s32[2048]{0:T(1024)S(1)}, u32[]{:S(2)}) copy-start(s32[2048]{0:T(1024)S(1)} %select_reduce_fusion) | copy-start | bytes 24580
  25.1 25.4 %copy-start.14 = (bf16[512,128]{1,0:T(8,128)(2,1)}, bf16[512,128]{1,0:T(8,128)(2,1)S(1)}, u32[]{:S(2)}) copy-start(bf16[512,128]{1,0:T(8,128)(2,1)S(1)} %collective-permute-done.9.refs_4_) | copy-start | bytes 393220
  25.1 15.1 %collective-permute-start.10 = (bf16[1024,128]{1,0:T(8,128)(2,1)S(1)}, bf16[1024,128]{1,0:T(8,128)(2,1)S(1)}, u32[]{:S(2)}, u32[]{:S(2)}) collective-permute-start(bf16[1024,128]{1,0:T(8,128)(2,1)S(1)} %pad_maximum_fusion.7), channel_id=1, source_target_pairs={{0,8},{4,12},{8,0},{12,4},{16,24},{20,28},{24,16},{28,20},{1,9},{5... | collective-permute-start | bytes 786440 | tf_op jit(solution)/shard_map/ppermute | solution.py:65
  27.6 23.8 %copy-start.13 = (bf16[512,128]{1,0:T(8,128)(2,1)}, bf16[512,128]{1,0:T(8,128)(2,1)S(1)}, u32[]{:S(2)}) copy-start(bf16[512,128]{1,0:T(8,128)(2,1)S(1)} %collective-permute-done.6.refs_4_) | copy-start | bytes 393220
  27.6 20.6 %collective-permute-start.7 = (bf16[1024,128]{1,0:T(8,128)(2,1)S(1)}, bf16[1024,128]{1,0:T(8,128)(2,1)S(1)}, u32[]{:S(2)}, u32[]{:S(2)}) collective-permute-start(bf16[1024,128]{1,0:T(8,128)(2,1)S(1)} %pad_maximum_fusion.6), channel_id=1, source_target_pairs={{0,8},{4,12},{8,0},{12,4},{16,24},{20,28},{24,16},{28,20},{1,9},{5... | collective-permute-start | bytes 786440 | tf_op jit(solution)/shard_map/ppermute | solution.py:65
  40.3 10.3 %collective-permute-start.11 = (bf16[2048,128]{1,0:T(8,128)(2,1)S(1)}, bf16[2048,128]{1,0:T(8,128)(2,1)S(1)}, u32[]{:S(2)}, u32[]{:S(2)}) collective-permute-start(bf16[2048,128]{1,0:T(8,128)(2,1)S(1)} %pad_maximum_fusion.5), channel_id=1, source_target_pairs={{0,4},{4,0},{8,12},{12,8},{16,20},{20,16},{24,28},{28,24},{1,5},{5... | collective-permute-start | bytes 1572872 | tf_op jit(solution)/shard_map/ppermute | solution.py:65
  48.3 12.5 %collective-permute-start.8 = (bf16[2048,128]{1,0:T(8,128)(2,1)S(1)}, bf16[2048,128]{1,0:T(8,128)(2,1)S(1)}, u32[]{:S(2)}, u32[]{:S(2)}) collective-permute-start(bf16[2048,128]{1,0:T(8,128)(2,1)S(1)} %pad_maximum_fusion.4), channel_id=1, source_target_pairs={{0,4},{4,0},{8,12},{12,8},{16,20},{20,16},{24,28},{28,24},{1,5},{5... | collective-permute-start | bytes 1572872 | tf_op jit(solution)/shard_map/ppermute | solution.py:65
  49.8 30.5 %collective-permute-start.2 = (bf16[512,1024]{1,0:T(8,128)(2,1)}, bf16[512,1024]{1,0:T(8,128)(2,1)S(1)}, u32[]{:S(2)}, u32[]{:S(2)}) collective-permute-start(bf16[512,1024]{1,0:T(8,128)(2,1)} %collective-permute-done.1.refs_2_), channel_id=1, source_target_pairs={{0,1},{1,0},{2,3},{3,2},{4,5},{5,4},{6,7},{7,6},{8,9},{9,8},{10,11... | collective-permute-start | bytes 3145736 | tf_op jit(solution)/shard_map/ppermute | solution.py:65
  55.0 20.4 %copy-start.2 = (bf16[256,1024]{1,0:T(8,128)(2,1)}, bf16[256,1024]{1,0:T(8,128)(2,1)S(1)}, u32[]{:S(2)}) copy-start(bf16[256,1024]{1,0:T(8,128)(2,1)S(1)} %slice.235.refs_4_) | copy-start | bytes 1572868
  55.0 9.2 %copy-start.1 = (bf16[512,1024]{1,0:T(8,128)(2,1)S(1)}, bf16[512,1024]{1,0:T(8,128)(2,1)}, u32[]{:S(2)}) copy-start(bf16[512,1024]{1,0:T(8,128)(2,1)} %assemble.3) | copy-start | bytes 3145732
  55.0 20.4 %collective-permute-start.16 = (bf16[256,1024]{1,0:T(8,128)(2,1)S(1)}, bf16[256,1024]{1,0:T(8,128)(2,1)S(1)}, u32[]{:S(2)}, u32[]{:S(2)}) collective-permute-start(bf16[256,1024]{1,0:T(8,128)(2,1)S(1)} %slice.235.refs_4_), channel_id=1, source_target_pairs={{0,2},{1,3},{2,0},{3,1},{4,6},{5,7},{6,4},{7,5},{8,10},{9,11},{10,... | collective-permute-start | bytes 1572872 | tf_op jit(solution)/shard_map/ppermute | solution.py:65
  55.8 19.6 %collective-permute-start.4 = (bf16[512,256]{1,0:T(8,128)(2,1)S(1)}, bf16[512,256]{1,0:T(8,128)(2,1)S(1)}, u32[]{:S(2)}, u32[]{:S(2)}) collective-permute-start(bf16[512,256]{1,0:T(8,128)(2,1)S(1)} %get-tuple-element.90), channel_id=1, source_target_pairs={{0,2},{1,3},{2,0},{3,1},{4,6},{5,7},{6,4},{7,5},{8,10},{9,11},{10,... | collective-permute-start | bytes 786440 | tf_op jit(solution)/shard_map/ppermute | solution.py:65
  60.8 19.5 %collective-permute-start.5 = (bf16[512,256]{1,0:T(8,128)(2,1)S(1)}, bf16[512,256]{1,0:T(8,128)(2,1)S(1)}, u32[]{:S(2)}, u32[]{:S(2)}) collective-permute-start(bf16[512,256]{1,0:T(8,128)(2,1)S(1)} %get-tuple-element.87), channel_id=1, source_target_pairs={{0,3},{1,2},{2,1},{3,0},{4,7},{5,6},{6,5},{7,4},{8,11},{9,10},{10,... | collective-permute-start | bytes 786440 | tf_op jit(solution)/shard_map/ppermute | solution.py:65
  75.4 42.2 %collective-permute-start.15 = (bf16[256,1024]{1,0:T(8,128)(2,1)S(1)}, bf16[256,1024]{1,0:T(8,128)(2,1)S(1)}, u32[]{:S(2)}, u32[]{:S(2)}) collective-permute-start(bf16[256,1024]{1,0:T(8,128)(2,1)S(1)} %slice.235.refs_4_), channel_id=1, source_target_pairs={{0,1},{1,0},{2,3},{3,2},{4,5},{5,4},{6,7},{7,6},{8,9},{9,8},{10,11... | collective-permute-start | bytes 1572872 | tf_op jit(solution)/shard_map/ppermute | solution.py:65
  75.5 18.1 %copy-start.4 = (bf16[256,1024]{1,0:T(8,128)(2,1)}, bf16[256,1024]{1,0:T(8,128)(2,1)S(1)}, u32[]{:S(2)}) copy-start(bf16[256,1024]{1,0:T(8,128)(2,1)S(1)} %collective-permute-done.16.refs_6_) | copy-start | bytes 1572868
  75.5 43.0 %collective-permute-start.17 = (bf16[256,1024]{1,0:T(8,128)(2,1)S(1)}, bf16[256,1024]{1,0:T(8,128)(2,1)S(1)}, u32[]{:S(2)}, u32[]{:S(2)}) collective-permute-start(bf16[256,1024]{1,0:T(8,128)(2,1)S(1)} %collective-permute-done.16.refs_6_), channel_id=1, source_target_pairs={{0,1},{1,0},{2,3},{3,2},{4,5},{5,4},{6,7},{7,6},{8,9},{9,8},{10,11... | collective-permute-start | bytes 1572872 | tf_op jit(solution)/shard_map/ppermute | solution.py:65
  115.7 2.7 collective-permute-start.12
  116.3 9.2 %collective-permute-start.13 = (bf16[512,256]{1,0:T(8,128)(2,1)S(1)}, bf16[512,256]{1,0:T(8,128)(2,1)S(1)}, u32[]{:S(2)}, u32[]{:S(2)}) collective-permute-start(bf16[512,256]{1,0:T(8,128)(2,1)S(1)} %get-tuple-element.84), channel_id=1, source_target_pairs={{0,2},{1,3},{2,0},{3,1},{4,6},{5,7},{6,4},{7,5},{8,10},{9,11},{10,... | collective-permute-start | bytes 786440 | tf_op jit(solution)/shard_map/ppermute | solution.py:65
  116.6 12.6 %collective-permute-start.14 = (bf16[512,256]{1,0:T(8,128)(2,1)S(1)}, bf16[512,256]{1,0:T(8,128)(2,1)S(1)}, u32[]{:S(2)}, u32[]{:S(2)}) collective-permute-start(bf16[512,256]{1,0:T(8,128)(2,1)S(1)} %get-tuple-element.83), channel_id=1, source_target_pairs={{0,3},{1,2},{2,1},{3,0},{4,7},{5,6},{6,5},{7,4},{8,11},{9,10},{10,... | collective-permute-start | bytes 786440 | tf_op jit(solution)/shard_map/ppermute | solution.py:65
  117.7 11.5 %copy-start.5 = (bf16[256,1024]{1,0:T(8,128)(2,1)}, bf16[256,1024]{1,0:T(8,128)(2,1)S(1)}, u32[]{:S(2)}) copy-start(bf16[256,1024]{1,0:T(8,128)(2,1)S(1)} %collective-permute-done.15.refs_5_) | copy-start | bytes 1572868
  117.7 36.0 %collective-permute-start.23 = (bf16[512,1024]{1,0:T(8,128)(2,1)S(1)}, bf16[512,1024]{1,0:T(8,128)(2,1)}, u32[]{:S(2)}, u32[]{:S(2)}) collective-permute-start(bf16[512,1024]{1,0:T(8,128)(2,1)S(1)} %bitcast.115), channel_id=1, source_target_pairs={{0,2},{1,3},{2,0},{3,1},{4,6},{5,7},{6,4},{7,5},{8,10},{9,11},{10,... | collective-permute-start | bytes 3145736 | tf_op jit(solution)/shard_map/ppermute | solution.py:65
  118.5 10.7 %copy-start.6 = (bf16[256,1024]{1,0:T(8,128)(2,1)}, bf16[256,1024]{1,0:T(8,128)(2,1)S(1)}, u32[]{:S(2)}) copy-start(bf16[256,1024]{1,0:T(8,128)(2,1)S(1)} %collective-permute-done.17.refs_7_) | copy-start | bytes 1572868
  118.5 10.7 %copy-start.19 = (bf16[512,256]{1,0:T(8,128)(2,1)}, bf16[512,256]{1,0:T(8,128)(2,1)S(1)}, u32[]{:S(2)}) copy-start(bf16[512,256]{1,0:T(8,128)(2,1)S(1)} %collective-permute-done.12.refs_1_) | copy-start | bytes 786436
  135.1 40.0 %collective-permute-start.21 = (bf16[512,1024]{1,0:T(8,128)(2,1)}, bf16[512,1024]{1,0:T(8,128)(2,1)S(1)}, u32[]{:S(2)}, u32[]{:S(2)}) collective-permute-start(bf16[512,1024]{1,0:T(8,128)(2,1)} %get-tuple-element.46.refs_0_), channel_id=1, source_target_pairs={{0,2},{1,3},{2,0},{3,1},{4,6},{5,7},{6,4},{7,5},{8,10},{9,11},{10,... | collective-permute-start | bytes 3145736 | tf_op jit(solution)/shard_map/ppermute | solution.py:65
  153.7 28.2 %collective-permute-start.24 = (bf16[512,1024]{1,0:T(8,128)(2,1)}, bf16[512,1024]{1,0:T(8,128)(2,1)}, u32[]{:S(2)}, u32[]{:S(2)}) collective-permute-start(bf16[512,1024]{1,0:T(8,128)(2,1)} %collective-permute-done.23.refs_2_.refs_6_), channel_id=1, source_target_pairs={{0,1},{1,0},{2,3},{3,2},{4,5},{5,4},{6,7},{7,6},{8,9},{9,8},{10,11... | collective-permute-start | bytes 3145736 | tf_op jit(solution)/shard_map/ppermute | solution.py:65
  175.1 6.8 %collective-permute-start.22 = (bf16[512,1024]{1,0:T(8,128)(2,1)S(1)}, bf16[512,1024]{1,0:T(8,128)(2,1)}, u32[]{:S(2)}, u32[]{:S(2)}) collective-permute-start(bf16[512,1024]{1,0:T(8,128)(2,1)S(1)} %collective-permute-done.21.refs_0_.refs_2_), channel_id=1, source_target_pairs={{0,1},{1,0},{2,3},{3,2},{4,5},{5,4},{6,7},{7,6},{8,9},{9,8},{10,11... | collective-permute-start | bytes 3145736 | tf_op jit(solution)/shard_map/ppermute | solution.py:65
  175.1 25.9 %collective-permute-start.19 = (bf16[512,1024]{1,0:T(8,128)(2,1)S(1)}, bf16[512,1024]{1,0:T(8,128)(2,1)}, u32[]{:S(2)}, u32[]{:S(2)}) collective-permute-start(bf16[512,1024]{1,0:T(8,128)(2,1)S(1)} %bitcast.116), channel_id=1, source_target_pairs={{0,1},{1,0},{2,3},{3,2},{4,5},{5,4},{6,7},{7,6},{8,9},{9,8},{10,11... | collective-permute-start | bytes 3145736 | tf_op jit(solution)/shard_map/ppermute | solution.py:65
  175.6 25.4 %collective-permute-start.18 = (bf16[512,1024]{1,0:T(8,128)(2,1)}, bf16[512,1024]{1,0:T(8,128)(2,1)}, u32[]{:S(2)}, u32[]{:S(2)}) collective-permute-start(bf16[512,1024]{1,0:T(8,128)(2,1)} %get-tuple-element.46.refs_0_), channel_id=1, source_target_pairs={{0,1},{1,0},{2,3},{3,2},{4,5},{5,4},{6,7},{7,6},{8,9},{9,8},{10,11... | collective-permute-start | bytes 3145736 | tf_op jit(solution)/shard_map/ppermute | solution.py:65
  200.5 19.2 %collective-permute-start.28 = (bf16[512,1024]{1,0:T(8,128)(2,1)S(1)}, bf16[512,1024]{1,0:T(8,128)(2,1)S(1)}, u32[]{:S(2)}, u32[]{:S(2)}) collective-permute-start(bf16[512,1024]{1,0:T(8,128)(2,1)S(1)} %slice_bitcast_fusion.6), channel_id=1, source_target_pairs={{0,1},{1,0},{2,3},{3,2},{4,5},{5,4},{6,7},{7,6},{8,9},{9,8},{10,11... | collective-permute-start | bytes 3145736 | tf_op jit(solution)/shard_map/ppermute | solution.py:65
  219.6 26.1 %copy-start.9 = (bf16[2,512,1024]{2,1,0:T(8,128)(2,1)S(1)}, bf16[2,512,1024]{2,1,0:T(8,128)(2,1)}, u32[]{:S(2)}) copy-start(bf16[2,512,1024]{2,1,0:T(8,128)(2,1)} %get-tuple-element.53) | copy-start | bytes 6291460
  219.6 2.7 collective-permute-start.27
  220.4 25.3 %collective-permute-start.29 = (bf16[512,1024]{1,0:T(8,128)(2,1)S(1)}, bf16[512,1024]{1,0:T(8,128)(2,1)S(1)}, u32[]{:S(2)}, u32[]{:S(2)}) collective-permute-start(bf16[512,1024]{1,0:T(8,128)(2,1)S(1)} %fusion.2), channel_id=1, source_target_pairs={{0,2},{1,3},{2,0},{3,1},{4,6},{5,7},{6,4},{7,5},{8,10},{9,11},{10,... | collective-permute-start | bytes 3145736 | tf_op jit(solution)/shard_map/ppermute | solution.py:65
  257.6 2.7 collective-permute-start.40
  257.6 4.4 collective-permute-start.30
  258.1 9.2 %collective-permute-start.31 = (bf16[256,512]{1,0:T(8,128)(2,1)S(1)}, bf16[256,512]{1,0:T(8,128)(2,1)S(1)}, u32[]{:S(2)}, u32[]{:S(2)}) collective-permute-start(bf16[256,512]{1,0:T(8,128)(2,1)S(1)} %copy-done.32), channel_id=1, source_target_pairs={{0,2},{1,3},{2,0},{3,1},{4,6},{5,7},{6,4},{7,5},{8,10},{9,11},{10,... | collective-permute-start | bytes 786440 | tf_op jit(solution)/shard_map/ppermute | solution.py:65
  258.5 12.6 %collective-permute-start.32 = (bf16[256,512]{1,0:T(8,128)(2,1)S(1)}, bf16[256,512]{1,0:T(8,128)(2,1)S(1)}, u32[]{:S(2)}, u32[]{:S(2)}) collective-permute-start(bf16[256,512]{1,0:T(8,128)(2,1)S(1)} %copy-done.30), channel_id=1, source_target_pairs={{0,3},{1,2},{2,1},{3,0},{4,7},{5,6},{6,5},{7,4},{8,11},{9,10},{10,... | collective-permute-start | bytes 786440 | tf_op jit(solution)/shard_map/ppermute | solution.py:65
  259.5 50.8 %collective-permute-start.39 = (bf16[256,1024]{1,0:T(8,128)(2,1)}, bf16[256,1024]{1,0:T(8,128)(2,1)S(1)}, u32[]{:S(2)}, u32[]{:S(2)}) collective-permute-start(bf16[256,1024]{1,0:T(8,128)(2,1)} %get-tuple-element.64), channel_id=1, source_target_pairs={{0,1},{1,0},{2,3},{3,2},{4,5},{5,4},{6,7},{7,6},{8,9},{9,8},{10,11... | collective-permute-start | bytes 1572872 | tf_op jit(solution)/shard_map/ppermute | solution.py:65
  261.5 48.9 %collective-permute-start.41 = (bf16[256,1024]{1,0:T(8,128)(2,1)S(1)}, bf16[256,1024]{1,0:T(8,128)(2,1)S(1)}, u32[]{:S(2)}, u32[]{:S(2)}) collective-permute-start(bf16[256,1024]{1,0:T(8,128)(2,1)S(1)} %add_convert_fusion.2), channel_id=1, source_target_pairs={{0,2},{1,3},{2,0},{3,1},{4,6},{5,7},{6,4},{7,5},{8,10},{9,11},{10,... | collective-permute-start | bytes 1572872 | tf_op jit(solution)/shard_map/ppermute | solution.py:65
  261.9 9.2 %copy-start.34 = (bf16[256,512]{1,0:T(8,128)(2,1)}, bf16[256,512]{1,0:T(8,128)(2,1)S(1)}, u32[]{:S(2)}) copy-start(bf16[256,512]{1,0:T(8,128)(2,1)S(1)} %collective-permute-done.30.refs_10_) | copy-start | bytes 786436
  302.1 8.2 %copy-start.17 = (bf16[256,1024]{1,0:T(8,128)(2,1)S(1)}, bf16[256,1024]{1,0:T(8,128)(2,1)}, u32[]{:S(2)}) copy-start(bf16[256,1024]{1,0:T(8,128)(2,1)} %get-tuple-element.63) | copy-start | bytes 1572868
  313.3 169.3 %reduce-scatter.5.cloned.1.call-start = ((), (), s32[]{:S(2)}) async-start(), calls=%async_computation.4 | async-start | bytes 4866048 | tf_op jit(solution)/shard_map/reduce_scatter | solution.py:580
  337.9 24.0 %collective-permute-start.25 = (bf16[512,1024]{1,0:T(8,128)(2,1)S(1)}, bf16[512,1024]{1,0:T(8,128)(2,1)S(1)}, u32[]{:S(2)}, u32[]{:S(2)}) collective-permute-start(bf16[512,1024]{1,0:T(8,128)(2,1)S(1)} %slice_bitcast_fusion), channel_id=1, source_target_pairs={{0,1},{1,0},{2,3},{3,2},{4,5},{5,4},{6,7},{7,6},{8,9},{9,8},{10,11... | collective-permute-start | bytes 3145736 | tf_op jit(solution)/shard_map/ppermute | solution.py:65
  361.4 3.0 collective-permute-start.34
  361.5 6.7 %collective-permute-start.20 = (bf16[512,1024]{1,0:T(8,128)(2,1)}, bf16[512,1024]{1,0:T(8,128)(2,1)}, u32[]{:S(2)}, u32[]{:S(2)}) collective-permute-start(bf16[512,1024]{1,0:T(8,128)(2,1)} %slice_bitcast_fusion.2), channel_id=1, source_target_pairs={{0,1},{1,0},{2,3},{3,2},{4,5},{5,4},{6,7},{7,6},{8,9},{9,8},{10,11... | collective-permute-start | bytes 3145736 | tf_op jit(solution)/shard_map/ppermute | solution.py:65
  363.3 26.3 %copy-start = (f32[512,1024]{1,0:T(8,128)S(1)}, f32[512,1024]{1,0:T(8,128)}, u32[]{:S(2)}) copy-start(f32[512,1024]{1,0:T(8,128)} %get-tuple-element.45.refs_1_) | copy-start | bytes 6291460
  363.3 26.3 %collective-permute-start.26 = (bf16[512,1024]{1,0:T(8,128)(2,1)}, bf16[512,1024]{1,0:T(8,128)(2,1)}, u32[]{:S(2)}, u32[]{:S(2)}) collective-permute-start(bf16[512,1024]{1,0:T(8,128)(2,1)} %fusion.4), channel_id=1, source_target_pairs={{0,2},{1,3},{2,0},{3,1},{4,6},{5,7},{6,4},{7,5},{8,10},{9,11},{10,... | collective-permute-start | bytes 3145736 | tf_op jit(solution)/shard_map/ppermute | solution.py:65
  363.7 102.6 %collective-permute-start.33 = (bf16[512,1024]{1,0:T(8,128)(2,1)}, bf16[512,1024]{1,0:T(8,128)(2,1)S(1)}, u32[]{:S(2)}, u32[]{:S(2)}) collective-permute-start(bf16[512,1024]{1,0:T(8,128)(2,1)} %get-tuple-element.73), channel_id=1, source_target_pairs={{0,1},{1,0},{2,3},{3,2},{4,5},{5,4},{6,7},{7,6},{8,9},{9,8},{10,11... | collective-permute-start | bytes 3145736 | tf_op jit(solution)/shard_map/ppermute | solution.py:65
  367.3 25.9 %copy-start.16 = (bf16[4,512,256]{2,1,0:T(8,128)(2,1)S(1)}, bf16[4,512,256]{2,1,0:T(8,128)(2,1)}, u32[]{:S(2)}) copy-start(bf16[4,512,256]{2,1,0:T(8,128)(2,1)} %get-tuple-element.61) | copy-start | bytes 3145732
  367.3 99.0 %collective-permute-start.35 = (bf16[512,1024]{1,0:T(8,128)(2,1)}, bf16[512,1024]{1,0:T(8,128)(2,1)}, u32[]{:S(2)}, u32[]{:S(2)}) collective-permute-start(bf16[512,1024]{1,0:T(8,128)(2,1)} %fusion), channel_id=1, source_target_pairs={{0,2},{1,3},{2,0},{3,1},{4,6},{5,7},{6,4},{7,5},{8,10},{9,11},{10,... | collective-permute-start | bytes 3145736 | tf_op jit(solution)/shard_map/ppermute | solution.py:65
  393.3 71.2 %collective-permute-start.36 = (bf16[512,256]{1,0:T(8,128)(2,1)S(1)}, bf16[512,256]{1,0:T(8,128)(2,1)S(1)}, u32[]{:S(2)}, u32[]{:S(2)}) collective-permute-start(bf16[512,256]{1,0:T(8,128)(2,1)S(1)} %get-tuple-element.82), channel_id=1, source_target_pairs={{0,1},{1,0},{2,3},{3,2},{4,5},{5,4},{6,7},{7,6},{8,9},{9,8},{10,11... | collective-permute-start | bytes 786440 | tf_op jit(solution)/shard_map/ppermute | solution.py:65
  393.4 71.1 %collective-permute-start.37 = (bf16[512,256]{1,0:T(8,128)(2,1)S(1)}, bf16[512,256]{1,0:T(8,128)(2,1)S(1)}, u32[]{:S(2)}, u32[]{:S(2)}) collective-permute-start(bf16[512,256]{1,0:T(8,128)(2,1)S(1)} %get-tuple-element.81), channel_id=1, source_target_pairs={{0,2},{1,3},{2,0},{3,1},{4,6},{5,7},{6,4},{7,5},{8,10},{9,11},{10,... | collective-permute-start | bytes 786440 | tf_op jit(solution)/shard_map/ppermute | solution.py:65
  393.9 70.6 %collective-permute-start.38 = (bf16[512,256]{1,0:T(8,128)(2,1)S(1)}, bf16[512,256]{1,0:T(8,128)(2,1)S(1)}, u32[]{:S(2)}, u32[]{:S(2)}) collective-permute-start(bf16[512,256]{1,0:T(8,128)(2,1)S(1)} %get-tuple-element.80), channel_id=1, source_target_pairs={{0,3},{1,2},{2,1},{3,0},{4,7},{5,6},{6,5},{7,4},{8,11},{9,10},{10,... | collective-permute-start | bytes 786440 | tf_op jit(solution)/shard_map/ppermute | solution.py:65
  (18 other events, 52.0 us)
Sparse Core Ops, SparseCore 0:
  19.3 83.8 all-gather.1
  313.4 76.3 reduce-scatter.2
  393.5 89.0 reduce-scatter.4

commit v2 on v1

v2 whole, which is shorter than its diff:
```python
import functools
import math

import jax
import jax.numpy as jnp
from jax import lax
from jax.experimental import pallas as pl
from jax.experimental.pallas import tpu as pltpu
from jax.sharding import PartitionSpec as P

HEAD_DIM = 64
HALF = HEAD_DIM // 2
SEQ = 2048
NDOC = 16
NORM_EPS = 1e-06
NEG = -1e30
F32 = jnp.float32
BF16 = jnp.bfloat16
VMEM_LIMIT = 58 << 20

VMEM = pl.BlockSpec(memory_space=pltpu.VMEM)
SMEM = pl.BlockSpec(memory_space=pltpu.SMEM)


def shape(dims, dtype):
    return jax.ShapeDtypeStruct(dims, dtype)


def dot(a, b):
    return jnp.dot(a, b, preferred_element_type=F32)


def dot_nt(a, b):
    return lax.dot_general(a, b, (((1,), (1,)), ((), ())), preferred_element_type=F32)


def dot_tn(a, b):
    return lax.dot_general(a, b, (((0,), (0,)), ((), ())), preferred_element_type=F32)


def padded(dims, dtype):
    size = jnp.dtype(dtype).itemsize
    *lead, rows, lanes = (1, 1, *dims)
    return math.prod(lead) * (-(-rows // 8) * 8) * (-(-lanes // 128) * 128) * size


def call(body, name, ins, outs, scratch=(), flops=0, after=()):
    held = [(a.shape, a.dtype) for a, s in ins if s is VMEM] + [(o.shape, o.dtype) for o in outs]
    held += [(v.shape, v.dtype) for v in scratch]
    need = sum(padded(*h) for h in held)
    skip = len(ins)

    def kernel(*refs):
        body(*refs[:skip], *refs[skip + len(after) :])

    return pl.pallas_call(
        kernel,
        name=name,
        out_shape=outs,
        in_specs=[s for _, s in ins] + [pl.BlockSpec(memory_space=pl.ANY)] * len(after),
        out_specs=[VMEM] * len(outs),
        scratch_shapes=list(scratch),
        compiler_params=pltpu.CompilerParams(vmem_limit_bytes=VMEM_LIMIT),
        cost_estimate=pl.CostEstimate(flops=flops, bytes_accessed=need, transcendentals=0),
    )(*[a for a, _ in ins], *after)


def grid_call(body, name, steps, scalars, ins, outs, scratch=(), flops=0, after=()):
    moved = sum(padded(a.shape, a.dtype) for a, _, _ in ins)
    moved += sum(padded(o.shape, o.dtype) for o, _, _ in outs)
    skip = len(scalars) + len(ins)

    def kernel(*refs):
        body(*refs[:skip], *refs[skip + len(after) :])

    return pl.pallas_call(
        kernel,
        name=name,
        grid_spec=pltpu.PrefetchScalarGridSpec(
            num_scalar_prefetch=len(scalars),
            grid=(steps,),
            in_specs=[pl.BlockSpec(b, f) for _, b, f in ins]
            + [pl.BlockSpec(memory_space=pl.ANY)] * len(after),
            out_specs=[pl.BlockSpec(b, f) for _, b, f in outs],
            scratch_shapes=list(scratch),
        ),
        out_shape=[o for o, _, _ in outs],
        compiler_params=pltpu.CompilerParams(vmem_limit_bytes=VMEM_LIMIT),
        cost_estimate=pl.CostEstimate(flops=flops, bytes_accessed=moved, transcendentals=0),
    )(*scalars, *[a for a, _, _ in ins], *after)


def whole(*arrays):
    return [(a, a.shape, lambda i, *s, d=len(a.shape): (0,) * d) for a in arrays]


def by_rows(tile, *arrays):
    return [(a, (tile, a.shape[1]), lambda i, *s: (i, 0)) for a in arrays]


def by_chunk(tile, *arrays):
    per = arrays[0].shape[0] // tile
    return [
        (a, (tile, a.shape[1]), lambda i, *s, j=j: (jnp.clip(i - j * per, 0, per - 1), 0))
        for j, a in enumerate(arrays)
    ]


def token_tile(per):
    return lambda i, me: (i // per ^ me[0]) * per + i % per


def gate(value, after):
    if not after:
        return value
    return pl.pallas_call(
        lambda *refs: None,
        name="gate",
        out_shape=shape(value.shape, value.dtype),
        in_specs=[pl.BlockSpec(memory_space=pl.ANY)] * (1 + len(after)),
        out_specs=pl.BlockSpec(memory_space=pl.ANY),
        input_output_aliases={0: 0},
    )(value, *after)


def in_vmem(*arrays):
    return [(a, VMEM) for a in arrays]


def row_scale(stream):
    return lax.rsqrt(jnp.mean(stream * stream, axis=-1, keepdims=True) + NORM_EPS)


def swap(value, axis, size, bit):
    return lax.ppermute(value, axis, [(i, i ^ bit) for i in range(size)])


def bits_down(size):
    return [1 << b for b in reversed(range(size.bit_length() - 1))]


def gather_relative(value, axis, size, hold=None):
    parts = {0: value}
    for bit in bits_down(size):
        moved = {0: swap(value, axis, size, bit)}
        if bit == 1 and hold:
            after = hold(parts[0], moved[0])
            parts.update({j: gate(v, after) for j, v in parts.items() if j})
        moved.update({j: swap(v, axis, size, bit) for j, v in parts.items() if j})
        parts.update({j | bit: v for j, v in moved.items()})
    return [parts[j] for j in range(size)]


def fold_kernel(*refs):
    *terms, out = refs
    out[...] = sum(t[...].astype(F32) for t in terms).astype(BF16)


def sum_relative(parts, axis, size, after=()):
    parts = dict(enumerate([[p] for p in parts]))
    bit, sent = 1, []
    while bit < size:
        kept = {}
        for j in sorted((j for j in parts if not j & bit), reverse=True):
            away = parts[j | bit]
            if len(away) > 1:
                out = [shape(away[0].shape, BF16)]
                away = call(fold_kernel, "fold", in_vmem(*away), out, after=after)
                sent += away
            kept[j] = parts[j] + [swap(away[0], axis, size, bit)]
        parts = kept
        bit *= 2
    return parts[0], sent


def exchange_relative(parts, axis, size):
    return [p if j == 0 else swap(p, axis, size, j) for j, p in enumerate(parts)]


def sum_everywhere(value, sizes):
    for axis, size in sizes:
        for bit in reversed(bits_down(size)):
            value = value + swap(value, axis, size, bit)
    return value


def column_orders(size):
    bits = bits_down(size)
    return [bits, bits[-1:] + bits[:-1]]


def ring_sources(dp, size):
    line = size // 2
    place = dp // 2 ^ dp // 4
    held = [jnp.remainder(place - k, line) for k in range(line)]
    held = [2 * (p ^ p // 2) for p in held]
    return jnp.stack([h + (dp & 1) for h in held] + [h + 1 - (dp & 1) for h in held])


def gather_columns(rows, size):
    line = size // 2
    ring = [p ^ p // 2 for p in range(line)]
    pairs = [(2 * ring[p] + i, 2 * ring[(p + 1) % line] + i) for p in range(line) for i in range(2)]
    held = [rows]
    for _ in range(line - 1):
        held.append(lax.ppermute(held[-1], "dp", pairs))
    return held + [swap(h, "dp", size, 1) for h in held]


def column_places(size, bits):
    places = [0]
    for bit in reversed(bits):
        places = places + [j | bit for j in places]
    return places


def scatter_columns(kept, sent, size, bits, after):
    for bit in bits:
        total = kept.astype(F32) + swap(sent, "dp", size, bit).astype(F32)
        if bit == bits[-1]:
            return total[0]
        half = total.shape[0] // 2
        kept, sent = total[:half], total[half:].astype(BF16)
        if bit == bits[0]:
            sent = gate(sent, after)


def pick(step, per, refs, out_ref):
    for j, ref in enumerate(refs):

        @pl.when(step // per == j)
        def _(ref=ref):
            out_ref[...] = ref[...]


def join_columns(from_ref, parts, outs):
    for i, part in enumerate(parts):
        lanes = part.shape[1]
        at = slice(None)
        if len(parts) > 1:
            at = pl.ds(pl.multiple_of(from_ref[i] * lanes, 128), lanes)
        for row, rows, out in outs:
            out[:, at] = part[row : row + rows, :]


def project_kernel(n, per, count, me_ref, from_ref, *refs):
    xs, fvs = refs[:n], refs[n : 2 * n]
    parts = refs[2 * n : 2 * n + count]
    gain_ref, cos_ref, sin_ref, q_out, k_out, kt_out, v_out, vt_out, w_ref, wo_ref, x_ref, fv_ref = (
        refs[2 * n + count :]
    )
    width = q_out.shape[0]
    step = pl.program_id(0)

    @pl.when(step == 0)
    def _():
        join_columns(from_ref, parts, [(0, 3 * width, w_ref), (3 * width, width, wo_ref)])

    pick(step, per, xs, x_ref)
    pick(step, per, fvs, fv_ref)
    stream = x_ref[...].astype(F32)
    normed = (stream * row_scale(stream) * gain_ref[...]).astype(BF16)
    qk = dot_nt(w_ref[: 2 * width, :], normed)
    cos, sin = cos_ref[...], sin_ref[...]
    turned = []
    for row in range(0, 2 * width, HEAD_DIM):
        first, second = qk[row : row + HALF], qk[row + HALF : row + HEAD_DIM]
        turned += [first * cos - second * sin, second * cos + first * sin]
    turned = jnp.concatenate(turned, axis=0)
    q_out[...] = (turned[:width] * HEAD_DIM ** (-0.5)).astype(BF16)
    keys = turned[width:]
    kt_out[...] = keys.astype(BF16)
    k_out[...] = keys.T.astype(BF16)
    values = 0.5 * dot_nt(normed, w_ref[2 * width :, :]) + 0.5 * fv_ref[...].astype(F32)
    v_out[...] = values.astype(BF16)
    vt_out[...] = values.T.astype(BF16)


def doc_of(len_ref, token):
    run, first, last = jnp.int32(0), jnp.int32(0), jnp.int32(SEQ)
    for doc in range(NDOC):
        end = run + len_ref[0, doc]
        inside = (token >= run) & (token < end)
        first, last = jnp.where(inside, run, first), jnp.where(inside, end, last)
        run = end
    return first, last


def attend_kernel(bq, per, heads, skip, len_ref, me_ref, q_ref, k_ref, vt_ref, start_ref, *refs):
    *ctx_refs, ot_ref, lse_ref, s_ref = refs[skip:]
    bk = bq
    block = pl.program_id(0)
    first, _ = doc_of(len_ref, block * bq)
    starts = start_ref[...]

    def score(kb, tops, diagonal):
        at = pl.ds(pl.multiple_of(kb * bk, bk), bk)
        key_index = lax.broadcasted_iota(jnp.int32, (bk, bq), 0) + kb * bk
        allowed = key_index >= starts
        if diagonal:
            allowed &= key_index <= lax.broadcasted_iota(jnp.int32, (bk, bq), 1) + block * bq
        out = []
        for h in range(heads):
            rows = slice(h * HEAD_DIM, (h + 1) * HEAD_DIM)
            scores = jnp.where(allowed, dot(k_ref[at, rows], q_ref[rows, :]), NEG)
            s_ref[h, at, :] = scores
            out.append(jnp.maximum(tops[h], jnp.max(scores.reshape(bk // 8, 8, bq), axis=0)))
        return tuple(out)

    tops = score(block, tuple(jnp.full((8, bq), NEG, F32) for _ in range(heads)), True)
    tops = lax.fori_loop(first // bk, block, lambda kb, c: score(kb, c, False), tops)
    tops = [jnp.max(t, axis=0, keepdims=True) for t in tops]

    def gather(kb, carry):
        at = pl.ds(pl.multiple_of(kb * bk, bk), bk)
        out = []
        for h in range(heads):
            rows = slice(h * HEAD_DIM, (h + 1) * HEAD_DIM)
            total, acc = carry[h]
            probs = jnp.exp(s_ref[h, at, :] - tops[h])
            total = total + jnp.sum(probs.reshape(bk // 8, 8, bq), axis=0)
            out.append((total, acc + dot(vt_ref[rows, at], probs.astype(BF16))))
        return tuple(out)

    zero = tuple((jnp.zeros((8, bq), F32), jnp.zeros((HEAD_DIM, bq), F32)) for _ in range(heads))
    sums = lax.fori_loop(first // bk, block + 1, gather, zero)
    outs = []
    for h in range(heads):
        total = jnp.sum(sums[h][0], axis=0, keepdims=True)
        outs.append(sums[h][1] * (1.0 / total))
        lse_ref[h : h + 1, :] = tops[h] + jnp.log(total)
    out = jnp.concatenate(outs, axis=0)
    ot_ref[...] = out.astype(BF16)
    out = out.T.astype(BF16)
    for j, ref in enumerate(ctx_refs):

        @pl.when((block // per) ^ me_ref[0] == j)
        def _(ref=ref):
            ref[pl.ds(pl.multiple_of((block % per) * bq, bq), bq), :] = out


def attend(lengths, me, q_t, keys, v_t, starts, shard, after):
    width = q_t.shape[0]
    heads = width // HEAD_DIM
    bq = min(512, shard)
    per = shard // bq
    n = SEQ // shard
    spec = pltpu.PrefetchScalarGridSpec(
        num_scalar_prefetch=2,
        grid=(SEQ // bq,),
        in_specs=[
            pl.BlockSpec((width, bq), lambda i, l, h: (0, i)),
            pl.BlockSpec((SEQ, width), lambda i, l, h: (0, 0)),
            pl.BlockSpec((width, SEQ), lambda i, l, h: (0, 0)),
            pl.BlockSpec((1, bq), lambda i, l, h: (0, i)),
        ]
        + [pl.BlockSpec(memory_space=pl.ANY)] * len(after),
        out_specs=[
            *[pl.BlockSpec((shard, width), lambda i, l, h: (0, 0))] * n,
            pl.BlockSpec((width, bq), lambda i, l, h: (0, i)),
            pl.BlockSpec((heads, bq), lambda i, l, h: (0, i)),
        ],
        scratch_shapes=[pltpu.VMEM((heads, SEQ, bq), F32)],
    )
    return pl.pallas_call(
        functools.partial(attend_kernel, bq, per, heads, len(after)),
        name="attend",
        grid_spec=spec,
        out_shape=[
            *[shape((shard, width), BF16)] * n,
            shape((width, SEQ), BF16),
            shape((heads, SEQ), F32),
        ],
        compiler_params=pltpu.CompilerParams(vmem_limit_bytes=VMEM_LIMIT),
        cost_estimate=pl.CostEstimate(
            flops=16 * SEQ * SEQ * width, bytes_accessed=8 * SEQ * width, transcendentals=0
        ),
    )(lengths, me, q_t, keys, v_t, starts, *after)


def attend_back_kernel(n, block, len_ref, me_ref, *refs):
    q_ref, k_ref, kt_ref, v_ref, ot_ref, lse_ref, start_ref, cos_ref, sin_ref = refs[:9]
    dos = refs[9 : 9 + n]
    out_ref, *first_refs = refs[9 + n : 10 + 2 * n]
    dq_ref, dk_ref, dv_ref, do_ref, delta_ref = refs[10 + 2 * n :]
    width = q_ref.shape[0]
    heads = width // HEAD_DIM
    shard = SEQ // n
    for j in range(n):
        at = pl.ds(pl.multiple_of((me_ref[0] ^ j) * shard, shard), shard)
        do_ref[:, at] = dos[j][...]
        product = dos[j][...].astype(F32) * ot_ref[:, at].astype(F32)
        for h in range(heads):
            delta_ref[h : h + 1, at] = jnp.sum(
                product[h * HEAD_DIM : (h + 1) * HEAD_DIM], axis=0, keepdims=True
            )
    dq_ref[...] = jnp.zeros_like(dq_ref)
    dk_ref[...] = jnp.zeros_like(dk_ref)
    dv_ref[...] = jnp.zeros_like(dv_ref)

    def pair(kb, qb, diagonal):
        k_at = pl.ds(pl.multiple_of(kb * block, block), block)
        q_at = pl.ds(pl.multiple_of(qb * block, block), block)
        key_index = lax.broadcasted_iota(jnp.int32, (block, block), 0) + kb * block
        allowed = key_index >= start_ref[:, q_at]
        if diagonal:
            allowed &= key_index <= lax.broadcasted_iota(jnp.int32, (block, block), 1) + qb * block
        every = range(heads)
        rows = [slice(h * HEAD_DIM, (h + 1) * HEAD_DIM) for h in every]
        q_t = [q_ref[r, q_at] for r in rows]
        do_t = [do_ref[r, q_at] for r in rows]
        scores = [dot(k_ref[k_at, r], q_t[h]) for h, r in enumerate(rows)]
        dprobs = [dot(v_ref[k_at, r], do_t[h]) for h, r in enumerate(rows)]
        probs = [
            jnp.exp(jnp.where(allowed, scores[h], NEG) - lse_ref[h : h + 1, q_at]) for h in every
        ]
        dscores = [
            (probs[h] * (dprobs[h] - delta_ref[h : h + 1, q_at])).astype(BF16) for h in every
        ]
        probs = [p.astype(BF16) for p in probs]
        dv = [dot_nt(do_t[h], probs[h]) for h in every]
        dk = [dot_nt(q_t[h], dscores[h]) for h in every]
        dq = [dot(kt_ref[rows[h], k_at], dscores[h]) for h in every]
        for h in every:
            dv_ref[rows[h], k_at] += dv[h]
            dk_ref[rows[h], k_at] += dk[h]
            dq_ref[rows[h], q_at] += dq[h]

    def outer(kb, carry):
        _, end = doc_of(len_ref, kb * block + block - 1)
        pair(kb, kb, True)

        def inner(qb, c):
            pair(kb, qb, False)
            return c

        lax.fori_loop(kb + 1, (end - 1) // block + 1, inner, 0)
        return carry

    lax.fori_loop(0, SEQ // block, outer, 0)
    cos, sin = cos_ref[...], sin_ref[...]
    for base, ref, scale in ((0, dq_ref, HEAD_DIM ** (-0.5)), (width, dk_ref, 1.0)):
        for row in range(0, width, HEAD_DIM):
            first = ref[row : row + HALF, :] * scale
            second = ref[row + HALF : row + HEAD_DIM, :] * scale
            out_ref[base + row : base + row + HALF, :] = (first * cos + second * sin).astype(BF16)
            out_ref[base + row + HALF : base + row + HEAD_DIM, :] = (
                second * cos - first * sin
            ).astype(BF16)
    for j in range(n):
        at = pl.ds(pl.multiple_of((me_ref[0] ^ j) * shard, shard), shard)
        grad = 0.5 * dv_ref[:, at]
        out_ref[2 * width :, at] = grad.astype(BF16)
        first_refs[j][...] = grad.T.astype(BF16)


def add_rows(out_ref, rows):
    total = jnp.sum(rows, axis=0, keepdims=True)

    @pl.when(pl.program_id(0) == 0)
    def _():
        out_ref[...] = total

    @pl.when(pl.program_id(0) > 0)
    def _():
        out_ref[...] += total


def join_kernel(n, *refs):
    ctx, w_out = refs[:n], refs[n : 2 * n]
    x_ref, gain_ref, mid_ref, normed_ref = refs[2 * n :]
    total = x_ref[...].astype(F32)
    for c, w in zip(ctx, w_out):
        total = total + dot(c[...], w[...])
    mid_ref[...] = total
    normed_ref[...] = (total * row_scale(total) * gain_ref[...]).astype(BF16)


def mlp_kernel(n, per, count, from_ref, *refs):
    normed, grads = refs[:n], refs[n : 2 * n]
    parts = refs[2 * n : 2 * n + count]
    outs, (tokens_ref, og_ref) = refs[2 * n + count : -2], refs[-2:]
    mixed_ref, dgate_ref, dup_ref, *gn_refs = outs
    w_ref = parts[0]
    step = pl.program_id(0)
    if count > 1:
        *gn_refs, w_ref = gn_refs

        @pl.when(step == 0)
        def _():
            join_columns(from_ref, parts, [(0, w_ref.shape[0], w_ref)])

    pick(step, per, normed, tokens_ref)
    pick(step, per, grads, og_ref)
    hidden = mixed_ref.shape[1]
    w_gate, w_up, w_down = (w_ref.at[i * hidden : (i + 1) * hidden, :] for i in range(3))
    gate = dot_nt(tokens_ref[...], w_gate[...])
    up = dot_nt(tokens_ref[...], w_up[...])
    gm = dot_nt(og_ref[...], w_down[...])
    sig = 1.0 / (1.0 + jnp.exp(-gate))
    act = gate * sig
    mixed_ref[...] = (act * up).astype(BF16)
    dup = (gm * act).astype(BF16)
    dgate = (gm * up * sig * (1.0 + gate * (1.0 - sig))).astype(BF16)
    dup_ref[...] = dup
    dgate_ref[...] = dgate
    back = (dot(dgate, w_gate[...]) + dot(dup, w_up[...])).astype(BF16)
    for j, ref in enumerate(gn_refs):

        @pl.when(step // per == j)
        def _(ref=ref):
            ref[...] = back


def mlp_rest_kernel(n, tile, *refs):
    normed, grads = refs[:n], refs[n : 2 * n]
    dgates, dups, mixeds = refs[2 * n : 2 * n + 2], refs[2 * n + 2 : 2 * n + 4], refs[2 * n + 4 : 2 * n + 6]
    w_ref, *outs, grad_ref, acc_ref = refs[2 * n + 6 :]
    half = n // 2
    shard = normed[0].shape[0]
    hidden = acc_ref.shape[0]
    lanes = grad_ref.shape[2]
    w_down = w_ref.at[2 * hidden :, :]
    for j in range(n):

        def step(t, carry, j=j):
            rows = pl.ds(pl.multiple_of(t * tile, tile), tile)
            part = mixeds[j // half][pl.ds(j % half * shard + t * tile, tile), :]
            outs[j][rows, :] = dot(part, w_down[...]).astype(BF16)
            return carry

        lax.fori_loop(0, outs[j].shape[0] // tile, step, 0)
    for which, (lefts, rights) in enumerate(((dgates, normed), (dups, normed), (mixeds, grads))):
        for j in range(n):
            left = lefts[j // half][j % half * shard : (j % half + 1) * shard, :]
            part = dot_tn(left, rights[j][...])
            if j == 0:
                acc_ref[...] = part
            else:
                acc_ref[...] += part
        for i in range(grad_ref.shape[0]):
            grad_ref[i, which * hidden : (which + 1) * hidden, :] = acc_ref[
                :, i * lanes : (i + 1) * lanes
            ].astype(BF16)


def middle_back_kernel(n, count, *refs):
    mid_ref, og_ref, gain_ref = refs[:3]
    w_out = refs[3 : 3 + n]
    terms = refs[3 + n : 3 + n + count]
    gmid_ref, ga_ref, gain_out, *gctx = refs[3 + n + count :]
    mid = mid_ref[...]
    grad = sum(t[...].astype(F32) for t in terms)
    scale = row_scale(mid)
    normed = mid * scale
    scaled = grad * gain_ref[...]
    back = scale * (scaled - normed * jnp.mean(scaled * normed, axis=-1, keepdims=True))
    add_rows(gain_out, grad * normed)
    gmid = og_ref[...].astype(F32) + back
    gmid_ref[...] = gmid
    ga = gmid.astype(BF16)
    ga_ref[...] = ga
    for w, out in zip(w_out, gctx):
        out[...] = dot_nt(w[...], ga).astype(BF16)


def out_weight_kernel(n, *refs):
    ctx, ga_ref, outs = refs[:n], refs[n], refs[n + 1 :]
    for c, out in zip(ctx, outs):
        out[...] = dot_tn(c[...], ga_ref[...]).astype(BF16)


def unproject_kernel(n, per, me_ref, *refs):
    xs = refs[:n]
    gp_ref, w_ref = refs[n : n + 2]
    *gns, gain_out, x_ref = refs[n + 2 :]
    step = pl.program_id(0)
    pick(step, per, xs, x_ref)
    grad = dot_tn(gp_ref[...], w_ref[...])
    for j, ref in enumerate(gns):

        @pl.when(step // per == j)
        def _(ref=ref):
            ref[...] = grad.astype(BF16)

    stream = x_ref[...].astype(F32)
    add_rows(gain_out, grad * (stream * row_scale(stream)))


def qkv_weight_kernel(n, count, orders, me_ref, dp_ref, *refs):
    xs = refs[:n]
    gp_ref, gain_ref = refs[n : n + 2]
    terms = refs[n + 2 : n + 2 + count]
    *outs, acc_ref = refs[n + 2 + count :]
    shard = xs[0].shape[0]
    lanes = outs[0].shape[2]
    wide = gp_ref.shape[0]
    for j in range(n):
        at = pl.ds(pl.multiple_of((me_ref[0] ^ j) * shard, shard), shard)
        stream = xs[j][...].astype(F32)
        normed = (stream * row_scale(stream) * gain_ref[...]).astype(BF16)
        part = dot(gp_ref[:, at], normed)
        if j == 0:
            acc_ref[:wide, :] = part
        else:
            acc_ref[:wide, :] += part
    acc_ref[wide:, :] = sum(t[...].astype(F32) for t in terms)
    if orders is None:
        for i in range(outs[0].shape[0]):
            outs[0][i] = acc_ref[:, i * lanes : (i + 1) * lanes].astype(BF16)
        return
    rows = acc_ref.shape[0] // 2
    for half, places in enumerate(orders):
        for i, j in enumerate(places):
            at = pl.ds(pl.multiple_of((dp_ref[0] ^ j) * lanes, 128), lanes)
            out = outs[2 * half + i // (len(places) // 2)]
            out[i % (len(places) // 2)] = acc_ref[half * rows : (half + 1) * rows, at].astype(BF16)


def input_back_kernel(n, count, me_ref, x_ref, gain_ref, gmid_ref, *refs):
    terms, dvs = refs[:count], refs[count : count + (n if len(refs) > count + 1 else 0)]
    out_ref, *first_ref = refs[count + len(dvs) :]
    stream = x_ref[...].astype(F32)
    scale = row_scale(stream)
    normed = stream * scale
    scaled = sum(t[...].astype(F32) for t in terms) * gain_ref[...]
    back = scale * (scaled - normed * jnp.mean(scaled * normed, axis=-1, keepdims=True))
    out_ref[...] = gmid_ref[...] + back
    for j, dv in enumerate(dvs):
        width = dv.shape[1]
        at = pl.ds(pl.multiple_of((me_ref[0] ^ j) * width, 128), width)
        first_ref[0][:, at] = dv[...].astype(F32)


def doc_tables(lengths):
    index = jnp.arange(SEQ, dtype=jnp.int32)
    ends = jnp.cumsum(lengths)
    begins = ends - lengths
    starts = jnp.max(jnp.where(begins[:, None] <= index[None, :], begins[:, None], 0), axis=0)
    inverse = jnp.exp(jnp.arange(HALF, dtype=F32) * (-2.0 * math.log(10000.0) / HEAD_DIM))
    angles = (index - starts).astype(F32)[None, :] * inverse[:, None]
    return starts[None, :], jnp.cos(angles), jnp.sin(angles)


def local(
    n,
    n_dp,
    hidden_in,
    first_values,
    doc_lengths,
    out_grad,
    qkv_weight,
    out_weight,
    gate_up_weight,
    down_weight,
    attn_gain,
    mlp_gain,
):
    shard, width = hidden_in.shape[1], qkv_weight.shape[2]
    hidden = down_weight.shape[0]
    lanes = qkv_weight.shape[0]
    dim = hidden_in.shape[2]
    tile = min(256, shard)
    me = lax.axis_index("head").reshape(1).astype(jnp.int32)
    dp = lax.axis_index("dp").reshape(1).astype(jnp.int32)
    x_own, og_own = hidden_in[0], out_grad[0]
    gain_one, gain_two = attn_gain[None, :], mlp_gain[None, :]

    rows = jnp.concatenate(
        [qkv_weight.transpose(1, 2, 0).reshape(3 * width, lanes), out_weight], axis=0
    )
    mlp_rows = jnp.concatenate(
        [gate_up_weight.transpose(1, 2, 0).reshape(2 * hidden, lanes), down_weight], axis=0
    )
    sources = ring_sources(dp[0], n_dp)
    ringed = lanes % 128 == 0
    if ringed:
        parts = gather_columns(rows, n_dp)
        xs = gather_relative(x_own, "head", n, lambda *x: [parts[n_dp // 2 - 1]])
        mlp_columns = gather_columns(gate(mlp_rows, [xs[n // 2], parts[n_dp // 2 - 1]]), n_dp)
        line = n_dp // 2
        early, middle_ones, late = mlp_columns[1:2], mlp_columns[2:3] + mlp_columns[line:line + 1], mlp_columns[3:]
    else:
        xs = gather_relative(x_own, "head", n)
        parts = [lax.all_gather(rows, "dp", axis=1, tiled=True)]
        mlp_columns = [lax.all_gather(mlp_rows, "dp", axis=1, tiled=True)]
        early, middle_ones, late = [], [], []

    fv_parts = [
        lax.dynamic_slice(first_values[0], (0, (me[0] ^ j) * width), (shard, width))
        for j in range(n)
    ]
    fvs = exchange_relative(fv_parts, "head", n)
    starts, cos, sin = doc_tables(doc_lengths[0])

    per = shard // tile
    at = token_tile(per)
    columns = lambda i, me, *_: (0, at(i, me))
    rows_at = lambda i, me, *_: (at(i, me), 0)
    q_t, keys, k_t, values, v_t, w_qkv, w_out = grid_call(
        functools.partial(project_kernel, n, per, len(parts)),
        "project",
        n * per,
        [me, sources],
        by_chunk(tile, *xs)
        + by_chunk(tile, *fvs)
        + whole(*parts, gain_one)
        + [(t, (HALF, tile), columns) for t in (cos, sin)],
        [
            (shape((width, SEQ), BF16), (width, tile), columns),
            (shape((SEQ, width), BF16), (tile, width), rows_at),
            (shape((width, SEQ), BF16), (width, tile), columns),
            (shape((SEQ, width), BF16), (tile, width), rows_at),
            (shape((width, SEQ), BF16), (width, tile), columns),
        ]
        + whole(shape((3 * width, dim), BF16), shape((width, dim), BF16)),
        [pltpu.VMEM((tile, dim), BF16), pltpu.VMEM((tile, width), BF16)],
        flops=6 * SEQ * dim * width,
        after=early,
    )
    *ctx, o_t, lse = attend(doc_lengths, me, q_t, keys, v_t, starts, shard, middle_ones)

    ctxs = exchange_relative(ctx, "head", n)
    w_outs = gather_relative(w_out, "head", n, lambda *w: [o_t])
    ogs = gather_relative(og_own, "head", n, lambda *g: [o_t])
    middle, normed_two = grid_call(
        functools.partial(join_kernel, n),
        "join",
        per,
        [],
        by_rows(tile, *ctxs) + whole(*w_outs) + by_rows(tile, x_own) + whole(gain_two),
        by_rows(tile, shape((shard, dim), F32), shape((shard, dim), BF16)),
        flops=2 * shard * dim * dim,
        after=ogs[1:] + late,
    )

    half = n // 2
    groups = []

    def mlp(tokens, lo, weights, after=()):
        hiddens = [shape((half * shard, hidden), BF16)] * 3
        made = [shape((3 * hidden, dim), BF16)] if len(weights) > 1 else []
        out = grid_call(
            functools.partial(mlp_kernel, half, per, len(weights)),
            "mlp",
            half * per,
            [sources],
            by_chunk(tile, *tokens) + by_chunk(tile, *ogs[lo : lo + half]) + whole(*weights),
            by_rows(tile, *hiddens)
            + by_chunk(tile, *[shape((shard, dim), BF16)] * half)
            + whole(*made),
            [pltpu.VMEM((tile, dim), BF16)] * 2,
            flops=10 * half * shard * dim * hidden,
            after=after,
        )
        groups.append(out)
        return [out[3]]

    if n == 4:
        normed = gather_relative(
            normed_two, "head", n, lambda *tokens: mlp(tokens, 0, mlp_columns)
        )
    else:
        normed = gather_relative(normed_two, "head", n)
        mlp(normed[:half], 0, mlp_columns)
    w_mlp = groups[0][-1] if len(mlp_columns) > 1 else mlp_columns[0]
    mlp(normed[half:], half, [w_mlp])
    gn_two, gn_sent = sum_relative([p for g in groups for p in g[3 : 3 + half]], "head", n)

    *mlp_parts, mlp_grads = call(
        functools.partial(mlp_rest_kernel, n, tile),
        "mlp_rest",
        in_vmem(*normed, *ogs, *[g[k] for k in (1, 2, 0) for g in groups], w_mlp),
        [shape((shard, dim), BF16)] * n + [shape((n_dp, 3 * hidden, lanes), BF16)],
        [pltpu.VMEM((hidden, dim), F32)],
        flops=8 * SEQ * dim * hidden,
        after=gn_sent,
    )
    mlp_grads = gate(mlp_grads, gn_two[-1:])
    mlp_grads = lax.psum_scatter(mlp_grads, "dp", scatter_dimension=0, tiled=False).astype(F32)

    grad_middle, ga, gain_two_part, *gctx = grid_call(
        functools.partial(middle_back_kernel, n, len(gn_two)),
        "middle_back",
        per,
        [],
        by_rows(tile, middle, og_own)
        + whole(gain_two, *w_outs)
        + by_rows(tile, *gn_two),
        by_rows(tile, shape((shard, dim), F32), shape((shard, dim), BF16))
        + whole(shape((1, dim), F32))
        + [(shape((width, shard), BF16), (width, tile), lambda i: (0, i))] * n,
        flops=2 * shard * dim * dim,
        after=mlp_parts[:1],
    )
    dos = exchange_relative(gctx, "head", n)

    layer_terms, layer_sent = sum_relative(mlp_parts, "head", n, after=dos[2:])
    out_parts = call(
        functools.partial(out_weight_kernel, n),
        "out_weight",
        in_vmem(*ctxs, ga),
        [shape((width, dim), BF16)] * n,
        flops=2 * shard * dim * dim,
    )
    out_terms, out_sent = sum_relative(out_parts, "head", n)

    gp_t, *dv = call(
        functools.partial(attend_back_kernel, n, min(256, shard)),
        "attend_back",
        [(doc_lengths, SMEM), (me, SMEM)]
        + in_vmem(q_t, keys, k_t, values, o_t, lse, starts, cos, sin, *dos),
        [shape((3 * width, SEQ), BF16)] + [shape((shard, width), BF16)] * n,
        [pltpu.VMEM((width, SEQ), F32)] * 3
        + [pltpu.VMEM((width, SEQ), BF16), pltpu.VMEM((width // HEAD_DIM, SEQ), F32)],
        flops=20 * SEQ * SEQ * width,
        after=[*out_sent, *layer_sent],
    )
    dvs = exchange_relative(dv, "head", n)
    unprojected = grid_call(
        functools.partial(unproject_kernel, n, per),
        "unproject",
        n * per,
        [me],
        by_chunk(tile, *xs) + [(gp_t, (3 * width, tile), columns)] + whole(w_qkv),
        by_chunk(tile, *[shape((shard, dim), BF16)] * n) + whole(shape((1, dim), F32)),
        [pltpu.VMEM((tile, dim), BF16)],
        flops=6 * SEQ * dim * width,
        after=[layer_terms[-1], out_terms[-1]],
    )
    *gn_parts, gain_one_part = unprojected
    gn_one, gn_sent = sum_relative(gn_parts, "head", n, after=dvs[1:])
    layer_out = (middle + sum(t.astype(F32) for t in layer_terms)).astype(BF16)

    orders = None
    outs = [shape((n_dp, 4 * width, lanes), BF16)]
    if lanes % 128 == 0:
        bit_orders = [bits[::-1] for bits in column_orders(n_dp)]
        orders = [column_places(n_dp, bits) for bits in bit_orders]
        outs = [shape((n_dp // 2, 2 * width, lanes), BF16)] * 4
    grads = call(
        functools.partial(qkv_weight_kernel, n, len(out_terms), orders),
        "qkv_weight",
        [(me, SMEM), (dp, SMEM)] + in_vmem(*xs, gp_t, gain_one, *out_terms),
        outs,
        [pltpu.VMEM((4 * width, dim), F32)],
        flops=6 * SEQ * dim * width,
        after=gn_sent,
    )
    gains = jnp.concatenate([gain_one_part, gain_two_part], axis=0)
    gains = sum_everywhere(gate(gains, grads[:1]), [("head", n), ("dp", n_dp)])
    if orders is None:
        grads = lax.psum_scatter(grads[0], "dp", scatter_dimension=0, tiled=False).astype(F32)
    else:
        grads = jnp.concatenate(
            [
                scatter_columns(grads[2 * i], grads[2 * i + 1], n_dp, bits, gn_one[-1:])
                for i, bits in enumerate(bit_orders)
            ],
            axis=0,
        )
    small = min(128, shard)
    back_outs = by_rows(small, shape((shard, dim), F32))
    if width % 128 == 0:
        back_outs = back_outs * 2
    input_grad, *first_grad = grid_call(
        functools.partial(input_back_kernel, n, len(gn_one)),
        "input_back",
        shard // small,
        [me],
        by_rows(small, x_own)
        + whole(gain_one)
        + by_rows(small, grad_middle, *gn_one, *(dvs if width % 128 == 0 else [])),
        back_outs,
    )
    if not first_grad:
        stacked = jnp.stack(dvs)
        placed = [
            lax.dynamic_index_in_dim(stacked, me[0] ^ i, keepdims=False) for i in range(n)
        ]
        first_grad = [jnp.concatenate(placed, axis=1).astype(F32)]
    return (
        layer_out[None],
        input_grad[None],
        first_grad[0][None],
        grads[: 3 * width].reshape(3, width, lanes).transpose(2, 0, 1),
        grads[3 * width :],
        mlp_grads[: 2 * hidden].reshape(2, hidden, lanes).transpose(2, 0, 1),
        mlp_grads[2 * hidden :],
        gains[0],
        gains[1],
    )


def solution(mesh):
    tokens = P("dp", "head", None)
    columns = P("dp", None, "head")
    rows = P("head", "dp")
    return jax.shard_map(
        functools.partial(local, mesh.shape["head"], mesh.shape["dp"]),
        mesh=mesh,
        in_specs=(tokens, tokens, P("dp", None), tokens, columns, rows, columns, rows, P(), P()),
        out_specs=(tokens, tokens, tokens, columns, rows, columns, rows, P(), P()),
        check_vma=False,
    )
```

time: 501 us -> 407 us (0.81)
  blocking collectives: 68.6 us -> 0 us
  waiting for transfers between devices: 150 us -> 116 us
  starting transfers between devices: 27.7 us -> 50.5 us
  other arithmetic: 26.9 us -> 12.4 us
  Pallas kernels: 170 us -> 181 us
  local copies, waits for them, and re-layouts: 35.1 us -> 26.2 us
    psum x1 -> x0, blocking collectives: 68.6 us -> none  [local(): lax.psum(jnp.concatenate([gain_one_part, gain_two_part], axis=0), ('dp',...]
    ppermute x42 -> x55, waiting for transfers between devices: 145 us -> 101 us  [swap(): return lax.ppermute(value, axis, [(i, i ^ bit) for i in range(size)])]
    ppermute x0 -> x6, waiting for transfers between devices: none -> 15.8 us  [gather_columns(): held.append(lax.ppermute(held[-1], 'dp', pairs))]
    unnamed x74 -> x118, local copies, waits for them, and re-layouts: 4.05 us -> 17 us
    ppermute x42 -> x55, starting transfers between devices: 27.3 us -> 39.8 us  [swap(): return lax.ppermute(value, axis, [(i, i ^ bit) for i in range(size)])]
    squeeze x6 -> x0, local copies, waits for them, and re-layouts: 11.5 us -> none  [the longest x2 3.58 us: local(): mlp_parts += [out[j] for j in range(half)]]
    pallas_call x16 -> x25, Pallas kernels: 170 us -> 181 us  [the longest x7 82 us: grid_call(): pl.pallas_call(kernel, name=name, grid_spec=pltpu.PrefetchScalarGridSpec(...]
    slice x12 -> x5, local copies, waits for them, and re-layouts: 13.1 us -> 2.18 us  [the longest x4 1.51 us: scatter_columns(): kept, sent = (total[:half], total[half:].astype(BF16))]
  transfers between devices with their start and end apart: 45 -> 62, of which waited for: 18 -> 30; matrix products, arithmetic and copies ran while one was open for 10% -> 5% of each run, Pallas kernels for 32% -> 39%
where the time goes in v2:
time: 407 us; the launch traced here: 402 us
  Pallas kernels  181 us (44%)
  waiting for transfers between devices  116 us (29%)
  starting transfers between devices  50.5 us (12%)
  local copies, waits for them, and re-layouts  26.2 us (6%)
  between operations  14.9 us (4%)
  other arithmetic  12.4 us (3%)
    ppermute x55, waiting for transfers between devices, swap(): return lax.ppermute(value, axis, [(i, i ^ bit) for i in range(size)])  101 us
    pallas_call x7, Pallas kernels, grid_call(): pl.pallas_call(kernel, name=name, grid_spec=pltpu.PrefetchScalarGridSpec(...  82 us
    pallas_call x8, Pallas kernels, call(): pl.pallas_call(kernel, name=name, out_shape=outs, in_specs=[s for _, s in...  78.4 us
    ppermute x55, starting transfers between devices, swap(): return lax.ppermute(value, axis, [(i, i ^ bit) for i in range(size)])  39.8 us
    pallas_call x1, Pallas kernels, attend(): pl.pallas_call(functools.partial(attend_kernel, bq, per, heads, len(after...  20.7 us
    unnamed x118, local copies, waits for them, and re-layouts  17 us
    ppermute x6, waiting for transfers between devices, gather_columns(): held.append(lax.ppermute(held[-1], 'dp', pairs))  15.8 us
    ppermute x6, starting transfers between devices, gather_columns(): held.append(lax.ppermute(held[-1], 'dp', pairs))  10.6 us
  transfers between devices with their start and end apart: 62, of which 30 were waited for; matrix products, arithmetic and copies ran while one was open for 5% of the time, Pallas kernels for 39%

profile of v2, /device:TPU:0, one launch (start us, length us, event | category | flops | bytes accessed | tf_op | source)
XLA Modules:
  0.0 401.6 jit_solution(10658650722178239087)
XLA Ops:
  7.3 3.0 collective-permute-start.1
  12.3 1.6 collective-permute-start.2
  13.9 7.1 %collective-permute-done.2.refs_11_ = bf16[1024,128]{1,0:T(8,128)(2,1)S(1)} collective-permute-done((bf16[1024,128]{1,0:T(8,128)(2,1)S(1)}, bf16[1024,128]{1,0:T(8,128)(2,1)S(1)}, u32[]{:S(2)}, u32[]{:S(2)}) %collective-permute-start.2) | collective-permute-done | bytes 262176 | tf_op jit(solution)/shard_map/ppermute | solution.py:206
  21.8 1.5 collective-permute-start.9
  23.3 2.0 dynamic-slice_bitcast_fusion
  26.1 2.7 collective-permute-done.3.refs_12_
  30.4 6.0 %collective-permute-done.4.refs_1_.refs_2_.refs_13_ = bf16[1024,128]{1,0:T(8,128)(2,1)S(1)} collective-permute-done((bf16[1024,128]{1,0:T(8,128)(2,1)}, bf16[1024,128]{1,0:T(8,128)(2,1)S(1)}, u32[]{:S(2)}, u32[]{:S(2)}) %collective-permute-start.4) | collective-permute-done | bytes 262176 | tf_op jit(solution)/shard_map/ppermute | solution.py:206
  37.4 1.2 copy-done.6
  39.3 1.7 collective-permute-start.13
  41.1 1.6 collective-permute-start.10
  42.7 2.3 collective-permute-done.7.refs_8_
  45.1 1.5 collective-permute-start.11
  47.3 3.0 collective-permute-done.10.refs_15_
  50.3 1.5 collective-permute-start.12
  51.8 4.2 %collective-permute-done.11.refs_16_ = bf16[1024,128]{1,0:T(8,128)(2,1)} collective-permute-done((bf16[1024,128]{1,0:T(8,128)(2,1)}, bf16[1024,128]{1,0:T(8,128)(2,1)}, u32[]{:S(2)}, u32[]{:S(2)}) %collective-permute-start.11) | collective-permute-done | bytes 262176 | tf_op jit(solution)/shard_map/ppermute | solution.py:135
  56.1 1.5 collective-permute-start.15
  57.6 2.8 collective-permute-start.14
  60.4 1.8 multiply_sine_fusion
  62.8 1.3 collective-permute-start.26
  64.1 14.2 %project.1 = (bf16[256,2048]{1,0:T(8,128)(2,1)}, bf16[2048,256]{1,0:T(8,128)(2,1)}, bf16[256,2048]{1,0:T(8,128)(2,1)}, bf16[2048,256]{1,0:T(8,128)(2,1)}, bf16[2...) custom-call(s32[1]{0:T(128)} %bitcast.refs_0_.me_ref.refs_1_, s32[8]{0:T(128)} %stack.35.refs_1_.refs_0_, ...), custom_call_target="tpu_custom_call" | custom-call | flops 3221225472 | bytes 15237120 | tf_op jit(solution)/shard_map/project/pallas_call | solution.py:76
  79.5 3.0 collective-permute-start.25
  82.5 20.7 %attend.1 = (bf16[512,256]{1,0:T(8,128)(2,1)}, bf16[512,256]{1,0:T(8,128)(2,1)}, bf16[512,256]{1,0:T(8,128)(2,1)}, bf16[512,256]{1,0:T(8,128)(2,1)}, bf16[256,2048]{1,0:T(8,128)(2,1)}, /*index=5*/f32[4,2048]{1,0:T(4,128)}) custom-call(s32[1,16]{1,0:T(1,128)} %refs_0_.1, s32[1]{0:T(128)} %bitcast.refs_0_.me_ref.refs_1_, ...), custom_call_target="tpu_custom_call" | custom-call | flops 17179869184 | bytes 4194304 | tf_op jit(solution)/shard_map/attend/pallas_call | solution.py:365
  106.6 1.5 collective-permute-start.28
  108.1 5.5 %collective-permute-done.17.refs_2_ = bf16[512,256]{1,0:T(8,128)(2,1)S(1)} collective-permute-done((bf16[512,256]{1,0:T(8,128)(2,1)}, bf16[512,256]{1,0:T(8,128)(2,1)S(1)}, u32[]{:S(2)}, u32[]{:S(2)}) %collective-permute-start.17) | collective-permute-done | bytes 262176 | tf_op jit(solution)/shard_map/ppermute | solution.py:135
  113.6 4.8 %collective-permute-done.18.refs_3_ = bf16[512,256]{1,0:T(8,128)(2,1)} collective-permute-done((bf16[512,256]{1,0:T(8,128)(2,1)}, bf16[512,256]{1,0:T(8,128)(2,1)}, u32[]{:S(2)}, u32[]{:S(2)}) %collective-permute-start.18) | collective-permute-done | bytes 262176 | tf_op jit(solution)/shard_map/ppermute | solution.py:135
  118.9 2.5 collective-permute-done.27.refs_16_.refs_11_
  121.4 11.0 %collective-permute-done.28.refs_17_.refs_12_ = bf16[2112,128]{1,0:T(8,128)(2,1)S(1)} collective-permute-done((bf16[2112,128]{1,0:T(8,128)(2,1)}, bf16[2112,128]{1,0:T(8,128)(2,1)S(1)}, u32[]{:S(2)}, u32[]{:S(2)}) %collective-permute-start.28) | collective-permute-done | bytes 540704 | tf_op jit(solution)/shard_map/ppermute | solution.py:135
  133.2 4.8 %join.1 = (f32[512,1024]{1,0:T(8,128)}, bf16[512,1024]{1,0:T(8,128)(2,1)}) custom-call(bf16[512,256]{1,0:T(8,128)(2,1)} %get-tuple-element.70.refs_0_, bf16[512,256]{1,0:T(8,128)(2,1)} %copy-done.32, bf16[512,256]{1,0:T(8,128)(2,1)} %copy-done.33, bf16[512,256]{1,0:T(8,128)(2,1)} %collective-permute-done.18.refs_3_, ...), custom_call_target="tpu_custom_call" | custom-call | flops 1073741824 | bytes 7372800 | tf_op jit(solution)/shard_map/join/pallas_call | solution.py:76
  139.0 1.9 collective-permute-done.29.refs_2_.refs_1_
  141.9 20.4 %mlp.2 = (bf16[1024,704]{1,0:T(8,128)(2,1)}, bf16[1024,704]{1,0:T(8,128)(2,1)}, bf16[1024,704]{1,0:T(8,128)(2,1)}, bf16[512,1024]{1,0:T(8,128)(2,1)}, bf16[512,1...) custom-call(s32[8]{0:T(128)} %stack.35.refs_1_.refs_0_, bf16[512,1024]{1,0:T(8,128)(2,1)} %get-tuple-element.77.refs_1_.refs_0_, ...), custom_call_target="tpu_custom_call" | custom-call | flops 7381975040 | bytes 19660800 | tf_op jit(solution)/shard_map/mlp/pallas_call | solution.py:76
  162.3 1.5 collective-permute-done.30.refs_0_
  164.8 2.9 collective-permute-done.31.refs_2_.refs_3_
  168.7 17.8 %mlp.3 = (bf16[1024,704]{1,0:T(8,128)(2,1)}, bf16[1024,704]{1,0:T(8,128)(2,1)}, bf16[1024,704]{1,0:T(8,128)(2,1)}, bf16[512,1024]{1,0:T(8,128)(2,1)}, bf16[512,1024]{1,0:T(8,128)(2,1)}) custom-call(s32[8]{0:T(128)} %stack.35.refs_1_.refs_0_, bf16[512,1024]{1,0:T(8,128)(2,1)} %gate.13.refs_1_.refs_2_, bf16[512,1024]{1,0:T(8,128)(2,1)} %copy-done.43, ...), custom_call_target="tpu_custom_call" | custom-call | flops 7381975040 | bytes 15335424 | tf_op jit(solution)/shard_map/mlp/pallas_call | solution.py:76
  186.7 2.7 collective-permute-done.32.refs_1_
  190.4 2.7 fold.4.refs_15_
  194.1 23.4 %mlp_rest.1 = (bf16[512,1024]{1,0:T(8,128)(2,1)}, bf16[512,1024]{1,0:T(8,128)(2,1)}, bf16[512,1024]{1,0:T(8,128)(2,1)}, bf16[512,1024]{1,0:T(8,128)(2,1)}, bf16[8,2112,128]{2,1,0:T(8,128)(2,1)}) custom-call(bf16[512,1024]{1,0:T(8,128)(2,1)} %get-tuple-element.77.refs_1_.refs_0_, bf16[512,1024]{1,0:T(8,128)(2,1)} %copy-done.42, ...), custom_call_target="tpu_custom_call" | custom-call | flops 11811160064 | bytes 33554432 | tf_op jit(solution)/shard_map/mlp_rest/pallas_call | solution.py:56
  221.3 2.1 collective-permute-done.35.refs_8_
  224.5 6.5 %middle_back.1 = (f32[512,1024]{1,0:T(8,128)}, bf16[512,1024]{1,0:T(8,128)(2,1)}, f32[1,1024]{1,0:T(1,128)}, bf16[256,512]{1,0:T(8,128)(2,1)}, bf16[256,512]{1,0...) custom-call(f32[512,1024]{1,0:T(8,128)} %get-tuple-element.76.refs_0_, ...), custom_call_target="tpu_custom_call" | custom-call | flops 1073741824 | bytes 12648448 | tf_op jit(solution)/shard_map/middle_back/pallas_call | solution.py:76
  231.0 3.7 out_weight.1
  237.1 7.0 %collective-permute-done.37.refs_2_.refs_13_ = bf16[256,512]{1,0:T(8,128)(2,1)S(1)} collective-permute-done((bf16[256,512]{1,0:T(8,128)(2,1)S(1)}, bf16[256,512]{1,0:T(8,128)(2,1)S(1)}, u32[]{:S(2)}, u32[]{:S(2)}) %collective-permute-start.37) | collective-permute-done | bytes 262176 | tf_op jit(solution)/shard_map/ppermute | solution.py:135
  244.0 4.5 %collective-permute-done.38.refs_3_.refs_14_ = bf16[256,512]{1,0:T(8,128)(2,1)S(1)} collective-permute-done((bf16[256,512]{1,0:T(8,128)(2,1)S(1)}, bf16[256,512]{1,0:T(8,128)(2,1)S(1)}, u32[]{:S(2)}, u32[]{:S(2)}) %collective-permute-start.38) | collective-permute-done | bytes 262176 | tf_op jit(solution)/shard_map/ppermute | solution.py:135
  249.2 2.8 fold.5.refs_16_
  253.8 2.2 fold.6.refs_15_
  257.7 31.6 %attend_back.1 = (bf16[768,2048]{1,0:T(8,128)(2,1)}, bf16[512,256]{1,0:T(8,128)(2,1)}, bf16[512,256]{1,0:T(8,128)(2,1)}, bf16[512,256]{1,0:T(8,128)(2,1)}, bf16[512,256]{1,0:T(8,128)(2,1)}) custom-call(s32[1,16]{1,0:T(1,128)} %refs_0_.1, s32[1]{0:T(128)} %bitcast.refs_0_.me_ref.refs_1_, bf16[256,2048]{1,0:T(8,128)(2,1)} %get-tuple-element.67.q_ref.refs_2_, ...), custom_call_target="tpu_custom_call" | custom-call | flops 21474836480 | bytes 18546688 | tf_op jit(solution)/shard_map/attend_back/pallas_call | solution.py:56
  290.5 12.2 %unproject.1 = (bf16[512,1024]{1,0:T(8,128)(2,1)}, bf16[512,1024]{1,0:T(8,128)(2,1)}, bf16[512,1024]{1,0:T(8,128)(2,1)}, bf16[512,1024]{1,0:T(8,128)(2,1)}, f32[1,1024]{1,0:T(1,128)}) custom-call(s32[1]{0:T(128)} %bitcast.refs_0_.me_ref.refs_1_, bf16[512,1024]{1,0:T(8,128)(2,1)} %bitcast.53, bf16[512,1024]{1,0:T(8,128)(2,1)} %collective-permute-done.refs_3_.refs_2_, ...), custom_call_target="tpu_custom_call" | custom-call | flops 3221225472 | bytes 13139968 | tf_op jit(solution)/shard_map/unproject/pallas_call | solution.py:76
  304.8 1.4 collective-permute-done.45.refs_2_.refs_8_
  306.9 6.0 %collective-permute-done.46.refs_3_.refs_9_ = bf16[512,256]{1,0:T(8,128)(2,1)S(1)} collective-permute-done((bf16[512,256]{1,0:T(8,128)(2,1)S(1)}, bf16[512,256]{1,0:T(8,128)(2,1)S(1)}, u32[]{:S(2)}, u32[]{:S(2)}) %collective-permute-start.46) | collective-permute-done | bytes 262176 | tf_op jit(solution)/shard_map/ppermute | solution.py:135
  312.9 4.2 %collective-permute-done.47.refs_4_.refs_10_ = bf16[512,256]{1,0:T(8,128)(2,1)S(1)} collective-permute-done((bf16[512,256]{1,0:T(8,128)(2,1)S(1)}, bf16[512,256]{1,0:T(8,128)(2,1)S(1)}, u32[]{:S(2)}, u32[]{:S(2)}) %collective-permute-start.47) | collective-permute-done | bytes 262176 | tf_op jit(solution)/shard_map/ppermute | solution.py:135
  318.2 2.7 fold.7.refs_11_
  322.6 9.2 %qkv_weight.1 = (bf16[4,512,128]{2,1,0:T(8,128)(2,1)}, bf16[4,512,128]{2,1,0:T(8,128)(2,1)}, bf16[4,512,128]{2,1,0:T(8,128)(2,1)}, bf16[4,512,128]{2,1,0:T(8,128)(2,1)}) custom-call(s32[1]{0:T(128)} %bitcast.refs_0_.me_ref.refs_1_, s32[1]{0:T(128)} %bitcast.27.refs_1_, bf16[512,1024]{1,0:T(8,128)(2,1)} %bitcast.54, ...), custom_call_target="tpu_custom_call" | custom-call | flops 3221225472 | bytes 15237120 | tf_op jit(solution)/shard_map/qkv_weight/pallas_call | solution.py:56
  333.4 1.4 collective-permute-done.56
  336.2 10.7 %collective-permute-done.57 = f32[2,1024]{1,0:T(2,128)S(1)} collective-permute-done((f32[2,1024]{1,0:T(2,128)S(1)}, f32[2,1024]{1,0:T(2,128)S(1)}, u32[]{:S(2)}, u32[]{:S(2)}) %collective-permute-start.57) | collective-permute-done | bytes 8224 | tf_op jit(solution)/shard_map/ppermute | solution.py:135
  347.5 3.1 collective-permute-done.58
  351.1 3.1 collective-permute-done.59
  355.1 3.6 fusion
  358.7 6.2 %collective-permute-done.60 = f32[2,1024]{1,0:T(2,128)S(1)} collective-permute-done((f32[2,1024]{1,0:T(2,128)S(1)}, f32[2,1024]{1,0:T(2,128)S(1)}, u32[]{:S(2)}, u32[]{:S(2)}) %collective-permute-start.60) | collective-permute-done | bytes 8224 | tf_op jit(solution)/shard_map/ppermute | solution.py:135
  364.9 1.2 convert_add_fusion.1
  367.9 1.6 collective-permute-start.51
  371.3 1.8 collective-permute-start.54
  373.8 6.0 %input_back.1 = (f32[512,1024]{1,0:T(8,128)}, f32[512,1024]{1,0:T(8,128)}) custom-call(s32[1]{0:T(128)} %bitcast.refs_0_.me_ref.refs_1_, bf16[512,1024]{1,0:T(8,128)(2,1)} %bitcast.55, f32[1,1024]{1,0:T(1,128)} %bitcast.69, f32[512,1024]{1,0:T(8,128)} %get-tuple-element.95.refs_3_, bf16[512,1024]{1,0:T(8,128)(2,1)} %get-tuple-element.106.refs_4_, ...), custom_call_target="tpu_custom_call" | custom-call | bytes 11567104 | tf_op jit(solution)/shard_map/input_back/pallas_call | solution.py:76
  381.0 3.6 collective-permute-done.54
  384.7 1.5 collective-permute-start.55
  386.2 2.1 collective-permute-done.52
  388.3 1.4 collective-permute-done.55
  (241 shorter events, 53.4 us)
Async XLA Ops:
  7.2 384.2 %reduce-scatter.2.cloned.1.call-start = ((), (), s32[]{:S(2)}) async-start(), calls=%async_computation.1 | async-start | bytes 4866048 | tf_op jit(solution)/shard_map/reduce_scatter | solution.py:780
  7.3 29.1 %collective-permute-start.1 = (bf16[512,1024]{1,0:T(8,128)(2,1)}, bf16[512,1024]{1,0:T(8,128)(2,1)S(1)}, u32[]{:S(2)}, u32[]{:S(2)}) collective-permute-start(bf16[512,1024]{1,0:T(8,128)(2,1)} %bitcast.49), channel_id=1, source_target_pairs={{0,2},{1,3},{2,0},{3,1},{4,6},{5,7},{6,4},{7,5},{8,10},{9,11},{10,... | collective-permute-start | bytes 3145736 | tf_op jit(solution)/shard_map/ppermute | solution.py:135
  12.3 8.7 %collective-permute-start.2 = (bf16[1024,128]{1,0:T(8,128)(2,1)S(1)}, bf16[1024,128]{1,0:T(8,128)(2,1)S(1)}, u32[]{:S(2)}, u32[]{:S(2)}) collective-permute-start(bf16[1024,128]{1,0:T(8,128)(2,1)S(1)} %pad_maximum_fusion.2.refs_10_), channel_id=1, source_target_pairs={{0,8},{4,12},{8,24},{12,28},{24,16},{28,20},{16,0},{20,4},{1,9},{5... | collective-permute-start | bytes 786440 | tf_op jit(solution)/shard_map/ppermute | solution.py:206
  21.0 7.9 %collective-permute-start.3 = (bf16[1024,128]{1,0:T(8,128)(2,1)S(1)}, bf16[1024,128]{1,0:T(8,128)(2,1)}, u32[]{:S(2)}, u32[]{:S(2)}) collective-permute-start(bf16[1024,128]{1,0:T(8,128)(2,1)S(1)} %collective-permute-done.2.refs_11_), channel_id=1, source_target_pairs={{0,8},{4,12},{8,24},{12,28},{24,16},{28,20},{16,0},{20,4},{1,9},{5... | collective-permute-start | bytes 786440 | tf_op jit(solution)/shard_map/ppermute | solution.py:206
  21.8 15.6 %collective-permute-start.9 = (bf16[1024,128]{1,0:T(8,128)(2,1)S(1)}, bf16[1024,128]{1,0:T(8,128)(2,1)}, u32[]{:S(2)}, u32[]{:S(2)}) collective-permute-start(bf16[1024,128]{1,0:T(8,128)(2,1)S(1)} %pad_maximum_fusion.2.refs_10_), channel_id=1, source_target_pairs={{0,4},{4,0},{8,12},{12,8},{16,20},{20,16},{24,28},{28,24},{1,5},{5... | collective-permute-start | bytes 786440 | tf_op jit(solution)/shard_map/ppermute | solution.py:135
  23.2 39.6 %collective-permute-start = (bf16[512,1024]{1,0:T(8,128)(2,1)}, bf16[512,1024]{1,0:T(8,128)(2,1)}, u32[]{:S(2)}, u32[]{:S(2)}) collective-permute-start(bf16[512,1024]{1,0:T(8,128)(2,1)} %bitcast.50), channel_id=1, source_target_pairs={{0,1},{1,0},{2,3},{3,2},{4,5},{5,4},{6,7},{7,6},{8,9},{9,8},{10,11... | collective-permute-start | bytes 3145736 | tf_op jit(solution)/shard_map/ppermute | solution.py:135
  25.2 14.0 %collective-permute-start.8 = (bf16[512,256]{1,0:T(8,128)(2,1)S(1)}, bf16[512,256]{1,0:T(8,128)(2,1)}, u32[]{:S(2)}, u32[]{:S(2)}) collective-permute-start(bf16[512,256]{1,0:T(8,128)(2,1)S(1)} %get-tuple-element.125), channel_id=1, source_target_pairs={{0,3},{1,2},{2,1},{3,0},{4,7},{5,6},{6,5},{7,4},{8,11},{9,10},{10,... | collective-permute-start | bytes 786440 | tf_op jit(solution)/shard_map/ppermute | solution.py:135
  28.8 7.5 %collective-permute-start.4 = (bf16[1024,128]{1,0:T(8,128)(2,1)}, bf16[1024,128]{1,0:T(8,128)(2,1)S(1)}, u32[]{:S(2)}, u32[]{:S(2)}) collective-permute-start(bf16[1024,128]{1,0:T(8,128)(2,1)} %collective-permute-done.3.refs_12_), channel_id=1, source_target_pairs={{0,8},{4,12},{8,24},{12,28},{24,16},{28,20},{16,0},{20,4},{1,9},{5... | collective-permute-start | bytes 786440 | tf_op jit(solution)/shard_map/ppermute | solution.py:206
  36.3 4.8 %collective-permute-start.6 = (bf16[512,256]{1,0:T(8,128)(2,1)S(1)}, bf16[512,256]{1,0:T(8,128)(2,1)S(1)}, u32[]{:S(2)}, u32[]{:S(2)}) collective-permute-start(bf16[512,256]{1,0:T(8,128)(2,1)S(1)} %get-tuple-element.126), channel_id=1, source_target_pairs={{0,1},{1,0},{2,3},{3,2},{4,5},{5,4},{6,7},{7,6},{8,9},{9,8},{10,11... | collective-permute-start | bytes 786440 | tf_op jit(solution)/shard_map/ppermute | solution.py:135
  36.3 8.7 %collective-permute-start.7 = (bf16[512,256]{1,0:T(8,128)(2,1)S(1)}, bf16[512,256]{1,0:T(8,128)(2,1)S(1)}, u32[]{:S(2)}, u32[]{:S(2)}) collective-permute-start(bf16[512,256]{1,0:T(8,128)(2,1)S(1)} %get-tuple-element.128), channel_id=1, source_target_pairs={{0,2},{1,3},{2,0},{3,1},{4,6},{5,7},{6,4},{7,5},{8,10},{9,11},{10,... | collective-permute-start | bytes 786440 | tf_op jit(solution)/shard_map/ppermute | solution.py:135
  38.6 24.2 %collective-permute-start.5 = (bf16[512,1024]{1,0:T(8,128)(2,1)S(1)}, bf16[512,1024]{1,0:T(8,128)(2,1)}, u32[]{:S(2)}, u32[]{:S(2)}) collective-permute-start(bf16[512,1024]{1,0:T(8,128)(2,1)S(1)} %copy-done.6), channel_id=1, source_target_pairs={{0,1},{1,0},{2,3},{3,2},{4,5},{5,4},{6,7},{7,6},{8,9},{9,8},{10,11... | collective-permute-start | bytes 3145736 | tf_op jit(solution)/shard_map/ppermute | solution.py:135
  39.3 18.3 %collective-permute-start.13 = (bf16[2112,128]{1,0:T(8,128)(2,1)}, bf16[2112,128]{1,0:T(8,128)(2,1)}, u32[]{:S(2)}, u32[]{:S(2)}) collective-permute-start(bf16[2112,128]{1,0:T(8,128)(2,1)} %gate.10.refs_5_), channel_id=1, source_target_pairs={{0,8},{4,12},{8,24},{12,28},{24,16},{28,20},{16,0},{20,4},{1,9},{5... | collective-permute-start | bytes 1622024 | tf_op jit(solution)/shard_map/ppermute | solution.py:206
  41.1 37.3 %copy-start.36 = (s32[2048]{0:T(1024)}, s32[2048]{0:T(1024)S(1)}, u32[]{:S(2)}) copy-start(s32[2048]{0:T(1024)S(1)} %select_reduce_fusion) | copy-start | bytes 24580
  41.1 9.2 %collective-permute-start.10 = (bf16[1024,128]{1,0:T(8,128)(2,1)S(1)}, bf16[1024,128]{1,0:T(8,128)(2,1)S(1)}, u32[]{:S(2)}, u32[]{:S(2)}) collective-permute-start(bf16[1024,128]{1,0:T(8,128)(2,1)S(1)} %collective-permute-done.2.refs_11_), channel_id=1, source_target_pairs={{0,4},{4,0},{8,12},{12,8},{16,20},{20,16},{24,28},{28,24},{1,5},{5... | collective-permute-start | bytes 786440 | tf_op jit(solution)/shard_map/ppermute | solution.py:135
  45.1 11.0 %collective-permute-start.11 = (bf16[1024,128]{1,0:T(8,128)(2,1)}, bf16[1024,128]{1,0:T(8,128)(2,1)}, u32[]{:S(2)}, u32[]{:S(2)}) collective-permute-start(bf16[1024,128]{1,0:T(8,128)(2,1)} %collective-permute-done.3.refs_12_), channel_id=1, source_target_pairs={{0,4},{4,0},{8,12},{12,8},{16,20},{20,16},{24,28},{28,24},{1,5},{5... | collective-permute-start | bytes 786440 | tf_op jit(solution)/shard_map/ppermute | solution.py:135
  50.3 11.8 %collective-permute-start.12 = (bf16[1024,128]{1,0:T(8,128)(2,1)S(1)}, bf16[1024,128]{1,0:T(8,128)(2,1)S(1)}, u32[]{:S(2)}, u32[]{:S(2)}) collective-permute-start(bf16[1024,128]{1,0:T(8,128)(2,1)S(1)} %copy-done.17), channel_id=1, source_target_pairs={{0,4},{4,0},{8,12},{12,8},{16,20},{20,16},{24,28},{28,24},{1,5},{5... | collective-permute-start | bytes 786440 | tf_op jit(solution)/shard_map/ppermute | solution.py:135
  56.1 22.3 %collective-permute-start.15 = (bf16[2112,128]{1,0:T(8,128)(2,1)}, bf16[2112,128]{1,0:T(8,128)(2,1)S(1)}, u32[]{:S(2)}, u32[]{:S(2)}) collective-permute-start(bf16[2112,128]{1,0:T(8,128)(2,1)} %gate.10.refs_5_), channel_id=1, source_target_pairs={{0,4},{4,0},{8,12},{12,8},{16,20},{20,16},{24,28},{28,24},{1,5},{5... | collective-permute-start | bytes 1622024 | tf_op jit(solution)/shard_map/ppermute | solution.py:135
  57.6 22.0 %collective-permute-start.14 = (bf16[2112,128]{1,0:T(8,128)(2,1)}, bf16[2112,128]{1,0:T(8,128)(2,1)}, u32[]{:S(2)}, u32[]{:S(2)}) collective-permute-start(bf16[2112,128]{1,0:T(8,128)(2,1)} %collective-permute-done.13.refs_21_.refs_6_), channel_id=1, source_target_pairs={{0,8},{4,12},{8,24},{12,28},{24,16},{28,20},{16,0},{20,4},{1,9},{5... | collective-permute-start | bytes 1622024 | tf_op jit(solution)/shard_map/ppermute | solution.py:206
  62.2 41.0 %collective-permute-start.23 = (bf16[512,1024]{1,0:T(8,128)(2,1)}, bf16[512,1024]{1,0:T(8,128)(2,1)S(1)}, u32[]{:S(2)}, u32[]{:S(2)}) collective-permute-start(bf16[512,1024]{1,0:T(8,128)(2,1)} %bitcast.23.refs_3_.refs_4_.refs_1_), channel_id=1, source_target_pairs={{0,2},{1,3},{2,0},{3,1},{4,6},{5,7},{6,4},{7,5},{8,10},{9,11},{10,... | collective-permute-start | bytes 3145736 | tf_op jit(solution)/shard_map/ppermute | solution.py:135
  62.8 41.3 %collective-permute-start.22 = (bf16[512,1024]{1,0:T(8,128)(2,1)}, bf16[512,1024]{1,0:T(8,128)(2,1)}, u32[]{:S(2)}, u32[]{:S(2)}) collective-permute-start(bf16[512,1024]{1,0:T(8,128)(2,1)} %bitcast.23.refs_3_.refs_4_.refs_1_), channel_id=1, source_target_pairs={{0,1},{1,0},{2,3},{3,2},{4,5},{5,4},{6,7},{7,6},{8,9},{9,8},{10,11... | collective-permute-start | bytes 3145736 | tf_op jit(solution)/shard_map/ppermute | solution.py:135
  62.8 41.4 %collective-permute-start.26 = (bf16[2112,128]{1,0:T(8,128)(2,1)}, bf16[2112,128]{1,0:T(8,128)(2,1)S(1)}, u32[]{:S(2)}, u32[]{:S(2)}) collective-permute-start(bf16[2112,128]{1,0:T(8,128)(2,1)} %collective-permute-done.13.refs_21_.refs_6_), channel_id=1, source_target_pairs={{0,4},{4,0},{8,12},{12,8},{16,20},{20,16},{24,28},{28,24},{1,5},{5... | collective-permute-start | bytes 1622024 | tf_op jit(solution)/shard_map/ppermute | solution.py:135
  78.4 27.7 %collective-permute-start.20 = (bf16[256,1024]{1,0:T(8,128)(2,1)}, bf16[256,1024]{1,0:T(8,128)(2,1)S(1)}, u32[]{:S(2)}, u32[]{:S(2)}) collective-permute-start(bf16[256,1024]{1,0:T(8,128)(2,1)} %get-tuple-element.74.refs_4_.refs_3_), channel_id=1, source_target_pairs={{0,2},{1,3},{2,0},{3,1},{4,6},{5,7},{6,4},{7,5},{8,10},{9,11},{10,... | collective-permute-start | bytes 1572872 | tf_op jit(solution)/shard_map/ppermute | solution.py:135
  79.5 27.1 %collective-permute-start.25 = (bf16[2112,128]{1,0:T(8,128)(2,1)}, bf16[2112,128]{1,0:T(8,128)(2,1)}, u32[]{:S(2)}, u32[]{:S(2)}) collective-permute-start(bf16[2112,128]{1,0:T(8,128)(2,1)} %collective-permute-done.14.refs_0_.refs_7_), channel_id=1, source_target_pairs={{0,8},{4,12},{8,24},{12,28},{24,16},{28,20},{16,0},{20,4},{1,9},{5... | collective-permute-start | bytes 1622024 | tf_op jit(solution)/shard_map/ppermute | solution.py:206
  103.2 2.0 collective-permute-start.16
  104.2 17.2 %collective-permute-start.24 = (bf16[512,1024]{1,0:T(8,128)(2,1)}, bf16[512,1024]{1,0:T(8,128)(2,1)}, u32[]{:S(2)}, u32[]{:S(2)}) collective-permute-start(bf16[512,1024]{1,0:T(8,128)(2,1)} %gate.12.refs_11_.refs_3_.refs_6_), channel_id=1, source_target_pairs={{0,1},{1,0},{2,3},{3,2},{4,5},{5,4},{6,7},{7,6},{8,9},{9,8},{10,11... | collective-permute-start | bytes 3145736 | tf_op jit(solution)/shard_map/ppermute | solution.py:135
  104.2 9.4 %collective-permute-start.17 = (bf16[512,256]{1,0:T(8,128)(2,1)}, bf16[512,256]{1,0:T(8,128)(2,1)S(1)}, u32[]{:S(2)}, u32[]{:S(2)}) collective-permute-start(bf16[512,256]{1,0:T(8,128)(2,1)} %get-tuple-element.72), channel_id=1, source_target_pairs={{0,2},{1,3},{2,0},{3,1},{4,6},{5,7},{6,4},{7,5},{8,10},{9,11},{10,... | collective-permute-start | bytes 786440 | tf_op jit(solution)/shard_map/ppermute | solution.py:135
  105.2 13.2 %collective-permute-start.18 = (bf16[512,256]{1,0:T(8,128)(2,1)}, bf16[512,256]{1,0:T(8,128)(2,1)}, u32[]{:S(2)}, u32[]{:S(2)}) collective-permute-start(bf16[512,256]{1,0:T(8,128)(2,1)} %get-tuple-element.73), channel_id=1, source_target_pairs={{0,3},{1,2},{2,1},{3,0},{4,7},{5,6},{6,5},{7,4},{8,11},{9,10},{10,... | collective-permute-start | bytes 786440 | tf_op jit(solution)/shard_map/ppermute | solution.py:135
  106.1 15.3 %collective-permute-start.27 = (bf16[2112,128]{1,0:T(8,128)(2,1)}, bf16[2112,128]{1,0:T(8,128)(2,1)S(1)}, u32[]{:S(2)}, u32[]{:S(2)}) collective-permute-start(bf16[2112,128]{1,0:T(8,128)(2,1)} %collective-permute-done.14.refs_0_.refs_7_), channel_id=1, source_target_pairs={{0,4},{4,0},{8,12},{12,8},{16,20},{20,16},{24,28},{28,24},{1,5},{5... | collective-permute-start | bytes 1622024 | tf_op jit(solution)/shard_map/ppermute | solution.py:135
  106.6 25.8 %collective-permute-start.28 = (bf16[2112,128]{1,0:T(8,128)(2,1)}, bf16[2112,128]{1,0:T(8,128)(2,1)S(1)}, u32[]{:S(2)}, u32[]{:S(2)}) collective-permute-start(bf16[2112,128]{1,0:T(8,128)(2,1)} %collective-permute-done.25.refs_13_.refs_8_), channel_id=1, source_target_pairs={{0,4},{4,0},{8,12},{12,8},{16,20},{20,16},{24,28},{28,24},{1,5},{5... | collective-permute-start | bytes 1622024 | tf_op jit(solution)/shard_map/ppermute | solution.py:135
  113.6 5.3 %collective-permute-start.19 = (bf16[256,1024]{1,0:T(8,128)(2,1)S(1)}, bf16[256,1024]{1,0:T(8,128)(2,1)S(1)}, u32[]{:S(2)}, u32[]{:S(2)}) collective-permute-start(bf16[256,1024]{1,0:T(8,128)(2,1)S(1)} %copy-done.8), channel_id=1, source_target_pairs={{0,1},{1,0},{2,3},{3,2},{4,5},{5,4},{6,7},{7,6},{8,9},{9,8},{10,11... | collective-permute-start | bytes 1572872 | tf_op jit(solution)/shard_map/ppermute | solution.py:135
  118.4 3.0 collective-permute-start.21
  138.0 2.9 collective-permute-start.29
  138.0 25.8 %collective-permute-start.30 = (bf16[512,1024]{1,0:T(8,128)(2,1)}, bf16[512,1024]{1,0:T(8,128)(2,1)S(1)}, u32[]{:S(2)}, u32[]{:S(2)}) collective-permute-start(bf16[512,1024]{1,0:T(8,128)(2,1)} %get-tuple-element.77.refs_1_.refs_0_), channel_id=1, source_target_pairs={{0,2},{1,3},{2,0},{3,1},{4,6},{5,7},{6,4},{7,5},{8,10},{9,11},{10,... | collective-permute-start | bytes 3145736 | tf_op jit(solution)/shard_map/ppermute | solution.py:135
  164.8 2.9 collective-permute-start.31
  186.5 2.9 collective-permute-start.32
  193.1 25.4 %collective-permute-start.36 = (bf16[512,1024]{1,0:T(8,128)(2,1)}, bf16[512,1024]{1,0:T(8,128)(2,1)S(1)}, u32[]{:S(2)}, u32[]{:S(2)}) collective-permute-start(bf16[512,1024]{1,0:T(8,128)(2,1)} %fold.4.refs_15_), channel_id=1, source_target_pairs={{0,2},{1,3},{2,0},{3,1},{4,6},{5,7},{6,4},{7,5},{8,10},{9,11},{10,... | collective-permute-start | bytes 3145736 | tf_op jit(solution)/shard_map/ppermute | solution.py:135
  220.8 2.7 collective-permute-start.35
  221.1 15.9 %collective-permute-start.34 = (bf16[512,1024]{1,0:T(8,128)(2,1)S(1)}, bf16[512,1024]{1,0:T(8,128)(2,1)S(1)}, u32[]{:S(2)}, u32[]{:S(2)}) collective-permute-start(bf16[512,1024]{1,0:T(8,128)(2,1)S(1)} %copy-done.41), channel_id=1, source_target_pairs={{0,1},{1,0},{2,3},{3,2},{4,5},{5,4},{6,7},{7,6},{8,9},{9,8},{10,11... | collective-permute-start | bytes 3145736 | tf_op jit(solution)/shard_map/ppermute | solution.py:135
  234.7 18.3 %collective-permute-start.41 = (bf16[256,1024]{1,0:T(8,128)(2,1)}, bf16[256,1024]{1,0:T(8,128)(2,1)S(1)}, u32[]{:S(2)}, u32[]{:S(2)}) collective-permute-start(bf16[256,1024]{1,0:T(8,128)(2,1)} %get-tuple-element.103), channel_id=1, source_target_pairs={{0,1},{1,0},{2,3},{3,2},{4,5},{5,4},{6,7},{7,6},{8,9},{9,8},{10,11... | collective-permute-start | bytes 1572872 | tf_op jit(solution)/shard_map/ppermute | solution.py:135
  234.9 9.1 %collective-permute-start.37 = (bf16[256,512]{1,0:T(8,128)(2,1)S(1)}, bf16[256,512]{1,0:T(8,128)(2,1)S(1)}, u32[]{:S(2)}, u32[]{:S(2)}) collective-permute-start(bf16[256,512]{1,0:T(8,128)(2,1)S(1)} %copy-done.58), channel_id=1, source_target_pairs={{0,2},{1,3},{2,0},{3,1},{4,6},{5,7},{6,4},{7,5},{8,10},{9,11},{10,... | collective-permute-start | bytes 786440 | tf_op jit(solution)/shard_map/ppermute | solution.py:135
  235.9 12.6 %collective-permute-start.38 = (bf16[256,512]{1,0:T(8,128)(2,1)S(1)}, bf16[256,512]{1,0:T(8,128)(2,1)S(1)}, u32[]{:S(2)}, u32[]{:S(2)}) collective-permute-start(bf16[256,512]{1,0:T(8,128)(2,1)S(1)} %copy-done.57), channel_id=1, source_target_pairs={{0,3},{1,2},{2,1},{3,0},{4,7},{5,6},{6,5},{7,4},{8,11},{9,10},{10,... | collective-permute-start | bytes 786440 | tf_op jit(solution)/shard_map/ppermute | solution.py:135
  236.6 20.4 %collective-permute-start.40 = (bf16[256,512]{1,0:T(8,128)(2,1)S(1)}, bf16[256,512]{1,0:T(8,128)(2,1)S(1)}, u32[]{:S(2)}, u32[]{:S(2)}) collective-permute-start(bf16[256,512]{1,0:T(8,128)(2,1)S(1)} %copy-done.51), channel_id=1, source_target_pairs={{0,1},{1,0},{2,3},{3,2},{4,5},{5,4},{6,7},{7,6},{8,9},{9,8},{10,11... | collective-permute-start | bytes 786440 | tf_op jit(solution)/shard_map/ppermute | solution.py:135
  252.0 37.3 %collective-permute-start.39 = (bf16[512,1024]{1,0:T(8,128)(2,1)}, bf16[512,1024]{1,0:T(8,128)(2,1)S(1)}, u32[]{:S(2)}, u32[]{:S(2)}) collective-permute-start(bf16[512,1024]{1,0:T(8,128)(2,1)} %fold.5.refs_16_), channel_id=1, source_target_pairs={{0,2},{1,3},{2,0},{3,1},{4,6},{5,7},{6,4},{7,5},{8,10},{9,11},{10,... | collective-permute-start | bytes 3145736 | tf_op jit(solution)/shard_map/ppermute | solution.py:135
  255.9 33.4 %collective-permute-start.42 = (bf16[256,1024]{1,0:T(8,128)(2,1)}, bf16[256,1024]{1,0:T(8,128)(2,1)S(1)}, u32[]{:S(2)}, u32[]{:S(2)}) collective-permute-start(bf16[256,1024]{1,0:T(8,128)(2,1)} %fold.6.refs_15_), channel_id=1, source_target_pairs={{0,2},{1,3},{2,0},{3,1},{4,6},{5,7},{6,4},{7,5},{8,10},{9,11},{10,... | collective-permute-start | bytes 1572872 | tf_op jit(solution)/shard_map/ppermute | solution.py:135
  302.8 14.4 %collective-permute-start.44 = (bf16[512,1024]{1,0:T(8,128)(2,1)}, bf16[512,1024]{1,0:T(8,128)(2,1)S(1)}, u32[]{:S(2)}, u32[]{:S(2)}) collective-permute-start(bf16[512,1024]{1,0:T(8,128)(2,1)} %get-tuple-element.109), channel_id=1, source_target_pairs={{0,1},{1,0},{2,3},{3,2},{4,5},{5,4},{6,7},{7,6},{8,9},{9,8},{10,11... | collective-permute-start | bytes 3145736 | tf_op jit(solution)/shard_map/ppermute | solution.py:135
  303.0 51.8 %collective-permute-start.33 = (bf16[512,1024]{1,0:T(8,128)(2,1)}, bf16[512,1024]{1,0:T(8,128)(2,1)}, u32[]{:S(2)}, u32[]{:S(2)}) collective-permute-start(bf16[512,1024]{1,0:T(8,128)(2,1)} %get-tuple-element.89), channel_id=1, source_target_pairs={{0,1},{1,0},{2,3},{3,2},{4,5},{5,4},{6,7},{7,6},{8,9},{9,8},{10,11... | collective-permute-start | bytes 3145736 | tf_op jit(solution)/shard_map/ppermute | solution.py:135
  303.3 2.9 collective-permute-start.45
  303.5 18.3 %collective-permute-start.49 = (bf16[256,1024]{1,0:T(8,128)(2,1)S(1)}, bf16[256,1024]{1,0:T(8,128)(2,1)S(1)}, u32[]{:S(2)}, u32[]{:S(2)}) collective-permute-start(bf16[256,1024]{1,0:T(8,128)(2,1)S(1)} %copy-done.44), channel_id=1, source_target_pairs={{0,1},{1,0},{2,3},{3,2},{4,5},{5,4},{6,7},{7,6},{8,9},{9,8},{10,11... | collective-permute-start | bytes 1572872 | tf_op jit(solution)/shard_map/ppermute | solution.py:135
  303.8 9.1 %collective-permute-start.46 = (bf16[512,256]{1,0:T(8,128)(2,1)S(1)}, bf16[512,256]{1,0:T(8,128)(2,1)S(1)}, u32[]{:S(2)}, u32[]{:S(2)}) collective-permute-start(bf16[512,256]{1,0:T(8,128)(2,1)S(1)} %copy-done.53), channel_id=1, source_target_pairs={{0,2},{1,3},{2,0},{3,1},{4,6},{5,7},{6,4},{7,5},{8,10},{9,11},{10,... | collective-permute-start | bytes 786440 | tf_op jit(solution)/shard_map/ppermute | solution.py:135
  306.2 11.0 %collective-permute-start.47 = (bf16[512,256]{1,0:T(8,128)(2,1)S(1)}, bf16[512,256]{1,0:T(8,128)(2,1)S(1)}, u32[]{:S(2)}, u32[]{:S(2)}) collective-permute-start(bf16[512,256]{1,0:T(8,128)(2,1)S(1)} %copy-done.52), channel_id=1, source_target_pairs={{0,3},{1,2},{2,1},{3,0},{4,7},{5,6},{6,5},{7,4},{8,11},{9,10},{10,... | collective-permute-start | bytes 786440 | tf_op jit(solution)/shard_map/ppermute | solution.py:135
  321.0 45.9 %collective-permute-start.48 = (bf16[512,1024]{1,0:T(8,128)(2,1)}, bf16[512,1024]{1,0:T(8,128)(2,1)S(1)}, u32[]{:S(2)}, u32[]{:S(2)}) collective-permute-start(bf16[512,1024]{1,0:T(8,128)(2,1)} %fold.7.refs_11_), channel_id=1, source_target_pairs={{0,2},{1,3},{2,0},{3,1},{4,6},{5,7},{6,4},{7,5},{8,10},{9,11},{10,... | collective-permute-start | bytes 3145736 | tf_op jit(solution)/shard_map/ppermute | solution.py:135
  322.6 32.5 %copy-start.1 = (f32[512,1024]{1,0:T(8,128)S(1)}, f32[512,1024]{1,0:T(8,128)}, u32[]{:S(2)}) copy-start(f32[512,1024]{1,0:T(8,128)} %get-tuple-element.76.refs_0_) | copy-start | bytes 6291460
  331.9 33.1 %collective-permute-start.50 = (bf16[4,512,128]{2,1,0:T(8,128)(2,1)}, bf16[4,512,128]{2,1,0:T(8,128)(2,1)}, u32[]{:S(2)}, u32[]{:S(2)}) collective-permute-start(bf16[4,512,128]{2,1,0:T(8,128)(2,1)} %get-tuple-element.119), channel_id=1, source_target_pairs={{0,4},{4,0},{8,12},{12,8},{16,20},{20,16},{24,28},{28,24},{1,5},{5... | collective-permute-start | bytes 1572872 | tf_op jit(solution)/shard_map/ppermute | solution.py:135
  333.4 1.4 collective-permute-start.56
  335.5 11.5 %collective-permute-start.57 = (f32[2,1024]{1,0:T(2,128)S(1)}, f32[2,1024]{1,0:T(2,128)S(1)}, u32[]{:S(2)}, u32[]{:S(2)}) collective-permute-start(f32[2,1024]{1,0:T(2,128)S(1)} %add.127), channel_id=1, source_target_pairs={{0,2},{1,3},{2,0},{3,1},{4,6},{5,7},{6,4},{7,5},{8,10},{9,11},{10,... | collective-permute-start | bytes 24584 | tf_op jit(solution)/shard_map/ppermute | solution.py:135
  346.9 3.7 collective-permute-start.58
  350.6 3.7 collective-permute-start.59
  351.1 22.6 %collective-permute-start.43 = (bf16[512,1024]{1,0:T(8,128)(2,1)}, bf16[512,1024]{1,0:T(8,128)(2,1)}, u32[]{:S(2)}, u32[]{:S(2)}) collective-permute-start(bf16[512,1024]{1,0:T(8,128)(2,1)} %get-tuple-element.107), channel_id=1, source_target_pairs={{0,1},{1,0},{2,3},{3,2},{4,5},{5,4},{6,7},{7,6},{8,9},{9,8},{10,11... | collective-permute-start | bytes 3145736 | tf_op jit(solution)/shard_map/ppermute | solution.py:135
  354.3 15.2 %collective-permute-start.53 = (bf16[4,512,128]{2,1,0:T(8,128)(2,1)}, bf16[4,512,128]{2,1,0:T(8,128)(2,1)}, u32[]{:S(2)}, u32[]{:S(2)}) collective-permute-start(bf16[4,512,128]{2,1,0:T(8,128)(2,1)} %get-tuple-element.121), channel_id=1, source_target_pairs={{0,8},{4,12},{8,0},{12,4},{16,24},{20,28},{24,16},{28,20},{1,9},{5... | collective-permute-start | bytes 1572872 | tf_op jit(solution)/shard_map/ppermute | solution.py:135
  354.8 10.1 %collective-permute-start.60 = (f32[2,1024]{1,0:T(2,128)S(1)}, f32[2,1024]{1,0:T(2,128)S(1)}, u32[]{:S(2)}, u32[]{:S(2)}) collective-permute-start(f32[2,1024]{1,0:T(2,128)S(1)} %add.130), channel_id=1, source_target_pairs={{0,16},{4,20},{8,24},{12,28},{16,0},{20,4},{24,8},{28,12},{1,17},{... | collective-permute-start | bytes 24584 | tf_op jit(solution)/shard_map/ppermute | solution.py:135
  367.9 11.9 %collective-permute-start.51 = (bf16[2,512,128]{2,1,0:T(8,128)(2,1)}, bf16[2,512,128]{2,1,0:T(8,128)(2,1)S(1)}, u32[]{:S(2)}, u32[]{:S(2)}) collective-permute-start(bf16[2,512,128]{2,1,0:T(8,128)(2,1)} %gate.14), channel_id=1, source_target_pairs={{0,8},{4,12},{8,0},{12,4},{16,24},{20,28},{24,16},{28,20},{1,9},{5... | collective-permute-start | bytes 786440 | tf_op jit(solution)/shard_map/ppermute | solution.py:135
  371.3 13.3 %collective-permute-start.54 = (bf16[2,512,128]{2,1,0:T(8,128)(2,1)}, bf16[2,512,128]{2,1,0:T(8,128)(2,1)S(1)}, u32[]{:S(2)}, u32[]{:S(2)}) collective-permute-start(bf16[2,512,128]{2,1,0:T(8,128)(2,1)} %gate.15), channel_id=1, source_target_pairs={{0,16},{4,20},{8,24},{12,28},{16,0},{20,4},{24,8},{28,12},{1,17},{... | collective-permute-start | bytes 786440 | tf_op jit(solution)/shard_map/ppermute | solution.py:135
  379.9 8.4 %collective-permute-start.52 = (bf16[1,512,128]{2,1,0:T(8,128)(2,1)S(1)}, bf16[1,512,128]{2,1,0:T(8,128)(2,1)S(1)}, u32[]{:S(2)}, u32[]{:S(2)}) collective-permute-start(bf16[1,512,128]{2,1,0:T(8,128)(2,1)S(1)} %slice.97), channel_id=1, source_target_pairs={{0,16},{4,20},{8,24},{12,28},{16,0},{20,4},{24,8},{28,12},{1,17},{... | collective-permute-start | bytes 393224 | tf_op jit(solution)/shard_map/ppermute | solution.py:135
  384.7 5.0 %collective-permute-start.55 = (bf16[1,512,128]{2,1,0:T(8,128)(2,1)S(1)}, bf16[1,512,128]{2,1,0:T(8,128)(2,1)S(1)}, u32[]{:S(2)}, u32[]{:S(2)}) collective-permute-start(bf16[1,512,128]{2,1,0:T(8,128)(2,1)S(1)} %slice.96), channel_id=1, source_target_pairs={{0,4},{4,0},{8,12},{12,8},{16,20},{20,16},{24,28},{28,24},{1,5},{5... | collective-permute-start | bytes 393224 | tf_op jit(solution)/shard_map/ppermute | solution.py:135
  (57 other events, 431.9 us)
Sparse Core Ops, SparseCore 0:
  219.7 86.5 reduce-scatter.1

commit v3 on v2

v3 whole, which is shorter than its diff:
```python
import functools
import math

import jax
import jax.numpy as jnp
from jax import lax
from jax.experimental import pallas as pl
from jax.experimental.pallas import tpu as pltpu
from jax.sharding import PartitionSpec as P

HEAD_DIM = 64
HALF = HEAD_DIM // 2
SEQ = 2048
NDOC = 16
NORM_EPS = 1e-06
NEG = -1e30
F32 = jnp.float32
BF16 = jnp.bfloat16
VMEM_LIMIT = 65280 << 10
COST = pl.CostEstimate(flops=3 << 30, bytes_accessed=1, transcendentals=0)

VMEM = pl.BlockSpec(memory_space=pltpu.VMEM)
SMEM = pl.BlockSpec(memory_space=pltpu.SMEM)


def shape(dims, dtype):
    return jax.ShapeDtypeStruct(dims, dtype)


def dot(a, b):
    return jnp.dot(a, b, preferred_element_type=F32)


def dot_nt(a, b):
    return lax.dot_general(a, b, (((1,), (1,)), ((), ())), preferred_element_type=F32)


def dot_tn(a, b):
    return lax.dot_general(a, b, (((0,), (0,)), ((), ())), preferred_element_type=F32)


class Fetched:
    def __init__(self, source, buffer, sems, pieces):
        self.buffer, self.waiting = buffer, {}
        self.rows = buffer.shape[0] // pieces
        for i in range(pieces):
            at = (pl.ds(i * self.rows, self.rows),) if pieces > 1 else ()
            src, dst = (source.at[at], buffer.at[at]) if at else (source, buffer)
            self.waiting[i] = pltpu.make_async_copy(src, dst, sems.at[i])

    def start(self, i):
        if i in self.waiting:
            self.waiting[i].start()

    def tile(self, first, rows):
        for i in list(self.waiting):
            if first < (i + 1) * self.rows and first + rows > i * self.rows:
                self.waiting.pop(i).wait()
        return self.buffer[first : first + rows, :]

    @property
    def ref(self):
        for i in list(self.waiting):
            self.waiting.pop(i).wait()
        return self.buffer


class Stored:
    def __init__(self, target, buffer, sems):
        self.target, self.ref, self.sems, self.copies = target, buffer, sems, []

    def send(self, *at):
        copy = pltpu.make_async_copy(
            self.ref.at[at], self.target.at[at], self.sems.at[len(self.copies)]
        )
        copy.start()
        self.copies.append(copy)


def far_call(body, name, scalars, near, ins, outs, scratch=(), flops=0, after=()):
    pieces = [i[1] if isinstance(i, tuple) else 1 for i in ins]
    ins = [i[0] if isinstance(i, tuple) else i for i in ins]
    counts = [len(scalars), len(near), len(ins), len(after), len(outs)]
    held = [*ins, *[o for o, _ in outs]]

    def kernel(*refs):
        groups = []
        for count in (*counts, len(ins), len(outs), len(outs), len(ins)):
            groups.append(refs[:count])
            refs = refs[count:]
        scalar_refs, near_refs, sources, _, targets, buffers, out_buffers, out_sems, sems = groups
        fetched = [Fetched(*f) for f in zip(sources, buffers, sems, pieces)]
        for i in range(max(pieces)):
            for f in fetched:
                f.start(i)
        stored = [Stored(*t) for t in zip(targets, out_buffers, out_sems)]
        body(scalar_refs, near_refs, fetched, stored, *refs)
        for out in stored:
            if not out.copies:
                out.send()
        for out in stored:
            for copy in out.copies:
                copy.wait()

    far = pl.BlockSpec(memory_space=pl.ANY)
    moved = sum(math.prod(a.shape) * jnp.dtype(a.dtype).itemsize for a in held)
    return pl.pallas_call(
        kernel,
        name=name,
        out_shape=[o for o, _ in outs],
        in_specs=[SMEM] * len(scalars) + [VMEM] * len(near) + [far] * (len(ins) + len(after)),
        out_specs=[far] * len(outs),
        scratch_shapes=[pltpu.VMEM(a.shape, a.dtype) for a in held]
        + [pltpu.SemaphoreType.DMA((pieces,)) for _, pieces in outs]
        + [pltpu.SemaphoreType.DMA((count,)) for count in pieces]
        + list(scratch),
        compiler_params=pltpu.CompilerParams(vmem_limit_bytes=VMEM_LIMIT),
        cost_estimate=COST,
    )(*scalars, *near, *ins, *after)


def gate(value, after):
    if not after:
        return value
    return pl.pallas_call(
        lambda *refs: None,
        name="gate",
        out_shape=shape(value.shape, value.dtype),
        in_specs=[pl.BlockSpec(memory_space=pl.ANY)] * (1 + len(after)),
        out_specs=pl.BlockSpec(memory_space=pl.ANY),
        input_output_aliases={0: 0},
    )(value, *after)


def row_scale(stream):
    return lax.rsqrt(jnp.mean(stream * stream, axis=-1, keepdims=True) + NORM_EPS)


def swap(value, axis, size, bit):
    return lax.ppermute(value, axis, [(i, i ^ bit) for i in range(size)])


def bits_down(size):
    return [1 << b for b in reversed(range(size.bit_length() - 1))]


def gather_relative(value, axis, size, hold=None):
    parts = {0: value}
    for bit in bits_down(size):
        moved = {0: swap(value, axis, size, bit)}
        if bit == 1 and hold:
            after = hold(parts[0], moved[0])
            parts.update({j: gate(v, after) for j, v in parts.items() if j})
        moved.update({j: swap(v, axis, size, bit) for j, v in parts.items() if j})
        parts.update({j | bit: v for j, v in moved.items()})
    return [parts[j] for j in range(size)]


def fold_body(scalars, near, ins, outs):
    rows = outs[0].ref.shape[0]
    step = min(rows, 128)
    for row in range(0, rows, step):
        at = slice(row, row + step)
        outs[0].ref[at, :] = sum(t.tile(row, step).astype(F32) for t in ins).astype(BF16)
        outs[0].send(at)


def fold(terms):
    pieces = max(1, terms[0].shape[0] // 128)
    outs = [(shape(terms[0].shape, BF16), pieces)]
    return far_call(fold_body, "fold", [], [], [(t, pieces) for t in terms], outs)[0]


def sum_relative(parts, axis, size, after=(), first_after=()):
    parts = dict(enumerate([[p] for p in parts]))
    bit, sent = 1, []
    while bit < size:
        kept = {}
        for j in sorted((j for j in parts if not j & bit), reverse=True):
            away = parts[j | bit]
            if len(away) > 1:
                away = gate(fold(away), after)
                sent.append(away)
            else:
                away = gate(away[0], first_after)
            kept[j] = parts[j] + [swap(away, axis, size, bit)]
        parts = kept
        bit *= 2
    return parts[0], sent


def exchange_relative(parts, axis, size):
    return [p if j == 0 else swap(p, axis, size, j) for j, p in enumerate(parts)]


def exchange_two(parts, size, after):
    width = parts[0].shape[1]
    far = gate(swap(jnp.concatenate(parts[2:], axis=1), "head", size, 2), after)
    near = swap(parts[1], "head", size, 1)
    return [parts[0], near, far[:, :width], swap(far[:, width:], "head", size, 1)]


def sum_everywhere(value, sizes):
    for axis, size in sizes:
        for bit in reversed(bits_down(size)):
            value = value + swap(value, axis, size, bit)
    return value


def column_orders(size):
    bits = bits_down(size)
    return [bits, bits[-1:] + bits[:-1]]


def ring_sources(dp, size):
    line = size // 2
    place = dp // 2 ^ dp // 4
    held = [jnp.remainder(place - k, line) for k in range(line)]
    held = [2 * (p ^ p // 2) for p in held]
    return jnp.stack([h + (dp & 1) for h in held] + [h + 1 - (dp & 1) for h in held])


def ring_step(value, size):
    line = size // 2
    ring = [p ^ p // 2 for p in range(line)]
    pairs = [(2 * ring[p] + i, 2 * ring[(p + 1) % line] + i) for p in range(line) for i in range(2)]
    return lax.ppermute(value, "dp", pairs)


def gather_columns(rows, size, holds=()):
    held, other = [rows], []
    for step in range(size // 2):
        after = holds[step](held, other) if step < len(holds) else other[-1:]
        held[step] = gate(held[step], after)
        other.append(swap(held[step], "dp", size, 1))
        if step + 1 < size // 2:
            held.append(ring_step(held[step], size))
    return held + other


def column_places(size, bits):
    places = [0]
    for bit in reversed(bits):
        places = places + [j | bit for j in places]
    return places


def scatter_step(kept, received, size, bit, hold):
    total = kept.astype(F32) + received.astype(F32)
    half = total.shape[0] // 2
    return total[:half], swap(gate(total[half:].astype(BF16), hold), "dp", size, bit)


def join_columns(from_ref, parts, outs):
    for i, part in enumerate(parts):
        part = part.ref
        lanes = part.shape[1]
        at = slice(None)
        if len(parts) > 1:
            at = pl.ds(pl.multiple_of(from_ref[i] * lanes, 128), lanes)
        for row, rows, out in outs:
            out[:, at] = part[row : row + rows, :]


def project_body(n, tile, scalars, near, ins, outs):
    me_ref, from_ref = scalars
    gain_ref, cos_ref, sin_ref = near
    count = len(ins) - 2 * n
    parts, xs, fvs = ins[:count], ins[count : count + n], ins[count + n :]
    q_out, k_out, kt_out, v_out, vt_out, w_out, wo_out = outs
    width = q_out.ref.shape[0]
    shard = xs[0].buffer.shape[0]
    w_ref = w_out.ref
    join_columns(from_ref, parts, [(0, 3 * width, w_ref), (3 * width, width, wo_out.ref)])
    w_out.send()
    wo_out.send()
    for j in range(n):
        x_ref, fv_ref = xs[j].ref, fvs[j].ref
        base = pl.multiple_of((me_ref[0] ^ j) * shard, shard)
        for t in range(0, shard, tile):
            at = pl.ds(pl.multiple_of(base + t, tile), tile)
            stream = x_ref[t : t + tile, :].astype(F32)
            normed = (stream * row_scale(stream) * gain_ref[...]).astype(BF16)
            qk = dot_nt(w_ref[: 2 * width, :], normed)
            cos, sin = cos_ref[:, at], sin_ref[:, at]
            turned = []
            for row in range(0, 2 * width, HEAD_DIM):
                first, second = qk[row : row + HALF], qk[row + HALF : row + HEAD_DIM]
                turned += [first * cos - second * sin, second * cos + first * sin]
            turned = jnp.concatenate(turned, axis=0)
            q_out.ref[:, at] = (turned[:width] * HEAD_DIM ** (-0.5)).astype(BF16)
            keys = turned[width:]
            kt_out.ref[:, at] = keys.astype(BF16)
            k_out.ref[at, :] = keys.T.astype(BF16)
            first_values = fv_ref[t : t + tile, :].astype(F32)
            values = 0.5 * dot_nt(normed, w_ref[2 * width :, :]) + 0.5 * first_values
            v_out.ref[at, :] = values.astype(BF16)
            vt_out.ref[:, at] = values.T.astype(BF16)
        at = pl.ds(base, shard)
        for out in (q_out, kt_out, vt_out):
            out.send(slice(None), at)
        for out in (k_out, v_out):
            out.send(at, slice(None))


def doc_of(len_ref, token):
    run, first, last = jnp.int32(0), jnp.int32(0), jnp.int32(SEQ)
    for doc in range(NDOC):
        end = run + len_ref[0, doc]
        inside = (token >= run) & (token < end)
        first, last = jnp.where(inside, run, first), jnp.where(inside, end, last)
        run = end
    return first, last


def attend_kernel(bq, per, heads, skip, len_ref, me_ref, q_ref, k_ref, vt_ref, start_ref, *refs):
    *ctx_refs, ot_ref, lse_ref, s_ref = refs[skip:]
    bk = bq
    block = pl.program_id(0)
    first, _ = doc_of(len_ref, block * bq)
    starts = start_ref[...]

    def score(kb, tops, diagonal):
        at = pl.ds(pl.multiple_of(kb * bk, bk), bk)
        key_index = lax.broadcasted_iota(jnp.int32, (bk, bq), 0) + kb * bk
        allowed = key_index >= starts
        if diagonal:
            allowed &= key_index <= lax.broadcasted_iota(jnp.int32, (bk, bq), 1) + block * bq
        out = []
        for h in range(heads):
            rows = slice(h * HEAD_DIM, (h + 1) * HEAD_DIM)
            scores = jnp.where(allowed, dot(k_ref[at, rows], q_ref[rows, :]), NEG)
            s_ref[h, at, :] = scores
            out.append(jnp.maximum(tops[h], jnp.max(scores.reshape(bk // 8, 8, bq), axis=0)))
        return tuple(out)

    tops = score(block, tuple(jnp.full((8, bq), NEG, F32) for _ in range(heads)), True)
    tops = lax.fori_loop(first // bk, block, lambda kb, c: score(kb, c, False), tops)
    tops = [jnp.max(t, axis=0, keepdims=True) for t in tops]

    def gather(kb, carry):
        at = pl.ds(pl.multiple_of(kb * bk, bk), bk)
        out = []
        for h in range(heads):
            rows = slice(h * HEAD_DIM, (h + 1) * HEAD_DIM)
            total, acc = carry[h]
            probs = jnp.exp(s_ref[h, at, :] - tops[h])
            total = total + jnp.sum(probs.reshape(bk // 8, 8, bq), axis=0)
            out.append((total, acc + dot(vt_ref[rows, at], probs.astype(BF16))))
        return tuple(out)

    zero = tuple((jnp.zeros((8, bq), F32), jnp.zeros((HEAD_DIM, bq), F32)) for _ in range(heads))
    sums = lax.fori_loop(first // bk, block + 1, gather, zero)
    outs = []
    for h in range(heads):
        total = jnp.sum(sums[h][0], axis=0, keepdims=True)
        outs.append(sums[h][1] * (1.0 / total))
        lse_ref[h : h + 1, :] = tops[h] + jnp.log(total)
    out = jnp.concatenate(outs, axis=0)
    ot_ref[...] = out.astype(BF16)
    out = out.T.astype(BF16)
    for j, ref in enumerate(ctx_refs):

        @pl.when((block // per) ^ me_ref[0] == j)
        def _(ref=ref):
            ref[pl.ds(pl.multiple_of((block % per) * bq, bq), bq), :] = out


def attend(lengths, me, q_t, keys, v_t, starts, shard, after):
    width = q_t.shape[0]
    heads = width // HEAD_DIM
    bq = min(512, shard)
    per = shard // bq
    n = SEQ // shard
    spec = pltpu.PrefetchScalarGridSpec(
        num_scalar_prefetch=2,
        grid=(SEQ // bq,),
        in_specs=[
            pl.BlockSpec((width, bq), lambda i, l, h: (0, i)),
            pl.BlockSpec((SEQ, width), lambda i, l, h: (0, 0)),
            pl.BlockSpec((width, SEQ), lambda i, l, h: (0, 0)),
            pl.BlockSpec((1, bq), lambda i, l, h: (0, i)),
        ]
        + [pl.BlockSpec(memory_space=pl.ANY)] * len(after),
        out_specs=[
            *[pl.BlockSpec((shard, width), lambda i, l, h: (0, 0))] * n,
            pl.BlockSpec((width, bq), lambda i, l, h: (0, i)),
            pl.BlockSpec((heads, bq), lambda i, l, h: (0, i)),
        ],
        scratch_shapes=[pltpu.VMEM((heads, SEQ, bq), F32)],
    )
    return pl.pallas_call(
        functools.partial(attend_kernel, bq, per, heads, len(after)),
        name="attend",
        grid_spec=spec,
        out_shape=[
            *[shape((shard, width), BF16)] * n,
            shape((width, SEQ), BF16),
            shape((heads, SEQ), F32),
        ],
        compiler_params=pltpu.CompilerParams(vmem_limit_bytes=VMEM_LIMIT),
        cost_estimate=COST,
    )(lengths, me, q_t, keys, v_t, starts, *after)


def attend_back_body(n, block, scalars, near, ins, outs, *scratch):
    len_ref, me_ref = scalars
    lse_ref, start_ref, cos_ref, sin_ref = near
    dos, (ot_in, *rest) = ins[:n], ins[n:]
    gp_out, *firsts = outs
    out_ref = gp_out.ref
    dq_ref, dk_ref, dv_ref, do_ref, delta_ref = scratch
    width = dq_ref.shape[0]
    heads = width // HEAD_DIM
    shard = SEQ // n
    ot_ref = ot_in.ref
    for j in range(n):
        at = pl.ds(pl.multiple_of((me_ref[0] ^ j) * shard, shard), shard)
        grad = dos[j].ref[...]
        do_ref[:, at] = grad
        product = grad.astype(F32) * ot_ref[:, at].astype(F32)
        for h in range(heads):
            delta_ref[h : h + 1, at] = jnp.sum(
                product[h * HEAD_DIM : (h + 1) * HEAD_DIM], axis=0, keepdims=True
            )
    dq_ref[...] = jnp.zeros_like(dq_ref)
    dk_ref[...] = jnp.zeros_like(dk_ref)
    dv_ref[...] = jnp.zeros_like(dv_ref)
    q_ref, k_ref, kt_ref, v_ref = (r.ref for r in rest)

    def pair(kb, qb, diagonal):
        k_at = pl.ds(pl.multiple_of(kb * block, block), block)
        q_at = pl.ds(pl.multiple_of(qb * block, block), block)
        key_index = lax.broadcasted_iota(jnp.int32, (block, block), 0) + kb * block
        allowed = key_index >= start_ref[:, q_at]
        if diagonal:
            allowed &= key_index <= lax.broadcasted_iota(jnp.int32, (block, block), 1) + qb * block
        every = range(heads)
        rows = [slice(h * HEAD_DIM, (h + 1) * HEAD_DIM) for h in every]
        q_t = [q_ref[r, q_at] for r in rows]
        do_t = [do_ref[r, q_at] for r in rows]
        scores = [dot(k_ref[k_at, r], q_t[h]) for h, r in enumerate(rows)]
        dprobs = [dot(v_ref[k_at, r], do_t[h]) for h, r in enumerate(rows)]
        probs = [
            jnp.exp(jnp.where(allowed, scores[h], NEG) - lse_ref[h : h + 1, q_at]) for h in every
        ]
        dscores = [
            (probs[h] * (dprobs[h] - delta_ref[h : h + 1, q_at])).astype(BF16) for h in every
        ]
        probs = [p.astype(BF16) for p in probs]
        dv = [dot_nt(do_t[h], probs[h]) for h in every]
        dk = [dot_nt(q_t[h], dscores[h]) for h in every]
        dq = [dot(kt_ref[rows[h], k_at], dscores[h]) for h in every]
        for h in every:
            dv_ref[rows[h], k_at] += dv[h]
            dk_ref[rows[h], k_at] += dk[h]
            dq_ref[rows[h], q_at] += dq[h]

    def outer(kb, carry):
        _, end = doc_of(len_ref, kb * block + block - 1)
        pair(kb, kb, True)

        def inner(qb, c):
            pair(kb, qb, False)
            return c

        lax.fori_loop(kb + 1, (end - 1) // block + 1, inner, 0)
        return carry

    lax.fori_loop(0, SEQ // block, outer, 0)
    for j in range(n):
        at = pl.ds(pl.multiple_of((me_ref[0] ^ j) * shard, shard), shard)
        grad = 0.5 * dv_ref[:, at]
        out_ref[2 * width :, at] = grad.astype(BF16)
        firsts[j].ref[...] = grad.T.astype(BF16)
        firsts[j].send()
    gp_out.send(slice(2 * width, 3 * width))
    cos, sin = cos_ref[...], sin_ref[...]
    for base, ref, scale in ((0, dq_ref, HEAD_DIM ** (-0.5)), (width, dk_ref, 1.0)):
        for row in range(0, width, HEAD_DIM):
            first = ref[row : row + HALF, :] * scale
            second = ref[row + HALF : row + HEAD_DIM, :] * scale
            out_ref[base + row : base + row + HALF, :] = (first * cos + second * sin).astype(BF16)
            out_ref[base + row + HALF : base + row + HEAD_DIM, :] = (
                second * cos - first * sin
            ).astype(BF16)
        gp_out.send(slice(base, base + width))


def join_body(n, tile, scalars, near, ins, outs):
    (gain_ref,) = near
    ctx, x_in, w_out = ins[:n], ins[n], ins[n + 1 :]
    mid, normed = outs
    for row in range(0, x_in.buffer.shape[0], tile):
        at = slice(row, row + tile)
        total = x_in.tile(row, tile).astype(F32)
        for c, w in zip(ctx, w_out):
            total = total + dot(c.tile(row, tile), w.ref[...])
        normed.ref[at, :] = (total * row_scale(total) * gain_ref[...]).astype(BF16)
        normed.send(at)
        mid.ref[at, :] = total
        mid.send(at)


def mlp_body(n, tile, scalars, near, ins, outs):
    (from_ref,) = scalars
    count = len(ins) - 2 * n
    parts, normed, grads = ins[:count], ins[count : count + n], ins[count + n :]
    mixed, dgate_out, dup_out, *gns = outs
    hidden = mixed.ref.shape[1]
    shard = normed[0].buffer.shape[0]
    if count > 1:
        *gns, made = gns
        w_ref = made.ref
        join_columns(from_ref, parts, [(0, 3 * hidden, w_ref)])
        made.send()
    else:
        w_ref = parts[0].ref
    w_gate, w_up, w_down = (w_ref.at[i * hidden : (i + 1) * hidden, :] for i in range(3))
    for j in reversed(range(n)):
        tokens_ref, og_ref = normed[j].ref, grads[j].ref

        def step(t, carry, tokens_ref=tokens_ref, og_ref=og_ref, j=j):
            rows = pl.ds(pl.multiple_of(t * tile, tile), tile)
            at = pl.ds(pl.multiple_of(j * shard + t * tile, tile), tile)
            tokens = tokens_ref[rows, :]
            gate = dot_nt(tokens, w_gate[...])
            up = dot_nt(tokens, w_up[...])
            gm = dot_nt(og_ref[rows, :], w_down[...])
            sig = 1.0 / (1.0 + jnp.exp(-gate))
            act = gate * sig
            mixed.ref[at, :] = (act * up).astype(BF16)
            dup = (gm * act).astype(BF16)
            dgate = (gm * up * sig * (1.0 + gate * (1.0 - sig))).astype(BF16)
            dup_out.ref[at, :] = dup
            dgate_out.ref[at, :] = dgate
            gns[j].ref[rows, :] = (dot(dgate, w_gate[...]) + dot(dup, w_up[...])).astype(BF16)
            return carry

        lax.fori_loop(0, shard // tile, step, 0)
        gns[j].send()
        for out in (mixed, dgate_out, dup_out):
            out.send(slice(j * shard, (j + 1) * shard))


def mlp_rest_body(n, tile, scalars, near, ins, outs, acc_ref):
    w_in, mixeds, ogs = ins[0], ins[1:3], ins[3 : 3 + n]
    dgates, normed, dups = ins[3 + n : 5 + n], ins[5 + n : 5 + 2 * n], ins[5 + 2 * n :]
    *parts, grads = outs
    half = n // 2
    hidden = acc_ref.shape[0]
    lanes = grads.ref.shape[2]
    shard = normed[0].buffer.shape[0]
    w_down = w_in.ref.at[2 * hidden :, :]
    for j in reversed(range(n)):
        mixed_ref = mixeds[j // half].ref
        for t in range(0, shard, tile):
            rows = mixed_ref[j % half * shard + t : j % half * shard + t + tile, :]
            parts[j].ref[t : t + tile, :] = dot(rows, w_down[...]).astype(BF16)
        parts[j].send()
    for which, (lefts, rights) in ((2, (mixeds, ogs)), (0, (dgates, normed)), (1, (dups, normed))):
        for j in range(n):
            left = lefts[j // half].ref[j % half * shard : (j % half + 1) * shard, :]
            part = dot_tn(left, rights[j].ref[...])
            if j == 0:
                acc_ref[...] = part
            else:
                acc_ref[...] += part
        at = slice(which * hidden, (which + 1) * hidden)
        for i in range(grads.ref.shape[0]):
            grads.ref[i, at, :] = acc_ref[:, i * lanes : (i + 1) * lanes].astype(BF16)
        grads.send(slice(None), at)


def middle_back_body(n, tile, scalars, near, ins, outs):
    (gain_ref,) = near
    mid_in, og_in, *terms = ins[:-n]
    w_out = ins[-n:]
    gmid_out, ga_out, gain_out, *gctx = outs
    for row in range(0, mid_in.buffer.shape[0], tile):
        at = slice(row, row + tile)
        mid = mid_in.tile(row, tile)
        grad = sum(t.tile(row, tile).astype(F32) for t in terms)
        scale = row_scale(mid)
        normed = mid * scale
        scaled = grad * gain_ref[...]
        back = scale * (scaled - normed * jnp.mean(scaled * normed, axis=-1, keepdims=True))
        total = jnp.sum(grad * normed, axis=0, keepdims=True)
        gain_out.ref[...] = total if row == 0 else gain_out.ref[...] + total
        gmid = og_in.tile(row, tile).astype(F32) + back
        ga = gmid.astype(BF16)
        for w, out in reversed(list(zip(w_out, gctx))):
            out.ref[:, at] = dot_nt(w.ref[...], ga).astype(BF16)
            out.send(slice(None), at)
        ga_out.ref[at, :] = ga
        ga_out.send(at)
        gmid_out.ref[at, :] = gmid
        gmid_out.send(at)


def out_weight_body(n, scalars, near, ins, outs):
    *ctx, ga = ins
    for c, out in reversed(list(zip(ctx, outs))):
        out.ref[...] = dot_tn(c.ref[...], ga.ref[...]).astype(BF16)
        out.send()


def unproject_body(n, tile, scalars, near, ins, outs):
    (me_ref,) = scalars
    w_in, gp_in, *xs = ins
    *gns, gain_out = outs
    shard = xs[0].buffer.shape[0]
    gp_ref, w_ref = gp_in.ref, w_in.ref
    total = 0.0
    for j in reversed(range(n)):
        base = (me_ref[0] ^ j) * shard
        for t in range(0, shard, tile):
            at = pl.ds(pl.multiple_of(base + t, tile), tile)
            grad = dot_tn(gp_ref[:, at], w_ref[...])
            gns[j].ref[t : t + tile, :] = grad.astype(BF16)
            stream = xs[j].ref[t : t + tile, :].astype(F32)
            total = total + jnp.sum(grad * (stream * row_scale(stream)), axis=0, keepdims=True)
        gns[j].send()
    gain_out.ref[...] = total


def qkv_weight_body(n, orders, scalars, near, ins, outs, acc_ref):
    me_ref, dp_ref = scalars
    (gain_ref,) = near
    gp_in, xs, terms = ins[0], ins[1 : 1 + n], ins[1 + n :]
    shard = xs[0].buffer.shape[0]
    lanes = outs[0].ref.shape[2]
    gp_ref = gp_in.ref
    wide = gp_ref.shape[0]
    for j in range(n):
        at = pl.ds(pl.multiple_of((me_ref[0] ^ j) * shard, shard), shard)
        stream = xs[j].ref[...].astype(F32)
        normed = (stream * row_scale(stream) * gain_ref[...]).astype(BF16)
        part = dot(gp_ref[:, at], normed)
        if j == 0:
            acc_ref[:wide, :] = part
        else:
            acc_ref[:wide, :] += part
    acc_ref[wide:, :] = sum(t.ref[...].astype(F32) for t in terms)
    if orders is None:
        for i in range(outs[0].ref.shape[0]):
            outs[0].ref[i] = acc_ref[:, i * lanes : (i + 1) * lanes].astype(BF16)
        return
    rows = acc_ref.shape[0] // 2
    for half, places in enumerate(orders):
        for i, j in reversed(list(enumerate(places))):
            at = pl.ds(pl.multiple_of((dp_ref[0] ^ j) * lanes, 128), lanes)
            out = outs[2 * half + i // (len(places) // 2)]
            out.ref[i % (len(places) // 2)] = acc_ref[half * rows : (half + 1) * rows, at].astype(BF16)
            if i % (len(places) // 2) == 0:
                out.send()


def layer_out_body(tile, scalars, near, ins, outs):
    for row in range(0, ins[0].buffer.shape[0], tile):
        at = slice(row, row + tile)
        outs[0].ref[at, :] = sum(t.tile(row, tile).astype(F32) for t in ins).astype(BF16)
        outs[0].send(at)


def input_back_body(n, tile, scalars, near, ins, outs):
    (me_ref,) = scalars
    (gain_ref,) = near
    x_in, gmid_in, *rest = ins
    terms, dvs = rest[:3], rest[3:]
    if n != 4:
        terms, dvs = rest, []
    for row in range(0, x_in.buffer.shape[0], tile):
        at = slice(row, row + tile)
        stream = x_in.tile(row, tile).astype(F32)
        scale = row_scale(stream)
        normed = stream * scale
        scaled = sum(t.tile(row, tile).astype(F32) for t in terms) * gain_ref[...]
        back = scale * (scaled - normed * jnp.mean(scaled * normed, axis=-1, keepdims=True))
        outs[0].ref[at, :] = gmid_in.tile(row, tile) + back
        outs[0].send(at)
    for j, dv in enumerate(dvs):
        width = dv.buffer.shape[1]
        at = pl.ds(pl.multiple_of((me_ref[0] ^ j) * width, 128), width)
        outs[1].ref[:, at] = dv.ref[...].astype(F32)


def doc_tables(lengths):
    index = jnp.arange(SEQ, dtype=jnp.int32)
    ends = jnp.cumsum(lengths)
    begins = ends - lengths
    starts = jnp.max(jnp.where(begins[:, None] <= index[None, :], begins[:, None], 0), axis=0)
    inverse = jnp.exp(jnp.arange(HALF, dtype=F32) * (-2.0 * math.log(10000.0) / HEAD_DIM))
    angles = (index - starts).astype(F32)[None, :] * inverse[:, None]
    return starts[None, :], jnp.cos(angles), jnp.sin(angles)


def local(
    n,
    n_dp,
    hidden_in,
    first_values,
    doc_lengths,
    out_grad,
    qkv_weight,
    out_weight,
    gate_up_weight,
    down_weight,
    attn_gain,
    mlp_gain,
):
    shard, width = hidden_in.shape[1], qkv_weight.shape[2]
    hidden = down_weight.shape[0]
    lanes = qkv_weight.shape[0]
    dim = hidden_in.shape[2]
    tile = min(256, shard)
    me = lax.axis_index("head").reshape(1).astype(jnp.int32)
    dp = lax.axis_index("dp").reshape(1).astype(jnp.int32)
    x_own, og_own = hidden_in[0], out_grad[0]
    gain_one, gain_two = attn_gain[None, :], mlp_gain[None, :]

    per = shard // tile
    rows = jnp.concatenate(
        [qkv_weight.transpose(1, 2, 0).reshape(3 * width, lanes), out_weight], axis=0
    )
    mlp_rows = jnp.concatenate(
        [gate_up_weight.transpose(1, 2, 0).reshape(2 * hidden, lanes), down_weight], axis=0
    )
    fv_parts = [
        lax.dynamic_slice(first_values[0], (0, (me[0] ^ j) * width), (shard, width))
        for j in range(n)
    ]
    sources = ring_sources(dp[0], n_dp)
    line = n_dp // 2
    ringed = lanes % 128 == 0
    if ringed:
        parts = gather_columns(rows, n_dp)
        xs = gather_relative(x_own, "head", n, lambda *x: [parts[line - 1]])
        fvs = exchange_two(fv_parts, n, [parts[line - 1]])
    else:
        xs = gather_relative(x_own, "head", n)
        fvs = exchange_relative(fv_parts, "head", n)
        parts = [lax.all_gather(rows, "dp", axis=1, tiled=True)]

    starts, cos, sin = doc_tables(doc_lengths[0])

    done = {}

    def project(after=()):
        return far_call(
            functools.partial(project_body, n, tile),
            "project",
            [me, sources],
            [gain_one, cos, sin],
            [*parts, *xs, *fvs],
            [
                (shape((width, SEQ), BF16), n),
                (shape((SEQ, width), BF16), n),
                (shape((width, SEQ), BF16), n),
                (shape((SEQ, width), BF16), n),
                (shape((width, SEQ), BF16), n),
                (shape((3 * width, dim), BF16), 1),
                (shape((width, dim), BF16), 1),
            ],
            flops=6 * SEQ * dim * width,
            after=after,
        )

    def first_stage(held, other):
        done["project"] = project(held[1:2])
        return done["project"][:1]

    def second_stage(held, other):
        q_t, keys, _, _, v_t, *_ = done["project"]
        done["attend"] = attend(
            doc_lengths, me, q_t, keys, v_t, starts, shard, held[2:3] + other[:2]
        )
        return done["attend"][-1:]

    if ringed:
        begin = lambda held, other: [parts[line - 1]]
        stages = [begin] + [lambda held, other: []] * (line - 3) + [first_stage, second_stage]
        mlp_columns = gather_columns(mlp_rows, n_dp, stages)
    else:
        mlp_columns = [lax.all_gather(mlp_rows, "dp", axis=1, tiled=True)]
        done["project"] = project()
        second_stage([], [])
    q_t, keys, k_t, values, v_t, w_qkv, w_out = done["project"]
    *ctx, o_t, lse = done["attend"]

    ctxs = exchange_relative(ctx, "head", n)
    w_outs = gather_relative(w_out, "head", n, lambda *w: [o_t, *mlp_columns[-2:-1]])
    ogs = gather_relative(og_own, "head", n, lambda *g: [o_t])
    middle, normed_two = far_call(
        functools.partial(join_body, n, tile),
        "join",
        [],
        [gain_two],
        [*[(a, per) for a in (*ctxs, x_own)], *w_outs],
        [(shape((shard, dim), F32), per), (shape((shard, dim), BF16), per)],
        flops=2 * shard * dim * dim,
        after=ogs[1:] + (mlp_columns[-1:] if ringed else []),
    )

    half = n // 2
    groups = []

    def mlp(tokens, lo, weights):
        hiddens = [(shape((half * shard, hidden), BF16), half)] * 3
        made = [(shape((3 * hidden, dim), BF16), 1)] if len(weights) > 1 else []
        out = far_call(
            functools.partial(mlp_body, half, tile),
            "mlp",
            [sources],
            [],
            [*weights, *tokens, *ogs[lo : lo + half]],
            hiddens + [(shape((shard, dim), BF16), 1)] * half + made,
            flops=10 * half * shard * dim * hidden,
        )
        groups.append(out)
        return [out[3]]

    if n == 4:
        normed = gather_relative(normed_two, "head", n, lambda *tokens: mlp(tokens, 0, mlp_columns))
    else:
        normed = gather_relative(normed_two, "head", n)
        mlp(normed[:half], 0, mlp_columns)
    w_mlp = groups[0][-1] if ringed else mlp_columns[0]
    mlp(normed[half:], half, [w_mlp])
    gn_two, gn_sent = sum_relative([p for g in groups for p in g[3 : 3 + half]], "head", n)

    *mlp_parts, mlp_grads = far_call(
        functools.partial(mlp_rest_body, n, tile),
        "mlp_rest",
        [],
        [],
        [w_mlp, groups[0][0], groups[1][0], *ogs]
        + [groups[0][1], groups[1][1], *normed, groups[0][2], groups[1][2]],
        [(shape((shard, dim), BF16), 1)] * n + [(shape((n_dp, 3 * hidden, lanes), BF16), 3)],
        [pltpu.VMEM((hidden, dim), F32)],
        flops=8 * SEQ * dim * hidden,
        after=[*gn_sent, gn_two[1]],
    )
    mlp_grads = gate(mlp_grads, gn_two[-1:])
    mlp_grads = lax.psum_scatter(mlp_grads, "dp", scatter_dimension=0, tiled=False).astype(F32)

    grad_middle, ga, gain_two_part, *gctx = far_call(
        functools.partial(middle_back_body, n, tile),
        "middle_back",
        [],
        [gain_two],
        [*[(a, per) for a in (middle, og_own, *gn_two)], *w_outs],
        [
            (shape((shard, dim), F32), per),
            (shape((shard, dim), BF16), per),
            (shape((1, dim), F32), 1),
        ]
        + [(shape((width, shard), BF16), per)] * n,
        flops=2 * shard * dim * dim,
        after=mlp_parts[:1],
    )
    dos = exchange_relative(gctx, "head", n)
    layer_terms, _ = sum_relative(mlp_parts, "head", n, after=dos[2:])
    out_parts = far_call(
        functools.partial(out_weight_body, n),
        "out_weight",
        [],
        [],
        [*ctxs, ga],
        [(shape((width, dim), BF16), 1)] * n,
        flops=2 * shard * dim * dim,
        after=dos[1:2],
    )
    out_terms, out_sent = sum_relative(out_parts, "head", n, after=dos[2:])

    gp_t, *dv = far_call(
        functools.partial(attend_back_body, n, min(256, shard)),
        "attend_back",
        [doc_lengths, me],
        [lse, starts, cos, sin],
        [*dos, o_t, q_t, keys, k_t, values],
        [(shape((3 * width, SEQ), BF16), 3)] + [(shape((shard, width), BF16), 1)] * n,
        [pltpu.VMEM((width, SEQ), F32)] * 3
        + [pltpu.VMEM((width, SEQ), BF16), pltpu.VMEM((width // HEAD_DIM, SEQ), F32)],
        flops=20 * SEQ * SEQ * width,
        after=out_sent,
    )
    dvs = exchange_relative(dv, "head", n)

    *gn_parts, gain_one_part = far_call(
        functools.partial(unproject_body, n, tile),
        "unproject",
        [me],
        [],
        [w_qkv, gp_t, *xs],
        [(shape((shard, dim), BF16), 1)] * n + [(shape((1, dim), F32), 1)],
        flops=6 * SEQ * dim * width,
        after=[layer_terms[-1], out_terms[-1]],
    )
    gn_one, gn_sent = sum_relative(gn_parts, "head", n, first_after=dvs[1:])
    orders = None
    outs = [(shape((n_dp, 4 * width, lanes), BF16), 1)]
    if ringed:
        bit_orders = [bits[::-1] for bits in column_orders(n_dp)]
        orders = [column_places(n_dp, bits) for bits in bit_orders]
        outs = [(shape((n_dp // 2, 2 * width, lanes), BF16), 1)] * 4
    grads = far_call(
        functools.partial(qkv_weight_body, n, orders),
        "qkv_weight",
        [me, dp],
        [gain_one],
        [gp_t, *xs, *out_terms],
        outs,
        [pltpu.VMEM((4 * width, dim), F32)],
        flops=6 * SEQ * dim * width,
        after=gn_sent,
    )
    (layer_out,) = far_call(
        functools.partial(layer_out_body, tile),
        "layer_out",
        [],
        [],
        [(a, per) for a in (middle, *layer_terms)],
        [(shape((shard, dim), BF16), per)],
        after=grads[:1],
    )
    gains = gate(jnp.concatenate([gain_one_part, gain_two_part], axis=0), gn_one[-1:])
    gains = sum_everywhere(gains, [("dp", n_dp), ("head", n)])
    if ringed:
        held = [
            (grads[2 * i], swap(grads[2 * i + 1], "dp", n_dp, bits[0]))
            for i, bits in enumerate(bit_orders)
        ]
        for step in range(1, len(bit_orders[0])):
            hold = gn_one[-1:] if step == 1 else []
            held = [
                scatter_step(*h, n_dp, bits[step], hold) for h, bits in zip(held, bit_orders)
            ]
        grads = jnp.concatenate([(k + r.astype(F32))[0] for k, r in held], axis=0)
    else:
        grads = lax.psum_scatter(grads[0], "dp", scatter_dimension=0, tiled=False).astype(F32)

    back_outs = [(shape((shard, dim), F32), per)]
    if n == 4:
        back_outs.append((shape((shard, dim), F32), 1))
    input_grad, *first_grad = far_call(
        functools.partial(input_back_body, n, tile),
        "input_back",
        [me],
        [gain_one],
        [*[(a, per) for a in (x_own, grad_middle, *gn_one)], *(dvs if n == 4 else [])],
        back_outs,
        after=[layer_out],
    )
    if not first_grad:
        stacked = jnp.stack(dvs)
        placed = [
            lax.dynamic_index_in_dim(stacked, me[0] ^ i, keepdims=False) for i in range(n)
        ]
        first_grad = [jnp.concatenate(placed, axis=1).astype(F32)]
    return (
        layer_out[None],
        input_grad[None],
        first_grad[0][None],
        grads[: 3 * width].reshape(3, width, lanes).transpose(2, 0, 1),
        grads[3 * width :],
        mlp_grads[: 2 * hidden].reshape(2, hidden, lanes).transpose(2, 0, 1),
        mlp_grads[2 * hidden :],
        gains[0],
        gains[1],
    )


def solution(mesh):
    tokens = P("dp", "head", None)
    columns = P("dp", None, "head")
    rows = P("head", "dp")
    return jax.shard_map(
        functools.partial(local, mesh.shape["head"], mesh.shape["dp"]),
        mesh=mesh,
        in_specs=(tokens, tokens, P("dp", None), tokens, columns, rows, columns, rows, P(), P()),
        out_specs=(tokens, tokens, tokens, columns, rows, columns, rows, P(), P()),
        check_vma=False,
    )
```

time: 407 us -> 373 us (0.916)
  local copies, waits for them, and re-layouts: 26.2 us -> 12.9 us
  waiting for transfers between devices: 116 us -> 107 us
  Pallas kernels: 181 us -> 173 us
  starting transfers between devices: 50.5 us -> 46.3 us
    unnamed x118 -> x52, local copies, waits for them, and re-layouts: 17 us -> 3.97 us
    pallas_call x15 -> x16, Pallas kernels: 160 us -> 152 us  [far_call(): pl.pallas_call(kernel, name=name, out_shape=[o for o, _ in outs], in_spec...]
    ppermute x55, waiting for transfers between devices: 101 us -> 93.1 us  [swap(): return lax.ppermute(value, axis, [(i, i ^ bit) for i in range(size)])]
  transfers between devices with their start and end apart: 62 -> 62, of which waited for: 30 -> 31; matrix products, arithmetic and copies ran while one was open for 5% -> 4% of each run, Pallas kernels for 39% -> 41%
where the time goes in v3:
time: 373 us; the launch traced here: 366 us
  Pallas kernels  173 us (46%)
  waiting for transfers between devices  107 us (29%)
  starting transfers between devices  46.3 us (12%)
  between operations  14.9 us (4%)
  local copies, waits for them, and re-layouts  12.9 us (3%)
  other arithmetic  11.9 us (3%)
    pallas_call x16, Pallas kernels, far_call(): pl.pallas_call(kernel, name=name, out_shape=[o for o, _ in outs], in_spec...  152 us
    ppermute x55, waiting for transfers between devices, swap(): return lax.ppermute(value, axis, [(i, i ^ bit) for i in range(size)])  93.1 us
    ppermute x55, starting transfers between devices, swap(): return lax.ppermute(value, axis, [(i, i ^ bit) for i in range(size)])  36.9 us
    pallas_call x1, Pallas kernels, attend(): pl.pallas_call(functools.partial(attend_kernel, bq, per, heads, len(after...  20.7 us
    ppermute x6, waiting for transfers between devices, ring_step(): return lax.ppermute(value, 'dp', pairs)  14 us
    ppermute x6, starting transfers between devices, ring_step(): return lax.ppermute(value, 'dp', pairs)  9.43 us
  transfers between devices with their start and end apart: 62, of which 31 were waited for; matrix products, arithmetic and copies ran while one was open for 4% of the time, Pallas kernels for 41%

profile of v3, /device:TPU:0, one launch (start us, length us, event | category | flops | bytes accessed | tf_op | source)
XLA Modules:
  0.0 365.8 jit_solution(9647440426661200464)
XLA Ops:
  7.2 1.2 copy.45
  9.3 3.0 collective-permute-start.1
  12.3 1.6 collective-permute-start
  13.9 1.5 collective-permute-start.8
  15.4 3.2 collective-permute-done.1.refs_1_.refs_9_
  18.6 2.4 collective-permute-done.refs_0_
  22.2 1.2 collective-permute-start.2
  24.2 1.6 collective-permute-start.11
  25.8 2.9 collective-permute-done.3.refs_1_.refs_10_
  28.7 1.5 collective-permute-done.2.refs_0_
  30.3 1.2 collective-permute-start.5
  31.5 1.8 pad_maximum_fusion.refs_0_
  34.3 2.5 collective-permute-done.5.refs_1_.refs_11_
  37.0 4.0 %collective-permute-done.4.refs_0_ = bf16[1024,128]{1,0:T(8,128)(2,1)S(1)} collective-permute-done((bf16[1024,128]{1,0:T(8,128)(2,1)}, bf16[1024,128]{1,0:T(8,128)(2,1)S(1)}, u32[]{:S(2)}, u32[]{:S(2)}) %collective-permute-start.4) | collective-permute-done | bytes 262176 | tf_op jit(solution)/shard_map/ppermute | solution.py:227
  42.6 7.1 %collective-permute-done.11.refs_0_ = bf16[512,512]{1,0:T(8,128)(2,1)S(1)} collective-permute-done((bf16[512,512]{1,0:T(8,128)(2,1)S(1)}, bf16[512,512]{1,0:T(8,128)(2,1)S(1)}, u32[]{:S(2)}, u32[]{:S(2)}) %collective-permute-start.11) | collective-permute-done | bytes 524320 | tf_op jit(solution)/shard_map/ppermute | solution.py:140
  49.6 2.6 collective-permute-start.13
  55.2 1.6 collective-permute-start.25
  57.4 6.0 %collective-permute-done.13.refs_21_.refs_2_ = bf16[2112,128]{1,0:T(8,128)(2,1)} collective-permute-done((bf16[2112,128]{1,0:T(8,128)(2,1)}, bf16[2112,128]{1,0:T(8,128)(2,1)}, u32[]{:S(2)}, u32[]{:S(2)}) %collective-permute-start.13) | collective-permute-done | bytes 540704 | tf_op jit(solution)/shard_map/ppermute | solution.py:227
  63.9 1.7 collective-permute-start.14
  65.6 1.8 multiply_sine_fusion
  67.5 10.8 %project.1 = (bf16[256,2048]{1,0:T(8,128)(2,1)}, bf16[2048,256]{1,0:T(8,128)(2,1)}, bf16[256,2048]{1,0:T(8,128)(2,1)}, bf16[2048,256]{1,0:T(8,128)(2,1)}, bf16[2...) custom-call(s32[1]{0:T(128)} %bitcast.1.refs_0_.me_ref.refs_1_, ...), custom_call_target="tpu_custom_call" | custom-call | flops 3221225472 | bytes 1 | tf_op jit(solution)/shard_map/project/pallas_call | solution.py:107
  78.3 1.6 collective-permute-start.27
  79.9 1.5 collective-permute-start.22
  81.4 1.6 collective-permute-done.16.refs_2_.refs_6_
  84.0 20.7 %attend.1 = (bf16[512,256]{1,0:T(8,128)(2,1)}, bf16[512,256]{1,0:T(8,128)(2,1)}, bf16[512,256]{1,0:T(8,128)(2,1)}, bf16[512,256]{1,0:T(8,128)(2,1)}, bf16[256,2048]{1,0:T(8,128)(2,1)}, /*index=5*/f32[4,2048]{1,0:T(4,128)}) custom-call(s32[1,16]{1,0:T(1,128)} %refs_0_.1, s32[1]{0:T(128)} %bitcast.1.refs_0_.me_ref.refs_1_, ...), custom_call_target="tpu_custom_call" | custom-call | flops 3221225472 | bytes 1 | tf_op jit(solution)/shard_map/attend/pallas_call | solution.py:392
  108.1 6.7 %collective-permute-done.18.refs_3_.refs_2_ = bf16[512,256]{1,0:T(8,128)(2,1)} collective-permute-done((bf16[512,256]{1,0:T(8,128)(2,1)S(1)}, bf16[512,256]{1,0:T(8,128)(2,1)}, u32[]{:S(2)}, u32[]{:S(2)}) %collective-permute-start.18) | collective-permute-done | bytes 262176 | tf_op jit(solution)/shard_map/ppermute | solution.py:140
  114.7 8.2 %collective-permute-done.19.refs_4_.refs_3_ = bf16[512,256]{1,0:T(8,128)(2,1)} collective-permute-done((bf16[512,256]{1,0:T(8,128)(2,1)S(1)}, bf16[512,256]{1,0:T(8,128)(2,1)}, u32[]{:S(2)}, u32[]{:S(2)}) %collective-permute-start.19) | collective-permute-done | bytes 262176 | tf_op jit(solution)/shard_map/ppermute | solution.py:140
  123.0 5.4 %join.1 = (f32[512,1024]{1,0:T(8,128)}, bf16[512,1024]{1,0:T(8,128)(2,1)}) custom-call(f32[1,1024]{1,0:T(1,128)} %bitcast.67, bf16[512,256]{1,0:T(8,128)(2,1)} %get-tuple-element.70.refs_1_.refs_0_, bf16[512,256]{1,0:T(8,128)(2,1)} %collective-permute-done.17.refs_2_.refs_1_, bf16[512,256]{1,0:T(8,128)(2,1)} %collective-permute-done.18.refs_3_.refs_2_, ...), custom_call_target="tpu_custom_call" | custom-call | flops 3221225472 | bytes 1 | tf_op jit(solution)/shard_map/join/pallas_call | solution.py:107
  129.7 1.9 collective-permute-done.29.refs_10_
  131.5 17.3 %mlp.2 = (bf16[1024,704]{1,0:T(8,128)(2,1)}, bf16[1024,704]{1,0:T(8,128)(2,1)}, bf16[1024,704]{1,0:T(8,128)(2,1)}, bf16[512,1024]{1,0:T(8,128)(2,1)}, bf16[512,1...) custom-call(s32[8]{0:T(128)} %stack.35.refs_1_.refs_0_, bf16[2112,128]{1,0:T(8,128)(2,1)} %gate.24.refs_1_, ...), custom_call_target="tpu_custom_call" | custom-call | flops 3221225472 | bytes 1 | tf_op jit(solution)/shard_map/mlp/pallas_call | solution.py:107
  148.8 5.6 %collective-permute-done.30.refs_0_ = bf16[512,1024]{1,0:T(8,128)(2,1)} collective-permute-done((bf16[512,1024]{1,0:T(8,128)(2,1)}, bf16[512,1024]{1,0:T(8,128)(2,1)}, u32[]{:S(2)}, u32[]{:S(2)}) %collective-permute-start.30) | collective-permute-done | bytes 1048608 | tf_op jit(solution)/shard_map/ppermute | solution.py:140
  154.4 3.0 collective-permute-done.31.refs_3_.refs_12_
  157.4 17.6 %mlp.3 = (bf16[1024,704]{1,0:T(8,128)(2,1)}, bf16[1024,704]{1,0:T(8,128)(2,1)}, bf16[1024,704]{1,0:T(8,128)(2,1)}, bf16[512,1024]{1,0:T(8,128)(2,1)}, bf16[512,1024]{1,0:T(8,128)(2,1)}) custom-call(s32[8]{0:T(128)} %stack.35.refs_1_.refs_0_, bf16[2112,1024]{1,0:T(8,128)(2,1)} %get-tuple-element.79.refs_1_.refs_0_, bf16[512,1024]{1,0:T(8,128)(2,1)} %gate.29.refs_2_.refs_11_, ...), custom_call_target="tpu_custom_call" | custom-call | flops 3221225472 | bytes 1 | tf_op jit(solution)/shard_map/mlp/pallas_call | solution.py:107
  175.6 2.5 collective-permute-done.32.refs_1_
  178.1 2.4 fold.4.refs_15_
  181.6 19.4 %mlp_rest.1 = (bf16[512,1024]{1,0:T(8,128)(2,1)}, bf16[512,1024]{1,0:T(8,128)(2,1)}, bf16[512,1024]{1,0:T(8,128)(2,1)}, bf16[512,1024]{1,0:T(8,128)(2,1)}, bf16[8,2112,128]{2,1,0:T(8,128)(2,1)}) custom-call(bf16[2112,1024]{1,0:T(8,128)(2,1)} %get-tuple-element.79.refs_1_.refs_0_, bf16[1024,704]{1,0:T(8,128)(2,1)} %get-tuple-element.80.refs_1_, ...), custom_call_target="tpu_custom_call" | custom-call | flops 3221225472 | bytes 1 | tf_op jit(solution)/shard_map/mlp_rest/pallas_call | solution.py:107
  201.0 5.1 %collective-permute-done.36.refs_5_.refs_1_ = bf16[512,1024]{1,0:T(8,128)(2,1)} collective-permute-done((bf16[512,1024]{1,0:T(8,128)(2,1)}, bf16[512,1024]{1,0:T(8,128)(2,1)}, u32[]{:S(2)}, u32[]{:S(2)}) %collective-permute-start.36) | collective-permute-done | bytes 1048608 | tf_op jit(solution)/shard_map/ppermute | solution.py:140
  206.1 8.0 %middle_back.1 = (f32[512,1024]{1,0:T(8,128)}, bf16[512,1024]{1,0:T(8,128)(2,1)}, f32[1,1024]{1,0:T(1,128)}, bf16[256,512]{1,0:T(8,128)(2,1)}, bf16[256,512]{1,0...) custom-call(f32[1,1024]{1,0:T(1,128)} %bitcast.68, f32[512,1024]{1,0:T(8,128)} %get-tuple-element.77.refs_1_.refs_0_, ...), custom_call_target="tpu_custom_call" | custom-call | flops 3221225472 | bytes 1 | tf_op jit(solution)/shard_map/middle_back/pallas_call | solution.py:107
  216.2 4.3 %out_weight.1 = (bf16[256,1024]{1,0:T(8,128)(2,1)}, bf16[256,1024]{1,0:T(8,128)(2,1)}, bf16[256,1024]{1,0:T(8,128)(2,1)}, bf16[256,1024]{1,0:T(8,128)(2,1)}) custom-call(bf16[512,256]{1,0:T(8,128)(2,1)} %get-tuple-element.70.refs_1_.refs_0_, bf16[512,256]{1,0:T(8,128)(2,1)} %collective-permute-done.17.refs_2_.refs_1_, ...), custom_call_target="tpu_custom_call" | custom-call | flops 3221225472 | bytes 1 | tf_op jit(solution)/shard_map/out_weight/pallas_call | solution.py:107
  221.2 2.4 fold.5.refs_0_
  224.2 3.9 %collective-permute-done.38.refs_2_.refs_9_ = bf16[256,512]{1,0:T(8,128)(2,1)} collective-permute-done((bf16[256,512]{1,0:T(8,128)(2,1)}, bf16[256,512]{1,0:T(8,128)(2,1)}, u32[]{:S(2)}, u32[]{:S(2)}) %collective-permute-start.38) | collective-permute-done | bytes 262176 | tf_op jit(solution)/shard_map/ppermute | solution.py:140
  229.1 2.0 fold.6.refs_0_
  232.2 30.9 %attend_back.1 = (bf16[768,2048]{1,0:T(8,128)(2,1)}, bf16[512,256]{1,0:T(8,128)(2,1)}, bf16[512,256]{1,0:T(8,128)(2,1)}, bf16[512,256]{1,0:T(8,128)(2,1)}, bf16[512,256]{1,0:T(8,128)(2,1)}) custom-call(s32[1,16]{1,0:T(1,128)} %refs_0_.1, s32[1]{0:T(128)} %bitcast.1.refs_0_.me_ref.refs_1_, f32[4,2048]{1,0:T(4,128)} %get-tuple-element.76.refs_1_.refs_2_, ...), custom_call_target="tpu_custom_call" | custom-call | flops 3221225472 | bytes 1 | tf_op jit(solution)/shard_map/attend_back/pallas_call | solution.py:107
  265.6 9.7 %unproject.1 = (bf16[512,1024]{1,0:T(8,128)(2,1)}, bf16[512,1024]{1,0:T(8,128)(2,1)}, bf16[512,1024]{1,0:T(8,128)(2,1)}, bf16[512,1024]{1,0:T(8,128)(2,1)}, f32[1,1024]{1,0:T(1,128)}) custom-call(s32[1]{0:T(128)} %bitcast.1.refs_0_.me_ref.refs_1_, bf16[768,1024]{1,0:T(8,128)(2,1)} %get-tuple-element.106.refs_1_, ...), custom_call_target="tpu_custom_call" | custom-call | flops 3221225472 | bytes 1 | tf_op jit(solution)/shard_map/unproject/pallas_call | solution.py:107
  275.3 1.6 collective-permute-done.46.refs_3_.refs_10_
  277.9 2.6 collective-permute-done.47.refs_1_
  280.5 2.4 fold.7.refs_11_
  282.9 1.2 collective-permute-start.49
  284.6 3.2 collective-permute-done.42.refs_9_
  287.8 10.1 %qkv_weight.1 = (bf16[4,512,128]{2,1,0:T(8,128)(2,1)}, bf16[4,512,128]{2,1,0:T(8,128)(2,1)}, bf16[4,512,128]{2,1,0:T(8,128)(2,1)}, bf16[4,512,128]{2,1,0:T(8,128)(2,1)}) custom-call(s32[1]{0:T(128)} %bitcast.1.refs_0_.me_ref.refs_1_, s32[1]{0:T(128)} %bitcast.24.refs_1_, f32[1,1024]{1,0:T(1,128)} %bitcast.70, ...), custom_call_target="tpu_custom_call" | custom-call | flops 3221225472 | bytes 1 | tf_op jit(solution)/shard_map/qkv_weight/pallas_call | solution.py:107
  297.9 1.6 collective-permute-start.50
  300.1 8.6 %collective-permute-done.49.refs_6_.refs_1_ = bf16[512,1024]{1,0:T(8,128)(2,1)} collective-permute-done((bf16[512,1024]{1,0:T(8,128)(2,1)}, bf16[512,1024]{1,0:T(8,128)(2,1)}, u32[]{:S(2)}, u32[]{:S(2)}) %collective-permute-start.49) | collective-permute-done | bytes 1048608 | tf_op jit(solution)/shard_map/ppermute | solution.py:140
  308.7 1.5 collective-permute-start.56
  311.3 1.3 collective-permute-done.56
  314.2 3.5 layer_out.1.refs_11_
  317.7 6.1 %collective-permute-done.57 = f32[2,1024]{1,0:T(2,128)S(1)} collective-permute-done((f32[2,1024]{1,0:T(2,128)S(1)}, f32[2,1024]{1,0:T(2,128)S(1)}, u32[]{:S(2)}, u32[]{:S(2)}) %collective-permute-start.57) | collective-permute-done | bytes 8224 | tf_op jit(solution)/shard_map/ppermute | solution.py:140
  324.3 1.3 convert_add_fusion.1
  325.7 2.6 collective-permute-done.58
  333.5 6.0 %input_back.1 = (f32[512,1024]{1,0:T(8,128)}, f32[512,1024]{1,0:T(8,128)}) custom-call(s32[1]{0:T(128)} %bitcast.1.refs_0_.me_ref.refs_1_, f32[1,1024]{1,0:T(1,128)} %bitcast.71, bf16[512,1024]{1,0:T(8,128)(2,1)} %bitcast.66, f32[512,1024]{1,0:T(8,128)} %get-tuple-element.113.refs_3_, bf16[512,1024]{1,0:T(8,128)(2,1)} %get-tuple-element.114.refs_4_, ...), custom_call_target="tpu_custom_call" | custom-call | flops 3221225472 | bytes 1 | tf_op jit(solution)/shard_map/input_back/pallas_call | solution.py:107
  340.2 4.2 %collective-permute-done.51 = bf16[2,512,128]{2,1,0:T(8,128)(2,1)} collective-permute-done((bf16[2,512,128]{2,1,0:T(8,128)(2,1)}, bf16[2,512,128]{2,1,0:T(8,128)(2,1)}, u32[]{:S(2)}, u32[]{:S(2)}) %collective-permute-start.51) | collective-permute-done | bytes 262176 | tf_op jit(solution)/shard_map/ppermute | solution.py:140
  344.4 1.2 slice_add_fusion.1
  346.1 1.6 collective-permute-done.54
  349.1 5.0 %collective-permute-done.52 = bf16[1,512,128]{2,1,0:T(8,128)(2,1)S(1)} collective-permute-done((bf16[1,512,128]{2,1,0:T(8,128)(2,1)S(1)}, bf16[1,512,128]{2,1,0:T(8,128)(2,1)S(1)}, u32[]{:S(2)}, u32[]{:S(2)}) %collective-permute-start.52) | collective-permute-done | bytes 131104 | tf_op jit(solution)/shard_map/ppermute | solution.py:140
  355.9 1.2 convert_element_type.48
  (187 shorter events, 41.6 us)
Async XLA Ops:
  7.2 16.2 %copy-start.7 = (bf16[1,512,1024]{2,1,0:T(8,128)(2,1)S(1)}, bf16[1,512,1024]{2,1,0:T(8,128)(2,1)}, u32[]{:S(2)}) copy-start(bf16[1,512,1024]{2,1,0:T(8,128)(2,1)} %param.11) | copy-start | bytes 3145732
  7.2 348.7 %reduce-scatter.2.cloned.1.call-start = ((), (), s32[]{:S(2)}) async-start(), calls=%async_computation.1 | async-start | bytes 4866048 | tf_op jit(solution)/shard_map/reduce_scatter | solution.py:845
  9.3 9.3 %collective-permute-start.1 = (bf16[1024,128]{1,0:T(8,128)(2,1)S(1)}, bf16[1024,128]{1,0:T(8,128)(2,1)S(1)}, u32[]{:S(2)}, u32[]{:S(2)}) collective-permute-start(bf16[1024,128]{1,0:T(8,128)(2,1)S(1)} %pad_maximum_fusion.3.refs_5_), channel_id=1, source_target_pairs={{0,4},{4,0},{8,12},{12,8},{16,20},{20,16},{24,28},{28,24},{1,5},{5... | collective-permute-start | bytes 786440 | tf_op jit(solution)/shard_map/ppermute | solution.py:140
  12.3 8.7 %collective-permute-start = (bf16[1024,128]{1,0:T(8,128)(2,1)S(1)}, bf16[1024,128]{1,0:T(8,128)(2,1)S(1)}, u32[]{:S(2)}, u32[]{:S(2)}) collective-permute-start(bf16[1024,128]{1,0:T(8,128)(2,1)S(1)} %pad_maximum_fusion.3.refs_5_), channel_id=1, source_target_pairs={{0,8},{4,12},{8,24},{12,28},{24,16},{28,20},{16,0},{20,4},{1,9},{5... | collective-permute-start | bytes 786440 | tf_op jit(solution)/shard_map/ppermute | solution.py:227
  13.9 38.4 %collective-permute-start.8 = (bf16[512,1024]{1,0:T(8,128)(2,1)}, bf16[512,1024]{1,0:T(8,128)(2,1)S(1)}, u32[]{:S(2)}, u32[]{:S(2)}) collective-permute-start(bf16[512,1024]{1,0:T(8,128)(2,1)} %bitcast.60), channel_id=1, source_target_pairs={{0,2},{1,3},{2,0},{3,1},{4,6},{5,7},{6,4},{7,5},{8,10},{9,11},{10,... | collective-permute-start | bytes 3145736 | tf_op jit(solution)/shard_map/ppermute | solution.py:140
  15.4 48.5 %collective-permute-start.7 = (bf16[512,1024]{1,0:T(8,128)(2,1)}, bf16[512,1024]{1,0:T(8,128)(2,1)}, u32[]{:S(2)}, u32[]{:S(2)}) collective-permute-start(bf16[512,1024]{1,0:T(8,128)(2,1)} %bitcast.61), channel_id=1, source_target_pairs={{0,1},{1,0},{2,3},{3,2},{4,5},{5,4},{6,7},{7,6},{8,9},{9,8},{10,11... | collective-permute-start | bytes 3145736 | tf_op jit(solution)/shard_map/ppermute | solution.py:140
  21.7 7.1 %collective-permute-start.3 = (bf16[1024,128]{1,0:T(8,128)(2,1)}, bf16[1024,128]{1,0:T(8,128)(2,1)S(1)}, u32[]{:S(2)}, u32[]{:S(2)}) collective-permute-start(bf16[1024,128]{1,0:T(8,128)(2,1)} %gate.19.refs_6_), channel_id=1, source_target_pairs={{0,4},{4,0},{8,12},{12,8},{16,20},{20,16},{24,28},{28,24},{1,5},{5... | collective-permute-start | bytes 786440 | tf_op jit(solution)/shard_map/ppermute | solution.py:140
  22.2 8.1 %collective-permute-start.2 = (bf16[1024,128]{1,0:T(8,128)(2,1)}, bf16[1024,128]{1,0:T(8,128)(2,1)}, u32[]{:S(2)}, u32[]{:S(2)}) collective-permute-start(bf16[1024,128]{1,0:T(8,128)(2,1)} %gate.19.refs_6_), channel_id=1, source_target_pairs={{0,8},{4,12},{8,24},{12,28},{24,16},{28,20},{16,0},{20,4},{1,9},{5... | collective-permute-start | bytes 786440 | tf_op jit(solution)/shard_map/ppermute | solution.py:227
  24.2 25.4 %collective-permute-start.11 = (bf16[512,512]{1,0:T(8,128)(2,1)S(1)}, bf16[512,512]{1,0:T(8,128)(2,1)S(1)}, u32[]{:S(2)}, u32[]{:S(2)}) collective-permute-start(bf16[512,512]{1,0:T(8,128)(2,1)S(1)} %pad_maximum_fusion.1), channel_id=1, source_target_pairs={{0,2},{1,3},{2,0},{3,1},{4,6},{5,7},{6,4},{7,5},{8,10},{9,11},{10,... | collective-permute-start | bytes 1572872 | tf_op jit(solution)/shard_map/ppermute | solution.py:140
  30.3 6.6 %collective-permute-start.5 = (bf16[1024,128]{1,0:T(8,128)(2,1)}, bf16[1024,128]{1,0:T(8,128)(2,1)S(1)}, u32[]{:S(2)}, u32[]{:S(2)}) collective-permute-start(bf16[1024,128]{1,0:T(8,128)(2,1)} %gate.20.refs_7_), channel_id=1, source_target_pairs={{0,4},{4,0},{8,12},{12,8},{16,20},{20,16},{24,28},{28,24},{1,5},{5... | collective-permute-start | bytes 786440 | tf_op jit(solution)/shard_map/ppermute | solution.py:140
  33.5 7.5 %collective-permute-start.4 = (bf16[1024,128]{1,0:T(8,128)(2,1)}, bf16[1024,128]{1,0:T(8,128)(2,1)S(1)}, u32[]{:S(2)}, u32[]{:S(2)}) collective-permute-start(bf16[1024,128]{1,0:T(8,128)(2,1)} %gate.20.refs_7_), channel_id=1, source_target_pairs={{0,8},{4,12},{8,24},{12,28},{24,16},{28,20},{16,0},{20,4},{1,9},{5... | collective-permute-start | bytes 786440 | tf_op jit(solution)/shard_map/ppermute | solution.py:227
  36.9 17.5 %collective-permute-start.10 = (bf16[512,256]{1,0:T(8,128)(2,1)S(1)}, bf16[512,256]{1,0:T(8,128)(2,1)S(1)}, u32[]{:S(2)}, u32[]{:S(2)}) collective-permute-start(bf16[512,256]{1,0:T(8,128)(2,1)S(1)} %get-tuple-element.126), channel_id=1, source_target_pairs={{0,1},{1,0},{2,3},{3,2},{4,5},{5,4},{6,7},{7,6},{8,9},{9,8},{10,11... | collective-permute-start | bytes 786440 | tf_op jit(solution)/shard_map/ppermute | solution.py:140
  37.0 41.3 %copy-start.16 = (s32[2048]{0:T(1024)}, s32[2048]{0:T(1024)S(1)}, u32[]{:S(2)}) copy-start(s32[2048]{0:T(1024)S(1)} %select_reduce_fusion) | copy-start | bytes 24580
  41.7 13.5 %collective-permute-start.6 = (bf16[1024,128]{1,0:T(8,128)(2,1)}, bf16[1024,128]{1,0:T(8,128)(2,1)S(1)}, u32[]{:S(2)}, u32[]{:S(2)}) collective-permute-start(bf16[1024,128]{1,0:T(8,128)(2,1)} %gate.21.refs_1_.refs_8_), channel_id=1, source_target_pairs={{0,4},{4,0},{8,12},{12,8},{16,20},{20,16},{24,28},{28,24},{1,5},{5... | collective-permute-start | bytes 786440 | tf_op jit(solution)/shard_map/ppermute | solution.py:140
  49.6 13.7 %collective-permute-start.13 = (bf16[2112,128]{1,0:T(8,128)(2,1)}, bf16[2112,128]{1,0:T(8,128)(2,1)}, u32[]{:S(2)}, u32[]{:S(2)}) collective-permute-start(bf16[2112,128]{1,0:T(8,128)(2,1)} %gate.24.refs_1_), channel_id=1, source_target_pairs={{0,8},{4,12},{8,24},{12,28},{24,16},{28,20},{16,0},{20,4},{1,9},{5... | collective-permute-start | bytes 1622024 | tf_op jit(solution)/shard_map/ppermute | solution.py:227
  53.2 14.2 %collective-permute-start.9 = (bf16[512,1024]{1,0:T(8,128)(2,1)}, bf16[512,1024]{1,0:T(8,128)(2,1)}, u32[]{:S(2)}, u32[]{:S(2)}) collective-permute-start(bf16[512,1024]{1,0:T(8,128)(2,1)} %gate.22.refs_15_.refs_5_.refs_6_), channel_id=1, source_target_pairs={{0,1},{1,0},{2,3},{3,2},{4,5},{5,4},{6,7},{7,6},{8,9},{9,8},{10,11... | collective-permute-start | bytes 3145736 | tf_op jit(solution)/shard_map/ppermute | solution.py:140
  54.4 2.5 collective-permute-start.12
  55.2 49.5 %collective-permute-start.25 = (bf16[512,1024]{1,0:T(8,128)(2,1)}, bf16[512,1024]{1,0:T(8,128)(2,1)}, u32[]{:S(2)}, u32[]{:S(2)}) collective-permute-start(bf16[512,1024]{1,0:T(8,128)(2,1)} %bitcast.23.refs_11_.refs_3_.refs_2_), channel_id=1, source_target_pairs={{0,2},{1,3},{2,0},{3,1},{4,6},{5,7},{6,4},{7,5},{8,10},{9,11},{10,... | collective-permute-start | bytes 3145736 | tf_op jit(solution)/shard_map/ppermute | solution.py:140
  56.8 23.1 %collective-permute-start.15 = (bf16[2112,128]{1,0:T(8,128)(2,1)}, bf16[2112,128]{1,0:T(8,128)(2,1)}, u32[]{:S(2)}, u32[]{:S(2)}) collective-permute-start(bf16[2112,128]{1,0:T(8,128)(2,1)} %gate.24.refs_1_), channel_id=1, source_target_pairs={{0,4},{4,0},{8,12},{12,8},{16,20},{20,16},{24,28},{28,24},{1,5},{5... | collective-permute-start | bytes 1622024 | tf_op jit(solution)/shard_map/ppermute | solution.py:140
  63.4 19.6 %collective-permute-start.16 = (bf16[2112,128]{1,0:T(8,128)(2,1)}, bf16[2112,128]{1,0:T(8,128)(2,1)}, u32[]{:S(2)}, u32[]{:S(2)}) collective-permute-start(bf16[2112,128]{1,0:T(8,128)(2,1)} %collective-permute-done.13.refs_21_.refs_2_), channel_id=1, source_target_pairs={{0,4},{4,0},{8,12},{12,8},{16,20},{20,16},{24,28},{28,24},{1,5},{5... | collective-permute-start | bytes 1622024 | tf_op jit(solution)/shard_map/ppermute | solution.py:140
  63.9 14.4 %collective-permute-start.14 = (bf16[2112,128]{1,0:T(8,128)(2,1)}, bf16[2112,128]{1,0:T(8,128)(2,1)}, u32[]{:S(2)}, u32[]{:S(2)}) collective-permute-start(bf16[2112,128]{1,0:T(8,128)(2,1)} %collective-permute-done.13.refs_21_.refs_2_), channel_id=1, source_target_pairs={{0,8},{4,12},{8,24},{12,28},{24,16},{28,20},{16,0},{20,4},{1,9},{5... | collective-permute-start | bytes 1622024 | tf_op jit(solution)/shard_map/ppermute | solution.py:227
  67.4 39.8 %collective-permute-start.24 = (bf16[512,1024]{1,0:T(8,128)(2,1)}, bf16[512,1024]{1,0:T(8,128)(2,1)}, u32[]{:S(2)}, u32[]{:S(2)}) collective-permute-start(bf16[512,1024]{1,0:T(8,128)(2,1)} %bitcast.23.refs_11_.refs_3_.refs_2_), channel_id=1, source_target_pairs={{0,1},{1,0},{2,3},{3,2},{4,5},{5,4},{6,7},{7,6},{8,9},{9,8},{10,11... | collective-permute-start | bytes 3145736 | tf_op jit(solution)/shard_map/ppermute | solution.py:140
  78.3 26.5 %collective-permute-start.27 = (bf16[2112,128]{1,0:T(8,128)(2,1)}, bf16[2112,128]{1,0:T(8,128)(2,1)}, u32[]{:S(2)}, u32[]{:S(2)}) collective-permute-start(bf16[2112,128]{1,0:T(8,128)(2,1)} %gate.25.refs_0_.refs_3_), channel_id=1, source_target_pairs={{0,8},{4,12},{8,24},{12,28},{24,16},{28,20},{16,0},{20,4},{1,9},{5... | collective-permute-start | bytes 1622024 | tf_op jit(solution)/shard_map/ppermute | solution.py:227
  79.9 26.4 %collective-permute-start.22 = (bf16[2112,128]{1,0:T(8,128)(2,1)}, bf16[2112,128]{1,0:T(8,128)(2,1)}, u32[]{:S(2)}, u32[]{:S(2)}) collective-permute-start(bf16[2112,128]{1,0:T(8,128)(2,1)} %gate.25.refs_0_.refs_3_), channel_id=1, source_target_pairs={{0,4},{4,0},{8,12},{12,8},{16,20},{20,16},{24,28},{28,24},{1,5},{5... | collective-permute-start | bytes 1622024 | tf_op jit(solution)/shard_map/ppermute | solution.py:140
  82.9 22.7 %collective-permute-start.21 = (bf16[256,1024]{1,0:T(8,128)(2,1)}, bf16[256,1024]{1,0:T(8,128)(2,1)}, u32[]{:S(2)}, u32[]{:S(2)}) collective-permute-start(bf16[256,1024]{1,0:T(8,128)(2,1)} %get-tuple-element.74.refs_6_), channel_id=1, source_target_pairs={{0,2},{1,3},{2,0},{3,1},{4,6},{5,7},{6,4},{7,5},{8,10},{9,11},{10,... | collective-permute-start | bytes 1572872 | tf_op jit(solution)/shard_map/ppermute | solution.py:140
  104.7 18.3 %collective-permute-start.26 = (bf16[512,1024]{1,0:T(8,128)(2,1)}, bf16[512,1024]{1,0:T(8,128)(2,1)}, u32[]{:S(2)}, u32[]{:S(2)}) collective-permute-start(bf16[512,1024]{1,0:T(8,128)(2,1)} %gate.27.refs_11_.refs_4_.refs_5_), channel_id=1, source_target_pairs={{0,1},{1,0},{2,3},{3,2},{4,5},{5,4},{6,7},{7,6},{8,9},{9,8},{10,11... | collective-permute-start | bytes 3145736 | tf_op jit(solution)/shard_map/ppermute | solution.py:140
  105.6 2.3 collective-permute-start.17
  105.6 17.3 %collective-permute-start.28 = (bf16[2112,128]{1,0:T(8,128)(2,1)}, bf16[2112,128]{1,0:T(8,128)(2,1)}, u32[]{:S(2)}, u32[]{:S(2)}) collective-permute-start(bf16[2112,128]{1,0:T(8,128)(2,1)} %gate.28.refs_4_), channel_id=1, source_target_pairs={{0,4},{4,0},{8,12},{12,8},{16,20},{20,16},{24,28},{28,24},{1,5},{5... | collective-permute-start | bytes 1622024 | tf_op jit(solution)/shard_map/ppermute | solution.py:140
  106.3 8.5 %collective-permute-start.18 = (bf16[512,256]{1,0:T(8,128)(2,1)S(1)}, bf16[512,256]{1,0:T(8,128)(2,1)}, u32[]{:S(2)}, u32[]{:S(2)}) collective-permute-start(bf16[512,256]{1,0:T(8,128)(2,1)S(1)} %copy-done.24), channel_id=1, source_target_pairs={{0,2},{1,3},{2,0},{3,1},{4,6},{5,7},{6,4},{7,5},{8,10},{9,11},{10,... | collective-permute-start | bytes 786440 | tf_op jit(solution)/shard_map/ppermute | solution.py:140
  107.2 15.7 %collective-permute-start.20 = (bf16[256,1024]{1,0:T(8,128)(2,1)}, bf16[256,1024]{1,0:T(8,128)(2,1)}, u32[]{:S(2)}, u32[]{:S(2)}) collective-permute-start(bf16[256,1024]{1,0:T(8,128)(2,1)} %get-tuple-element.74.refs_6_), channel_id=1, source_target_pairs={{0,1},{1,0},{2,3},{3,2},{4,5},{5,4},{6,7},{7,6},{8,9},{9,8},{10,11... | collective-permute-start | bytes 1572872 | tf_op jit(solution)/shard_map/ppermute | solution.py:140
  107.9 15.0 %collective-permute-start.23 = (bf16[256,1024]{1,0:T(8,128)(2,1)}, bf16[256,1024]{1,0:T(8,128)(2,1)}, u32[]{:S(2)}, u32[]{:S(2)}) collective-permute-start(bf16[256,1024]{1,0:T(8,128)(2,1)} %gate.26.refs_8_), channel_id=1, source_target_pairs={{0,1},{1,0},{2,3},{3,2},{4,5},{5,4},{6,7},{7,6},{8,9},{9,8},{10,11... | collective-permute-start | bytes 1572872 | tf_op jit(solution)/shard_map/ppermute | solution.py:140
  114.7 8.2 %collective-permute-start.19 = (bf16[512,256]{1,0:T(8,128)(2,1)S(1)}, bf16[512,256]{1,0:T(8,128)(2,1)}, u32[]{:S(2)}, u32[]{:S(2)}) collective-permute-start(bf16[512,256]{1,0:T(8,128)(2,1)S(1)} %copy-done.23), channel_id=1, source_target_pairs={{0,3},{1,2},{2,1},{3,0},{4,7},{5,6},{6,5},{7,4},{8,11},{9,10},{10,... | collective-permute-start | bytes 786440 | tf_op jit(solution)/shard_map/ppermute | solution.py:140
  128.4 3.1 collective-permute-start.29
  128.5 25.9 %collective-permute-start.30 = (bf16[512,1024]{1,0:T(8,128)(2,1)}, bf16[512,1024]{1,0:T(8,128)(2,1)}, u32[]{:S(2)}, u32[]{:S(2)}) collective-permute-start(bf16[512,1024]{1,0:T(8,128)(2,1)} %get-tuple-element.78.refs_9_), channel_id=1, source_target_pairs={{0,2},{1,3},{2,0},{3,1},{4,6},{5,7},{6,4},{7,5},{8,10},{9,11},{10,... | collective-permute-start | bytes 3145736 | tf_op jit(solution)/shard_map/ppermute | solution.py:140
  154.4 3.0 collective-permute-start.31
  175.0 3.1 collective-permute-start.32
  175.2 6.4 %collective-permute-start.33 = (bf16[512,1024]{1,0:T(8,128)(2,1)}, bf16[512,1024]{1,0:T(8,128)(2,1)}, u32[]{:S(2)}, u32[]{:S(2)}) collective-permute-start(bf16[512,1024]{1,0:T(8,128)(2,1)} %get-tuple-element.89), channel_id=1, source_target_pairs={{0,1},{1,0},{2,3},{3,2},{4,5},{5,4},{6,7},{7,6},{8,9},{9,8},{10,11... | collective-permute-start | bytes 3145736 | tf_op jit(solution)/shard_map/ppermute | solution.py:140
  180.4 25.6 %collective-permute-start.36 = (bf16[512,1024]{1,0:T(8,128)(2,1)}, bf16[512,1024]{1,0:T(8,128)(2,1)}, u32[]{:S(2)}, u32[]{:S(2)}) collective-permute-start(bf16[512,1024]{1,0:T(8,128)(2,1)} %fold.4.refs_15_), channel_id=1, source_target_pairs={{0,2},{1,3},{2,0},{3,1},{4,6},{5,7},{6,4},{7,5},{8,10},{9,11},{10,... | collective-permute-start | bytes 3145736 | tf_op jit(solution)/shard_map/ppermute | solution.py:140
  206.0 15.1 %collective-permute-start.35 = (bf16[512,1024]{1,0:T(8,128)(2,1)}, bf16[512,1024]{1,0:T(8,128)(2,1)}, u32[]{:S(2)}, u32[]{:S(2)}) collective-permute-start(bf16[512,1024]{1,0:T(8,128)(2,1)} %get-tuple-element.93), channel_id=1, source_target_pairs={{0,1},{1,0},{2,3},{3,2},{4,5},{5,4},{6,7},{7,6},{8,9},{9,8},{10,11... | collective-permute-start | bytes 3145736 | tf_op jit(solution)/shard_map/ppermute | solution.py:140
  214.1 2.1 collective-permute-start.40
  214.7 9.5 %collective-permute-start.37 = (bf16[256,512]{1,0:T(8,128)(2,1)}, bf16[256,512]{1,0:T(8,128)(2,1)}, u32[]{:S(2)}, u32[]{:S(2)}) collective-permute-start(bf16[256,512]{1,0:T(8,128)(2,1)} %get-tuple-element.94), channel_id=1, source_target_pairs={{0,2},{1,3},{2,0},{3,1},{4,6},{5,7},{6,4},{7,5},{8,10},{9,11},{10,... | collective-permute-start | bytes 786440 | tf_op jit(solution)/shard_map/ppermute | solution.py:140
  215.8 12.3 %collective-permute-start.38 = (bf16[256,512]{1,0:T(8,128)(2,1)}, bf16[256,512]{1,0:T(8,128)(2,1)}, u32[]{:S(2)}, u32[]{:S(2)}) collective-permute-start(bf16[256,512]{1,0:T(8,128)(2,1)} %get-tuple-element.95), channel_id=1, source_target_pairs={{0,3},{1,2},{2,1},{3,0},{4,7},{5,6},{6,5},{7,4},{8,11},{9,10},{10,... | collective-permute-start | bytes 786440 | tf_op jit(solution)/shard_map/ppermute | solution.py:140
  220.5 8.6 %collective-permute-start.41 = (bf16[256,1024]{1,0:T(8,128)(2,1)}, bf16[256,1024]{1,0:T(8,128)(2,1)}, u32[]{:S(2)}, u32[]{:S(2)}) collective-permute-start(bf16[256,1024]{1,0:T(8,128)(2,1)} %get-tuple-element.102), channel_id=1, source_target_pairs={{0,1},{1,0},{2,3},{3,2},{4,5},{5,4},{6,7},{7,6},{8,9},{9,8},{10,11... | collective-permute-start | bytes 1572872 | tf_op jit(solution)/shard_map/ppermute | solution.py:140
  228.0 37.0 %collective-permute-start.39 = (bf16[512,1024]{1,0:T(8,128)(2,1)}, bf16[512,1024]{1,0:T(8,128)(2,1)}, u32[]{:S(2)}, u32[]{:S(2)}) collective-permute-start(bf16[512,1024]{1,0:T(8,128)(2,1)} %gate.30), channel_id=1, source_target_pairs={{0,2},{1,3},{2,0},{3,1},{4,6},{5,7},{6,4},{7,5},{8,10},{9,11},{10,... | collective-permute-start | bytes 3145736 | tf_op jit(solution)/shard_map/ppermute | solution.py:140
  231.1 34.5 %collective-permute-start.43 = (bf16[256,1024]{1,0:T(8,128)(2,1)}, bf16[256,1024]{1,0:T(8,128)(2,1)}, u32[]{:S(2)}, u32[]{:S(2)}) collective-permute-start(bf16[256,1024]{1,0:T(8,128)(2,1)} %gate.31.refs_15_), channel_id=1, source_target_pairs={{0,2},{1,3},{2,0},{3,1},{4,6},{5,7},{6,4},{7,5},{8,10},{9,11},{10,... | collective-permute-start | bytes 1572872 | tf_op jit(solution)/shard_map/ppermute | solution.py:140
  263.1 12.2 %collective-permute-start.44 = (bf16[512,256]{1,0:T(8,128)(2,1)}, bf16[512,256]{1,0:T(8,128)(2,1)}, u32[]{:S(2)}, u32[]{:S(2)}) collective-permute-start(bf16[512,256]{1,0:T(8,128)(2,1)} %get-tuple-element.109), channel_id=1, source_target_pairs={{0,1},{1,0},{2,3},{3,2},{4,5},{5,4},{6,7},{7,6},{8,9},{9,8},{10,11... | collective-permute-start | bytes 786440 | tf_op jit(solution)/shard_map/ppermute | solution.py:140
  263.6 11.7 %collective-permute-start.45 = (bf16[512,256]{1,0:T(8,128)(2,1)}, bf16[512,256]{1,0:T(8,128)(2,1)}, u32[]{:S(2)}, u32[]{:S(2)}) collective-permute-start(bf16[512,256]{1,0:T(8,128)(2,1)} %get-tuple-element.110), channel_id=1, source_target_pairs={{0,2},{1,3},{2,0},{3,1},{4,6},{5,7},{6,4},{7,5},{8,10},{9,11},{10,... | collective-permute-start | bytes 786440 | tf_op jit(solution)/shard_map/ppermute | solution.py:140
  264.7 12.3 %collective-permute-start.46 = (bf16[512,256]{1,0:T(8,128)(2,1)}, bf16[512,256]{1,0:T(8,128)(2,1)}, u32[]{:S(2)}, u32[]{:S(2)}) collective-permute-start(bf16[512,256]{1,0:T(8,128)(2,1)} %get-tuple-element.111), channel_id=1, source_target_pairs={{0,3},{1,2},{2,1},{3,0},{4,7},{5,6},{6,5},{7,4},{8,11},{9,10},{10,... | collective-permute-start | bytes 786440 | tf_op jit(solution)/shard_map/ppermute | solution.py:140
  277.0 3.6 collective-permute-start.47
  282.9 25.8 %collective-permute-start.49 = (bf16[512,1024]{1,0:T(8,128)(2,1)}, bf16[512,1024]{1,0:T(8,128)(2,1)}, u32[]{:S(2)}, u32[]{:S(2)}) collective-permute-start(bf16[512,1024]{1,0:T(8,128)(2,1)} %fold.7.refs_11_), channel_id=1, source_target_pairs={{0,2},{1,3},{2,0},{3,1},{4,6},{5,7},{6,4},{7,5},{8,10},{9,11},{10,... | collective-permute-start | bytes 3145736 | tf_op jit(solution)/shard_map/ppermute | solution.py:140
  284.1 30.1 %collective-permute-start.34 = (bf16[512,1024]{1,0:T(8,128)(2,1)}, bf16[512,1024]{1,0:T(8,128)(2,1)}, u32[]{:S(2)}, u32[]{:S(2)}) collective-permute-start(bf16[512,1024]{1,0:T(8,128)(2,1)} %get-tuple-element.91), channel_id=1, source_target_pairs={{0,1},{1,0},{2,3},{3,2},{4,5},{5,4},{6,7},{7,6},{8,9},{9,8},{10,11... | collective-permute-start | bytes 3145736 | tf_op jit(solution)/shard_map/ppermute | solution.py:140
  284.2 3.7 %collective-permute-start.42 = (bf16[256,1024]{1,0:T(8,128)(2,1)}, bf16[256,1024]{1,0:T(8,128)(2,1)}, u32[]{:S(2)}, u32[]{:S(2)}) collective-permute-start(bf16[256,1024]{1,0:T(8,128)(2,1)} %get-tuple-element.105), channel_id=1, source_target_pairs={{0,1},{1,0},{2,3},{3,2},{4,5},{5,4},{6,7},{7,6},{8,9},{9,8},{10,11... | collective-permute-start | bytes 1572872 | tf_op jit(solution)/shard_map/ppermute | solution.py:140
  297.9 26.4 %collective-permute-start.50 = (bf16[4,512,128]{2,1,0:T(8,128)(2,1)}, bf16[4,512,128]{2,1,0:T(8,128)(2,1)}, u32[]{:S(2)}, u32[]{:S(2)}) collective-permute-start(bf16[4,512,128]{2,1,0:T(8,128)(2,1)} %get-tuple-element.119), channel_id=1, source_target_pairs={{0,4},{4,0},{8,12},{12,8},{16,20},{20,16},{24,28},{28,24},{1,5},{5... | collective-permute-start | bytes 1572872 | tf_op jit(solution)/shard_map/ppermute | solution.py:140
  299.5 34.1 %collective-permute-start.48 = (bf16[512,1024]{1,0:T(8,128)(2,1)}, bf16[512,1024]{1,0:T(8,128)(2,1)}, u32[]{:S(2)}, u32[]{:S(2)}) collective-permute-start(bf16[512,1024]{1,0:T(8,128)(2,1)} %gate.33), channel_id=1, source_target_pairs={{0,1},{1,0},{2,3},{3,2},{4,5},{5,4},{6,7},{7,6},{8,9},{9,8},{10,11... | collective-permute-start | bytes 3145736 | tf_op jit(solution)/shard_map/ppermute | solution.py:140
  308.7 3.9 %collective-permute-start.56 = (f32[2,1024]{1,0:T(2,128)}, f32[2,1024]{1,0:T(2,128)S(1)}, u32[]{:S(2)}, u32[]{:S(2)}) collective-permute-start(f32[2,1024]{1,0:T(2,128)} %gate.37), channel_id=1, source_target_pairs={{0,4},{4,0},{8,12},{12,8},{16,20},{20,16},{24,28},{28,24},{1,5},{5... | collective-permute-start | bytes 24584 | tf_op jit(solution)/shard_map/ppermute | solution.py:140
  310.2 18.1 %collective-permute-start.53 = (bf16[4,512,128]{2,1,0:T(8,128)(2,1)}, bf16[4,512,128]{2,1,0:T(8,128)(2,1)}, u32[]{:S(2)}, u32[]{:S(2)}) collective-permute-start(bf16[4,512,128]{2,1,0:T(8,128)(2,1)} %get-tuple-element.121), channel_id=1, source_target_pairs={{0,8},{4,12},{8,0},{12,4},{16,24},{20,28},{24,16},{28,20},{1,9},{5... | collective-permute-start | bytes 1572872 | tf_op jit(solution)/shard_map/ppermute | solution.py:140
  313.3 10.4 %collective-permute-start.57 = (f32[2,1024]{1,0:T(2,128)S(1)}, f32[2,1024]{1,0:T(2,128)S(1)}, u32[]{:S(2)}, u32[]{:S(2)}) collective-permute-start(f32[2,1024]{1,0:T(2,128)S(1)} %add.115), channel_id=1, source_target_pairs={{0,8},{4,12},{8,0},{12,4},{16,24},{20,28},{24,16},{28,20},{1,9},{5... | collective-permute-start | bytes 24584 | tf_op jit(solution)/shard_map/ppermute | solution.py:140
  323.8 4.5 %collective-permute-start.58 = (f32[2,1024]{1,0:T(2,128)S(1)}, f32[2,1024]{1,0:T(2,128)S(1)}, u32[]{:S(2)}, u32[]{:S(2)}) collective-permute-start(f32[2,1024]{1,0:T(2,128)S(1)} %add.116), channel_id=1, source_target_pairs={{0,16},{4,20},{8,24},{12,28},{16,0},{20,4},{24,8},{28,12},{1,17},{... | collective-permute-start | bytes 24584 | tf_op jit(solution)/shard_map/ppermute | solution.py:140
  328.3 4.4 %collective-permute-start.59 = (f32[2,1024]{1,0:T(2,128)S(1)}, f32[2,1024]{1,0:T(2,128)S(1)}, u32[]{:S(2)}, u32[]{:S(2)}) collective-permute-start(f32[2,1024]{1,0:T(2,128)S(1)} %add.117), channel_id=1, source_target_pairs={{0,1},{1,0},{2,3},{3,2},{4,5},{5,4},{6,7},{7,6},{8,9},{9,8},{10,11... | collective-permute-start | bytes 24584 | tf_op jit(solution)/shard_map/ppermute | solution.py:140
  331.3 13.0 %collective-permute-start.51 = (bf16[2,512,128]{2,1,0:T(8,128)(2,1)}, bf16[2,512,128]{2,1,0:T(8,128)(2,1)}, u32[]{:S(2)}, u32[]{:S(2)}) collective-permute-start(bf16[2,512,128]{2,1,0:T(8,128)(2,1)} %gate.34), channel_id=1, source_target_pairs={{0,8},{4,12},{8,0},{12,4},{16,24},{20,28},{24,16},{28,20},{1,9},{5... | collective-permute-start | bytes 786440 | tf_op jit(solution)/shard_map/ppermute | solution.py:140
  332.4 15.3 %collective-permute-start.54 = (bf16[2,512,128]{2,1,0:T(8,128)(2,1)}, bf16[2,512,128]{2,1,0:T(8,128)(2,1)}, u32[]{:S(2)}, u32[]{:S(2)}) collective-permute-start(bf16[2,512,128]{2,1,0:T(8,128)(2,1)} %gate.35), channel_id=1, source_target_pairs={{0,16},{4,20},{8,24},{12,28},{16,0},{20,4},{24,8},{28,12},{1,17},{... | collective-permute-start | bytes 786440 | tf_op jit(solution)/shard_map/ppermute | solution.py:140
  332.7 6.9 %collective-permute-start.60 = (f32[2,1024]{1,0:T(2,128)S(1)}, f32[2,1024]{1,0:T(2,128)S(1)}, u32[]{:S(2)}, u32[]{:S(2)}) collective-permute-start(f32[2,1024]{1,0:T(2,128)S(1)} %add.118), channel_id=1, source_target_pairs={{0,2},{1,3},{2,0},{3,1},{4,6},{5,7},{6,4},{7,5},{8,10},{9,11},{10,... | collective-permute-start | bytes 24584 | tf_op jit(solution)/shard_map/ppermute | solution.py:140
  345.5 8.6 %collective-permute-start.52 = (bf16[1,512,128]{2,1,0:T(8,128)(2,1)S(1)}, bf16[1,512,128]{2,1,0:T(8,128)(2,1)S(1)}, u32[]{:S(2)}, u32[]{:S(2)}) collective-permute-start(bf16[1,512,128]{2,1,0:T(8,128)(2,1)S(1)} %slice.107), channel_id=1, source_target_pairs={{0,16},{4,20},{8,24},{12,28},{16,0},{20,4},{24,8},{28,12},{1,17},{... | collective-permute-start | bytes 393224 | tf_op jit(solution)/shard_map/ppermute | solution.py:140
  348.7 5.5 %collective-permute-start.55 = (bf16[1,512,128]{2,1,0:T(8,128)(2,1)S(1)}, bf16[1,512,128]{2,1,0:T(8,128)(2,1)S(1)}, u32[]{:S(2)}, u32[]{:S(2)}) collective-permute-start(bf16[1,512,128]{2,1,0:T(8,128)(2,1)S(1)} %slice.106), channel_id=1, source_target_pairs={{0,4},{4,0},{8,12},{12,8},{16,20},{20,16},{24,28},{28,24},{1,5},{5... | collective-permute-start | bytes 393224 | tf_op jit(solution)/shard_map/ppermute | solution.py:140
  (24 other events, 121.4 us)
Sparse Core Ops, SparseCore 0:
  206.2 88.1 reduce-scatter.1
